TPU v7x, 128 devices: a whole 4x4x4 slice. The times are simulated.
128 devices in a mesh: face: 8 (over z_lo, y), tile: 16 (over x, z_hi, core).
Axes of the slice: x: 4, y: 4, z: 4 (z_hi: 2, z_lo: 2; z = z_hi * 2 + z_lo), core: 2. Of those that a mesh axis runs over, the one named last changes fastest.
Arguments:
- obs_values: bfloat16 [32768, 256], P(('face', 'tile')), may hold values from -6 to 6
- obs_tile: int32 [32768, 1], P(('face', 'tile')), may hold values from 0 to 127; in each aligned block of 256 rows (0 to 255, 256 to 511, ...) at most 4 rows name the same one
- interp: bfloat16 [128, 128, 4, 256], P(('face', 'tile')), may hold values from -0.375 to 0.375
- tile_spin: int32 [128, 1], P(('face', 'tile')), may hold values from 0 to 3
- w_embed: bfloat16 [256, 512], replicated, may hold values from -0.375 to 0.375
- dw_kernel: bfloat16 [49, 512], replicated, may hold values from -0.875 to 0.875
- norm_gain: bfloat16 [512], replicated, may hold values from 0.099609375 to 1.8984375
- w_one: bfloat16 [512, 2048], replicated, may hold values from -0.25 to 0.25
- w_two: bfloat16 [2048, 512], replicated, may hold values from -0.125 to 0.125
- cotangent: bfloat16 [32768, 512], P(('face', 'tile')), may hold values from -0.032958984 to 0.032958984
Outputs:
- features: bfloat16 [32768, 512], P(('face', 'tile'))
- grad_embed: float32 [256, 512], replicated
- grad_kernel: float32 [49, 512], replicated
- grad_gain: float32 [512], replicated
- grad_one: float32 [512, 2048], replicated
- grad_two: float32 [2048, 512], replicated
Inputs may be any that keep to these rules, and one draw needn't show every extreme that they name: `obs_tile`: in the rows of one device no tile is named more than 4 times; in some device one tile is named exactly 4 times.
All inputs are finite; a program needn't handle non-finite values.
Results may differ from a plain program's by a relative error of at most 0.0081.
Values may be sent and summed in bfloat16 or wider, within the bound.
No kernel may reach another device: no remote copies, remote signals or barrier semaphores. Data moves between devices by JAX's collectives and lax.ppermute only.
A program may use at most 256 MiB of HBM per device.

v0:
```python
from functools import partial
import math

import jax
import jax.numpy as jnp
from jax import lax
from jax.sharding import PartitionSpec as P


def shortened(value):

    def short(part):
        return part.astype(jnp.bfloat16) if part.dtype == jnp.float32 else part

    return jax.tree.map(short, value)


def padded_2(value, sides, width):
    for axis, dim in sides:
        size, length = (lax.axis_size(axis), value.shape[dim])
        up = [(i, (i + 1) % size) for i in range(size)]
        down = [(j, i) for i, j in up]
        last = lax.slice_in_dim(value, length - width, length, axis=dim)
        first = lax.slice_in_dim(value, 0, width, axis=dim)
        before = lax.ppermute(last, axis, up)
        after = lax.ppermute(first, axis, down)
        value = jnp.concatenate([before, value, after], axis=dim)
    return value


def quarter_turn(block, quarter):
    return lax.switch(
        quarter, [partial(jnp.rot90, k=turns, axes=(0, 1)) for turns in range(4)], block
    )


def tile_pass(field, embedded, cot_tile, dw_kernel, norm_gain, w_one, w_two):
    side_len = embedded.shape[0]
    channels = embedded.shape[2]
    cell_count = side_len * side_len
    kernel_taps = dw_kernel.astype(jnp.float32)
    gain_values = norm_gain.astype(jnp.float32)
    convolved = jnp.zeros((side_len, side_len, channels), jnp.float32)
    for kernel_tap in range(49):
        row_shift, col_shift = divmod(kernel_tap, 7)
        convolved = (
            convolved
            + field[row_shift : row_shift + side_len, col_shift : col_shift + side_len].astype(
                jnp.float32
            )
            * kernel_taps[kernel_tap]
        )
    flattened = convolved.reshape(cell_count, channels)
    centred = flattened - jnp.mean(flattened, axis=-1, keepdims=True)
    inverse = lax.rsqrt(jnp.mean(centred * centred, axis=-1, keepdims=True) + 1e-06)
    normal = centred * inverse
    scaled = (normal * gain_values).astype(jnp.bfloat16)
    hidden_pre = jnp.dot(scaled, w_one, preferred_element_type=jnp.float32)
    active, gelu_back = jax.vjp(partial(jax.nn.gelu, approximate=True), hidden_pre)
    active = active.astype(jnp.bfloat16)
    branch = jnp.dot(active, w_two, preferred_element_type=jnp.float32)
    output = (embedded.reshape(cell_count, channels).astype(jnp.float32) + branch).astype(
        jnp.bfloat16
    )
    contract_rows = (((0,), (0,)), ((), ()))
    contract_cols = (((1,), (1,)), ((), ()))
    grad_two = lax.dot_general(active, cot_tile, contract_rows, preferred_element_type=jnp.float32)
    d_active = lax.dot_general(cot_tile, w_two, contract_cols, preferred_element_type=jnp.float32)
    d_hidden = gelu_back(d_active)[0].astype(jnp.bfloat16)
    grad_one = lax.dot_general(scaled, d_hidden, contract_rows, preferred_element_type=jnp.float32)
    d_scaled = lax.dot_general(d_hidden, w_one, contract_cols, preferred_element_type=jnp.float32)
    grad_gain = jnp.sum(d_scaled * normal, axis=0)
    d_normal = d_scaled * gain_values
    d_conv = (
        d_normal
        - jnp.mean(d_normal, axis=-1, keepdims=True)
        - normal * jnp.mean(d_normal * normal, axis=-1, keepdims=True)
    ) * inverse
    d_conv = d_conv.reshape(side_len, side_len, channels)
    kernel_rows = []
    for kernel_tap in range(49):
        row_shift, col_shift = divmod(kernel_tap, 7)
        kernel_rows.append(
            jnp.sum(
                field[row_shift : row_shift + side_len, col_shift : col_shift + side_len].astype(
                    jnp.float32
                )
                * d_conv,
                axis=(0, 1),
            )
        )
    grad_kernel = jnp.stack(kernel_rows)
    spread = jnp.pad(d_conv, ((6, 6), (6, 6), (0, 0)))
    d_field = jnp.zeros((side_len + 6, side_len + 6, channels), jnp.float32)
    for kernel_tap in range(49):
        row_shift, col_shift = divmod(kernel_tap, 7)
        d_field = (
            d_field
            + spread[
                6 - row_shift : 12 - row_shift + side_len, 6 - col_shift : 12 - col_shift + side_len
            ]
            * kernel_taps[kernel_tap]
        )
    return (output, grad_one, grad_two, grad_gain, grad_kernel, d_field)


def on_device(
    obs_values, obs_tile, interp, tile_spin, w_embed, dw_kernel, norm_gain, w_one, w_two, cotangent
):
    tile_count = lax.axis_size(("face", "tile"))
    row_count, value_width = obs_values.shape
    slot_most = interp.shape[2]
    cell_count = interp.shape[3]
    side_len = math.isqrt(cell_count)
    channels = w_embed.shape[1]
    contract_rows = (((0,), (0,)), ((), ()))
    targets = obs_tile[:, 0]
    onehot = (targets[:, None] == jnp.arange(tile_count, dtype=jnp.int32)[None, :]).astype(
        jnp.int32
    )
    slot_rank = jnp.sum((jnp.cumsum(onehot, axis=0) - 1) * onehot, axis=1)
    slot_ids = targets * slot_most + slot_rank
    selector = (
        jnp.arange(tile_count * slot_most, dtype=jnp.int32)[:, None] == slot_ids[None, :]
    ).astype(jnp.bfloat16)
    leaving = jnp.dot(selector, obs_values, preferred_element_type=jnp.float32).astype(jnp.bfloat16)
    arrived_obs = lax.all_to_all(
        leaving.reshape(tile_count, slot_most * value_width),
        ("face", "tile"),
        split_axis=0,
        concat_axis=0,
        tiled=True,
    )
    arrived_obs = arrived_obs.reshape(tile_count * slot_most, value_width)
    gridded = lax.dot_general(
        interp.reshape(tile_count * slot_most, cell_count),
        arrived_obs,
        contract_rows,
        preferred_element_type=jnp.float32,
    ).astype(jnp.bfloat16)
    embedded = (
        jnp.dot(gridded, w_embed, preferred_element_type=jnp.float32)
        .astype(jnp.bfloat16)
        .reshape(side_len, side_len, channels)
    )
    spin_count = tile_spin[0, 0]
    back_turn = (4 - spin_count) % 4
    logical = quarter_turn(embedded, spin_count)
    extended = padded_2(shortened(logical), (("face", 0), ("tile", 1)), 3).astype(logical.dtype)
    positions = jnp.arange(side_len + 6, dtype=jnp.int32)
    outer_band = (positions < 3) | (positions >= side_len + 3)
    corner_mask = outer_band[:, None, None] & outer_band[None, :, None]
    padded = jnp.where(corner_mask, jnp.zeros((), jnp.bfloat16), extended)
    field = quarter_turn(padded, back_turn)
    output, grad_one, grad_two, grad_gain, grad_kernel, d_field = tile_pass(
        field, embedded, cotangent, dw_kernel, norm_gain, w_one, w_two
    )
    d_logical = quarter_turn(d_field, spin_count)
    sent_rims = d_logical.astype(jnp.bfloat16)
    beside_all = padded_2(sent_rims, (("face", 0), ("tile", 1)), 3)
    collected = d_logical[3 : side_len + 3, 3 : side_len + 3]
    collected = collected.at[0:3].add(beside_all[0:3, 6 : side_len + 6].astype(jnp.float32))
    collected = collected.at[side_len - 3 :].add(
        beside_all[side_len + 9 : side_len + 12, 6 : side_len + 6].astype(jnp.float32)
    )
    collected = collected.at[:, 0:3].add(beside_all[6 : side_len + 6, 0:3].astype(jnp.float32))
    collected = collected.at[:, side_len - 3 :].add(
        beside_all[6 : side_len + 6, side_len + 9 : side_len + 12].astype(jnp.float32)
    )
    d_embedded = quarter_turn(collected, back_turn) + cotangent.reshape(
        side_len, side_len, channels
    ).astype(jnp.float32)
    d_round = d_embedded.reshape(cell_count, channels).astype(jnp.bfloat16)
    grad_embed = lax.dot_general(
        gridded, d_round, contract_rows, preferred_element_type=jnp.float32
    )
    totals = lax.psum((grad_embed, grad_kernel, grad_gain, grad_one, grad_two), ("face", "tile"))
    return (output, totals[0], totals[1], totals[2], totals[3], totals[4])


def solution(mesh):
    in_specs = (
        P(("face", "tile"), None),
        P(("face", "tile"), None),
        P(("face", "tile"), None, None, None),
        P(("face", "tile"), None),
        P(),
        P(),
        P(),
        P(),
        P(),
        P(("face", "tile"), None),
    )
    out_specs = (P(("face", "tile"), None), P(), P(), P(), P(), P())
    return jax.shard_map(
        on_device, mesh=mesh, in_specs=in_specs, out_specs=out_specs, check_vma=False
    )
```

profile of v0, /device:TPU:1, one launch (start us, length us, event | category | flops | bytes accessed | tf_op | source)
XLA Modules:
  0.0 471.0 jit_solution(7381405460696700605)
XLA Ops:
  14.9 11.5 %all-to-all-start = ((bf16[128,2,512]{2,1,0:T(2,128)(2,1)}), bf16[128,2,512]{2,1,0:T(2,128)(2,1)S(1)}, u32[]{:S(2)}, u32[]{:S(2)}) async-start(bf16[128,2,512]{2,1,0:T(2,128)(2,1)} %reshape.341), calls=%async_computation | async-start | bytes 524288 | tf_op jit(solution)/shard_map/all_to_all | solution.py:127
  27.1 3.7 fusion.319
  32.8 4.3 all-to-all-done
  42.6 2.7 collective-permute-start.1
  46.9 3.2 collective-permute-start.2
  51.7 4.9 %collective-permute-done.3 = bf16[22,3,512]{2,1,0:T(4,128)(2,1)S(1)} collective-permute-done((bf16[22,3,512]{2,1,0:T(4,128)(2,1)S(1)}, bf16[22,3,512]{2,1,0:T(4,128)(2,1)S(1)}, u32[]{:S(2)}, u32[]{:S(2)}) %collective-permute-start.3) | collective-permute-done | bytes 67616 | tf_op jit(solution)/shard_map/ppermute | solution.py:26
  72.6 14.3 %fusion.308 = (f32[16,16]{1,0:T(8,128)S(1)}, f32[16,16,512]{2,1,0:T(8,128)S(1)}) fusion(f32[512]{0:T(512)S(1)} %bitcast.359, bf16[16,16,512]{2,0,1:T(8,128)(2,1)S(1)} %get-tuple-element.2215, f32[512]{0:T(512)S(1)} %bitcast.354, bf16[16,16,512]{2,0,1:T(8,128)(2,1)S(1)} %get-tuple-element.2168, f32[512]{0:T(512)S(1)} %bitcast.349, ...), kind=kLoop, calls=%fused_computation.646 | loop fusion | flops 19267328 | bytes 13470720 | tf_op jit(solution)/shard_map/reduce_sum | solution.py:54
  88.7 4.8 %fusion.199 = (bf16[256,2048]{1,0:T(8,128)(2,1)S(1)}, f32[256,2048]{1,0:T(8,128)}) fusion(f32[256,2048]{1,0:T(8,128)} %fusion.319, bf16[256,512]{1,0:T(8,128)(2,1)S(1)} %multiply_convert_fusion.1, bf16[512,2048]{1,0:T(8,128)(2,1)S(1)} %copy-done), kind=kOutput, calls=%fused_computation.401 | convolution fusion | flops 547356672 | bytes 7602176 | tf_op jit(solution)/shard_map/dot_general | solution.py:58
  95.9 4.1 fusion.295
  100.3 6.1 %fusion.296 = (f32[512]{0:T(512)}, f32[512]{0:T(512)}, f32[512]{0:T(512)}, f32[512]{0:T(512)}, f32[512]{0:T(512)}, /*index=5*/f32[512]{0:T(512)}, f32[512]{0:T(5...) fusion(bf16[16,16,512]{2,0,1:T(8,128)(2,1)S(1)} %copy-done.7, ...), kind=kLoop, calls=%fused_computation.602 | loop fusion | flops 7068672 | bytes 5279744 | tf_op jit(solution)/shard_map/reduce_sum | solution.py:84
  106.5 5.2 %fusion.297 = (f32[512]{0:T(512)}, f32[512]{0:T(512)}, f32[512]{0:T(512)}, f32[512]{0:T(512)}, f32[512]{0:T(512)}, /*index=5*/f32[512]{0:T(512)}, f32[512]{0:T(5...) fusion(bf16[16,16,512]{2,0,1:T(8,128)(2,1)S(1)} %get-tuple-elem, ...), kind=kLoop, calls=%fused_computation.603 | loop fusion | flops 7068672 | bytes 5279744 | tf_op jit(solution)/shard_map/reduce_sum | solution.py:84
  111.9 146.5 %conditional.6 = (f32[22,22,512]{2,0,1:T(8,128)S(1)}) conditional(s32[]{:T(128)} %bitcast.14, (f32[28,28,512]{2,1,0:T(8,128)S(1)}, f32[28,28,512]{2,1,0:T(8,128)S(1)}, f32[28,28,512]{2,1,0:T(8,128)S(1)}, f32[512]{0:T(512)S(1)}, f32[28,28,512]{2,1,0:T(8,128)S(1)}, /*index=5*/f32[512]{0:T(512)S(1)}, ...), branch_computations={%region_15.16_spmd, %region_16.17_spmd, %region_17.18_spmd, %regio... | conditional | flops 24037376 | bytes 209136160 | solution.py:32
  130.8 2.4 copy.596
  157.2 2.6 copy.584
  210.5 2.4 copy.560
  213.1 20.4 %fusion = f32[22,22,512]{2,0,1:T(8,128)S(1)} fusion(f32[28,28,512]{2,0,1:T(8,128)} %copy.561, f32[28,28,512]{2,0,1:T(8,128)} %copy.562, f32[28,28,512]{2,0,1:T(8,128)} %copy.563, f32[28,28,512]{2,0,1:T(8,128)} %copy.564, f32[28,28,512]{2,0,1:T(8,128)} %copy.565, f32[28,28,512]{2,0,1:T(8,128)} %copy.566, f32[28,28,512]{2,0,1:T(8,128)} %copy.567, ...), kind=kLoop, calls=%fused_computation.1 | loop fusion | flops 24037376 | bytes 49661952 | tf_op jit(solution)/shard_map/add | solution.py:98
  260.5 4.6 fusion.307
  265.2 2.7 fusion.321
  269.6 5.8 %stack.199 = f32[49,512]{1,0:T(8,128)} concatenate(f32[1,512]{1,0:T(1,128)S(1)} %bitcast.494, f32[1,512]{1,0:T(1,128)S(1)} %bitcast.495, f32[1,512]{1,0:T(1,128)S(1)} %bitcast.496, f32[1,512]{1,0:T(1,128)S(1)} %bitcast.497, f32[1,512]{1,0:T(1,128)S(1)} %bitcast.498, f32[1,512]{1,0:T(1,128)S(1)} %bitcast.499, f32[1,512]{1,0:T(1,128)S(1)} %bitcast.500, f32[1,512]{1,0:T(1,128)S(1)} %bitcast.501, ...), dimensions={0} | concatenate | bytes 200704 | tf_op jit(solution)/shard_map/stack | solution.py:92
  275.5 2.5 collective-permute-start.7
  284.3 71.9 %psum.37 = f32[512]{0:T(512)} all-reduce(f32[512]{0:T(512)S(1)} %copy-done.198), channel_id=1, replica_groups=mesh['face'=8,'tile'=16] {'face','tile'}, use_global_device_ids=true, to_apply=%region_75.76 | all-reduce | flops 512 | bytes 4096 | tf_op jit(solution)/shard_map/psum | solution.py:177
  356.2 3.1 fusion.200
  359.3 94.1 %all-reduce.4.cloned.1.call-done = (f32[256,512]{1,0:T(8,128)}, f32[49,512]{1,0:T(8,128)}, f32[512,2048]{1,0:T(8,128)}, f32[2048,512]{1,0:T(8,128)}) async-done(((f32[256,512]{1,0:T(8,128)}, f32[49,512]{1,0:T(8,128)}, f32[512,2048]{1,0:T(8,128)}, f32[2048,512]{1,0:T(8,128)}), (f32[256,512]{1,0:T(8,128)}, f32[49,512]{1,0:T(8,128)}, f32[512,2048]{1,0:T(8,128)}, ...) | async-done | bytes 9013264 | tf_op jit(solution)/shard_map/psum | solution.py:177
  455.9 4.8 %copy.851 = f32[512,2048]{1,0:T(8,128)} copy(f32[512,2048]{1,0:T(8,128)} %get-tuple-element.2282) | data formatting | bytes 8388608
  (521 shorter events, 142.8 us)
Async XLA Ops:
  7.2 81.5 %copy-start = (bf16[512,2048]{1,0:T(8,128)(2,1)S(1)}, bf16[512,2048]{1,0:T(8,128)(2,1)}, u32[]{:S(2)}) copy-start(bf16[512,2048]{1,0:T(8,128)(2,1)} %param.41) | copy-start | bytes 6291460
  11.3 15.1 %copy-start.92 = (bf16[49,512]{1,0:T(8,128)(2,1)S(1)}, bf16[49,512]{1,0:T(8,128)(2,1)}, u32[]{:S(2)}) copy-start(bf16[49,512]{1,0:T(8,128)(2,1)} %param.39) | copy-start | bytes 150532
  11.3 15.8 %copy-start.82 = (bf16[256,512]{1,0:T(8,128)(2,1)S(1)}, bf16[256,512]{1,0:T(8,128)(2,1)}, u32[]{:S(2)}) copy-start(bf16[256,512]{1,0:T(8,128)(2,1)} %param.43) | copy-start | bytes 786436
  14.9 22.3 %all-to-all-start = ((bf16[128,2,512]{2,1,0:T(2,128)(2,1)}), bf16[128,2,512]{2,1,0:T(2,128)(2,1)S(1)}, u32[]{:S(2)}, u32[]{:S(2)}) async-start(bf16[128,2,512]{2,1,0:T(2,128)(2,1)} %reshape.341), calls=%async_computation | async-start | bytes 524288 | tf_op jit(solution)/shard_map/all_to_all | solution.py:127
  26.4 427.0 %all-reduce.4.cloned.1.call-start = ((), (), s32[]{:S(2)}) async-start(), calls=%async_computation.1 | async-start | bytes 18055168 | tf_op jit(solution)/shard_map/psum | solution.py:177
  41.5 5.1 %collective-permute-start = (bf16[3,16,512]{2,1,0:T(8,128)(2,1)S(1)}, bf16[3,16,512]{2,1,0:T(8,128)(2,1)S(1)}, u32[]{:S(2)}, u32[]{:S(2)}) collective-permute-start(bf16[3,16,512]{2,1,0:T(8,128)(2,1)S(1)} %copy.794), channel_id=1, source_target_pairs={{0,16},{16,32},{32,48},{48,64},{64,80},{80,96},{96,112},{112,0},{1... | collective-permute-start | bytes 147464 | tf_op jit(solution)/shard_map/ppermute | solution.py:25
  42.6 4.3 collective-permute-start.1
  46.9 4.7 %collective-permute-start.2 = (bf16[22,3,512]{2,1,0:T(4,128)(2,1)S(1)}, bf16[22,3,512]{2,1,0:T(4,128)(2,1)S(1)}, u32[]{:S(2)}, u32[]{:S(2)}) collective-permute-start(bf16[22,3,512]{2,1,0:T(4,128)(2,1)S(1)} %get-tuple-element.2216), channel_id=1, source_target_pairs={{0,1},{1,2},{2,3},{3,4},{4,5},{5,6},{6,7},{7,8},{8,9},{9,10},{10,1... | collective-permute-start | bytes 202760 | tf_op jit(solution)/shard_map/ppermute | solution.py:25
  50.1 6.4 %collective-permute-start.3 = (bf16[22,3,512]{2,1,0:T(4,128)(2,1)S(1)}, bf16[22,3,512]{2,1,0:T(4,128)(2,1)S(1)}, u32[]{:S(2)}, u32[]{:S(2)}) collective-permute-start(bf16[22,3,512]{2,1,0:T(4,128)(2,1)S(1)} %get-tuple-element.2217), channel_id=1, source_target_pairs={{1,0},{2,1},{3,2},{4,3},{5,4},{6,5},{7,6},{8,7},{9,8},{10,9},{11,1... | collective-permute-start | bytes 202760 | tf_op jit(solution)/shard_map/ppermute | solution.py:26
  59.8 11.9 %copy-start.70 = (bf16[16,16,512]{2,0,1:T(8,128)(2,1)}, bf16[16,16,512]{2,0,1:T(8,128)(2,1)S(1)}, u32[]{:S(2)}) copy-start(bf16[16,16,512]{2,0,1:T(8,128)(2,1)S(1)} %get-tuple-element.2203) | copy-start | bytes 786436
  59.8 12.1 %copy-start.72 = (bf16[16,16,512]{2,0,1:T(8,128)(2,1)}, bf16[16,16,512]{2,0,1:T(8,128)(2,1)S(1)}, u32[]{:S(2)}) copy-start(bf16[16,16,512]{2,0,1:T(8,128)(2,1)S(1)} %get-tuple-element.2204) | copy-start | bytes 786436
  59.8 12.4 %copy-start.4 = (bf16[16,16,512]{2,0,1:T(8,128)(2,1)}, bf16[16,16,512]{2,0,1:T(8,128)(2,1)S(1)}, u32[]{:S(2)}) copy-start(bf16[16,16,512]{2,0,1:T(8,128)(2,1)S(1)} %get-tuple-element.2189) | copy-start | bytes 786436
  60.6 11.5 %copy-start.6 = (bf16[16,16,512]{2,0,1:T(8,128)(2,1)}, bf16[16,16,512]{2,0,1:T(8,128)(2,1)S(1)}, u32[]{:S(2)}) copy-start(bf16[16,16,512]{2,0,1:T(8,128)(2,1)S(1)} %get-tuple-element.2168) | copy-start | bytes 786436
  60.6 11.5 %copy-start.8 = (bf16[16,16,512]{2,0,1:T(8,128)(2,1)}, bf16[16,16,512]{2,0,1:T(8,128)(2,1)S(1)}, u32[]{:S(2)}) copy-start(bf16[16,16,512]{2,0,1:T(8,128)(2,1)S(1)} %get-tuple-element.2182) | copy-start | bytes 786436
  60.6 11.5 %copy-start.10 = (bf16[16,16,512]{2,0,1:T(8,128)(2,1)}, bf16[16,16,512]{2,0,1:T(8,128)(2,1)S(1)}, u32[]{:S(2)}) copy-start(bf16[16,16,512]{2,0,1:T(8,128)(2,1)S(1)} %get-tuple-element.2183) | copy-start | bytes 786436
  60.7 11.5 %copy-start.12 = (bf16[16,16,512]{2,0,1:T(8,128)(2,1)}, bf16[16,16,512]{2,0,1:T(8,128)(2,1)S(1)}, u32[]{:S(2)}) copy-start(bf16[16,16,512]{2,0,1:T(8,128)(2,1)S(1)} %get-tuple-element.2184) | copy-start | bytes 786436
  60.7 11.5 %copy-start.14 = (bf16[16,16,512]{2,0,1:T(8,128)(2,1)}, bf16[16,16,512]{2,0,1:T(8,128)(2,1)S(1)}, u32[]{:S(2)}) copy-start(bf16[16,16,512]{2,0,1:T(8,128)(2,1)S(1)} %get-tuple-element.2185) | copy-start | bytes 786436
  60.7 11.5 %copy-start.16 = (bf16[16,16,512]{2,0,1:T(8,128)(2,1)}, bf16[16,16,512]{2,0,1:T(8,128)(2,1)S(1)}, u32[]{:S(2)}) copy-start(bf16[16,16,512]{2,0,1:T(8,128)(2,1)S(1)} %get-tuple-element.2169) | copy-start | bytes 786436
  60.7 11.5 %copy-start.18 = (bf16[16,16,512]{2,0,1:T(8,128)(2,1)}, bf16[16,16,512]{2,0,1:T(8,128)(2,1)S(1)}, u32[]{:S(2)}) copy-start(bf16[16,16,512]{2,0,1:T(8,128)(2,1)S(1)} %get-tuple-element.2170) | copy-start | bytes 786436
  259.0 16.4 %collective-permute-start.5 = (bf16[3,22,512]{2,1,0:T(8,128)(2,1)S(1)}, bf16[3,22,512]{2,1,0:T(8,128)(2,1)S(1)}, u32[]{:S(2)}, u32[]{:S(2)}) collective-permute-start(bf16[3,22,512]{2,1,0:T(8,128)(2,1)S(1)} %get-tuple-element.2165), channel_id=1, source_target_pairs={{16,0},{32,16},{48,32},{64,48},{80,64},{96,80},{112,96},{0,112},{1... | collective-permute-start | bytes 202760 | tf_op jit(solution)/shard_map/ppermute | solution.py:26
  259.0 16.3 %collective-permute-start.4 = (bf16[3,22,512]{2,1,0:T(8,128)(2,1)S(1)}, bf16[3,22,512]{2,1,0:T(8,128)(2,1)S(1)}, u32[]{:S(2)}, u32[]{:S(2)}) collective-permute-start(bf16[3,22,512]{2,1,0:T(8,128)(2,1)S(1)} %get-tuple-element.2166), channel_id=1, source_target_pairs={{0,16},{16,32},{32,48},{48,64},{64,80},{80,96},{96,112},{112,0},{1... | collective-permute-start | bytes 202760 | tf_op jit(solution)/shard_map/ppermute | solution.py:25
  275.5 5.8 %collective-permute-start.7 = (bf16[28,3,512]{2,1,0:T(4,128)(2,1)S(1)}, bf16[28,3,512]{2,1,0:T(4,128)(2,1)S(1)}, u32[]{:S(2)}, u32[]{:S(2)}) collective-permute-start(bf16[28,3,512]{2,1,0:T(4,128)(2,1)S(1)} %get-tuple-element.2163), channel_id=1, source_target_pairs={{1,0},{2,1},{3,2},{4,3},{5,4},{6,5},{7,6},{8,7},{9,8},{10,9},{11,1... | collective-permute-start | bytes 258056 | tf_op jit(solution)/shard_map/ppermute | solution.py:26
  278.0 2.6 collective-permute-start.6
  283.6 72.5 %copy-start.2 = (f32[256,2048]{1,0:T(8,128)S(1)}, f32[256,2048]{1,0:T(8,128)}, u32[]{:S(2)}) copy-start(f32[256,2048]{1,0:T(8,128)} %get-tuple-element.2270) | copy-start | bytes 6291460
  (169 other events, 548.8 us)
Sparse Core Ops, SparseCore 0:
  283.8 169.5 all-reduce.3
where the time goes:
time: 479 us; the launch traced here: 471 us
  local copies, waits for them, and re-layouts  139 us (29%)
  waiting for transfers between devices  108 us (23%)
  blocking collectives  71.9 us (15%)
  other arithmetic  57.9 us (12%)
  loops' own time  30.4 us (6%)
  matrix products  23.8 us (5%)
  starting transfers between devices  23.3 us (5%)
  between operations  17.4 us (4%)
    add x49, local copies, waits for them, and re-layouts  95.8 us
    psum x1, waiting for transfers between devices, on_device(): lax.psum((grad_embed, grad_kernel, grad_gain, grad_one, grad_two), ('face...  94.1 us
    psum x1, blocking collectives, on_device(): lax.psum((grad_embed, grad_kernel, grad_gain, grad_one, grad_two), ('face...  71.9 us
    another operation x4, loops' own time, quarter_turn(): lax.switch(quarter, [partial(jnp.rot90, k=turns, axes=(0, 1)) for turns i...  30.4 us
    unnamed x369, local copies, waits for them, and re-layouts  25.8 us
    add x1, other arithmetic, tile_pass(): d_field + spread[6 - row_shift:12 - row_shift + side_len, 6 - col_shift:1...  20.4 us
    reduce_sum x3, other arithmetic, tile_pass(): jnp.sum(field[row_shift:row_shift + side_len, col_shift:col_shift + side_...  15.4 us
    reduce_sum x1, other arithmetic, tile_pass(): centred = flattened - jnp.mean(flattened, axis=-1, keepdims=True)  14.3 us
  transfers between devices with their start and end apart: 10, of which 7 were waited for; matrix products, arithmetic and copies ran while one was open for 5% of the time, Pallas kernels for 0%

commit v1 on v0

v1 whole, which is shorter than its diff:
```python
import jax
import jax.numpy as jnp
from jax import lax
from jax.experimental import pallas as pl
from jax.experimental.pallas import tpu as pltpu
from jax.sharding import PartitionSpec as P

F32 = jnp.float32
BF16 = jnp.bfloat16
SIDE = 16
CELLS = SIDE * SIDE
HALO = 3
TAPS = 7
FULL = SIDE + 2 * HALO
PITCH = 24
HALF = SIDE // 2
LANE = 128
ROWS2 = HALF + TAPS - 1
STRIP = HALO * SIDE
BOTH = ("face", "tile")
ROOT = 0.7978845608028654
CUBE = 0.044715

NN = (((1,), (0,)), ((), ()))
NT = (((1,), (1,)), ((), ()))
TN = (((0,), (0,)), ((), ()))


def dot(a, b, dims=NN):
    return lax.dot_general(a, b, dims, preferred_element_type=F32)


def call(kernel, outs, scratch, limit, *args):
    vmem = pl.BlockSpec(memory_space=pltpu.VMEM)
    return pl.pallas_call(
        kernel,
        out_shape=[jax.ShapeDtypeStruct(s, d) for s, d in outs],
        in_specs=[vmem] * len(args),
        out_specs=[vmem] * len(outs),
        scratch_shapes=[pltpu.VMEM(s, d) for s, d in scratch],
        compiler_params=pltpu.CompilerParams(vmem_limit_bytes=limit * 2**20),
    )(*args)


def block(i, j, pitch):
    return pl.ds(pl.multiple_of((i * pitch + j) * 8, 8), 8)


def comb(i, j, pitch, h, cb):
    return pl.ds((i * pitch + j) * 8 + h * 4 + cb, 8, stride=8)


def route_kernel(col_ref, row_ref, obs_ref, out_ref):
    row = row_ref[...]
    count = row.shape[1]
    earlier = lax.broadcasted_iota(jnp.int32, (count, count), 0) < lax.broadcasted_iota(
        jnp.int32, (count, count), 1
    )
    same = jnp.where((col_ref[...] == row) & earlier, 1.0, 0.0)
    rank = jnp.sum(same, axis=0, keepdims=True).astype(jnp.int32)
    place = row * 8 + rank
    lines = out_ref.shape[0]
    line = lax.broadcasted_iota(jnp.int32, (lines, count), 0)
    chosen = jnp.where((line - (line & 4)) == place, 1.0, 0.0).astype(BF16)
    moved = dot(chosen, obs_ref[...])
    first = (lax.broadcasted_iota(jnp.int32, (lines, LANE), 0) & 4) == 0
    out_ref[...] = jnp.where(first, moved[:, :LANE], moved[:, LANE:]).astype(BF16)


def embed_kernel(got_ref, weights_ref, w_embed_ref, pick_ref, grid_ref, emb_ref, *strip_refs):
    got = got_ref[...].astype(F32)
    first = (lax.broadcasted_iota(jnp.int32, got.shape, 0) & 4) == 0
    spread = jnp.concatenate(
        [jnp.where(first, got, 0.0), jnp.where(first, 0.0, got)], axis=1
    ).astype(BF16)
    gridded = dot(weights_ref[...], spread).astype(BF16)
    grid_ref[...] = gridded
    embedded = dot(gridded, w_embed_ref[...]).astype(BF16)
    emb_ref[...] = embedded
    strips = dot(pick_ref[...], embedded).astype(BF16)
    for k, ref in enumerate(strip_refs):
        ref[...] = strips[k * STRIP : (k + 1) * STRIP]


def forward_kernel(
    emb_ref, s0, s1, s2, s3, place_ref, kern_ref, gain_ref, w_one_ref, d_act_ref, cot_ref,
    field_ref, normal_ref, inv_ref, active_ref, d_hid_ref, one_ref, two_ref,
    cells_ref, flat_ref, conv_ref, scaled_ref,
):
    cells_ref[0:CELLS] = emb_ref[...]
    for k, ref in enumerate((s0, s1, s2, s3)):
        cells_ref[CELLS + k * STRIP : CELLS + (k + 1) * STRIP] = ref[...]
    flat_ref[...] = dot(place_ref[...], cells_ref[...])
    for x in range(FULL):
        for g in range(3):
            for cb in range(4):
                value = flat_ref[pl.ds(x * PITCH + 8 * g, 8), pl.ds(cb * LANE, LANE)]
                if x < ROWS2:
                    field_ref[comb(x, 8 * g, PITCH, 0, cb), :] = value
                if x >= HALF:
                    field_ref[comb(x - HALF, 8 * g, PITCH, 1, cb), :] = value

    def conv_row(i, carry):
        sums = [jnp.zeros((8, LANE), F32)] * SIDE
        for a in range(TAPS):
            taps = [kern_ref[pl.ds((a * TAPS + b) * 8, 8), :] for b in range(TAPS)]
            for y in range(FULL):
                here = field_ref[block(i + a, y, PITCH), :]
                for b in range(TAPS):
                    if 0 <= y - b < SIDE:
                        sums[y - b] = sums[y - b] + here * taps[b]
        for j in range(SIDE):
            conv_ref[block(i, j, SIDE), :] = sums[j]
        return carry

    lax.fori_loop(0, HALF, conv_row, 0)

    for r in range(SIDE):
        h, i = divmod(r, HALF)
        parts = [
            jnp.concatenate([conv_ref[comb(i, 8 * g, SIDE, h, cb), :] for g in range(2)], axis=0)
            for cb in range(4)
        ]
        value = jnp.concatenate(parts, axis=1)
        centred = value - jnp.mean(value, axis=1, keepdims=True)
        inverse = lax.rsqrt(jnp.mean(centred * centred, axis=1, keepdims=True) + 1e-06)
        normal = centred * inverse
        rows = pl.ds(r * SIDE, SIDE)
        normal_ref[rows, :] = normal
        inv_ref[rows, :] = jnp.broadcast_to(inverse, (SIDE, LANE))
        scaled_ref[rows, :] = (normal * gain_ref[...]).astype(BF16)

    step = 256
    for k in range(w_one_ref.shape[1] // step):
        some = pl.ds(k * step, step)
        pre = dot(scaled_ref[...], w_one_ref[:, some])
        square = pre * pre
        tanh = jnp.tanh(pre * (ROOT + (ROOT * CUBE) * square))
        upper = 0.5 + 0.5 * tanh
        active = (pre * upper).astype(BF16)
        slope = upper + (0.5 * pre) * (1.0 - tanh * tanh) * (ROOT + (3.0 * ROOT * CUBE) * square)
        d_hid = (d_act_ref[:, some] * slope).astype(BF16)
        active_ref[:, some] = active
        d_hid_ref[:, some] = d_hid
        two_ref[some, :] = dot(active, cot_ref[...], TN).astype(two_ref.dtype)
        one_ref[:, some] = dot(scaled_ref[...], d_hid, TN).astype(one_ref.dtype)


def backward_kernel(
    emb_ref, field_ref, normal_ref, inv_ref, active_ref, d_hid_ref, w_one_ref, w_two_ref,
    gain_ref, kern_ref, cot_ref, back_ref,
    out_ref, taps_ref, gain_out_ref, inner_ref, t0, t1, t2, t3,
    d_scaled_ref, d_conv_ref, spread_ref, flat_ref,
):
    d_scaled_ref[...] = dot(d_hid_ref[...], w_one_ref[...], NT)
    total = jnp.zeros((SIDE, normal_ref.shape[1]), F32)
    for r in range(SIDE):
        h, i = divmod(r, HALF)
        rows = pl.ds(r * SIDE, SIDE)
        normal, d_scaled = normal_ref[rows, :], d_scaled_ref[rows, :]
        total = total + d_scaled * normal
        d_normal = d_scaled * gain_ref[...]
        mean = jnp.mean(d_normal, axis=1, keepdims=True)
        along = jnp.mean(d_normal * normal, axis=1, keepdims=True)
        d_conv = (d_normal - mean - normal * along) * inv_ref[rows, 0:1]
        for g in range(2):
            for cb in range(4):
                d_conv_ref[comb(i, 8 * g, SIDE, h, cb), :] = d_conv[
                    8 * g : 8 * g + 8, cb * LANE : (cb + 1) * LANE
                ]
    gain_out_ref[...] = jnp.sum(total, axis=0, keepdims=True)

    spread_ref[...] = jnp.zeros_like(spread_ref)
    taps_ref[...] = jnp.zeros_like(taps_ref)

    def conv_row(i, carry):
        for a in range(TAPS):
            taps = [kern_ref[pl.ds((a * TAPS + b) * 8, 8), :] for b in range(TAPS)]
            for y in range(FULL):
                value = spread_ref[block(i + a, y, PITCH), :]
                for b in range(TAPS):
                    if 0 <= y - b < SIDE:
                        value = value + d_conv_ref[block(i, y - b, SIDE), :] * taps[b]
                spread_ref[block(i + a, y, PITCH), :] = value
        return carry

    lax.fori_loop(0, HALF, conv_row, 0)

    def tap_row(i, carry):
        for a in range(TAPS):
            sums = [taps_ref[pl.ds((a * TAPS + b) * 8, 8), :] for b in range(TAPS)]
            for y in range(FULL):
                here = field_ref[block(i + a, y, PITCH), :]
                for b in range(TAPS):
                    if 0 <= y - b < SIDE:
                        sums[b] = sums[b] + here * d_conv_ref[block(i, y - b, SIDE), :]
            for b in range(TAPS):
                taps_ref[pl.ds((a * TAPS + b) * 8, 8), :] = sums[b]
        return carry

    lax.fori_loop(0, HALF, tap_row, 0)

    def field_part(x, start, cb):
        value = None
        if x < ROWS2:
            value = spread_ref[comb(x, start, PITCH, 0, cb), :]
        if x >= HALF:
            more = spread_ref[comb(x - HALF, start, PITCH, 1, cb), :]
            value = more if value is None else value + more
        return value

    for x in range(FULL):
        for cb in range(4):
            lanes = pl.ds(cb * LANE, LANE)
            for g in range(3):
                flat_ref[pl.ds(x * PITCH + 8 * g, 8), lanes] = field_part(x, 8 * g, cb)
            if HALO <= x < SIDE + HALO:
                for g in range(2):
                    rows = pl.ds((x - HALO) * SIDE + 8 * g, 8)
                    inner_ref[rows, lanes] = field_part(x, HALO + 8 * g, cb)
    inner_ref[...] = inner_ref[...] + cot_ref[...].astype(F32)
    strips = dot(back_ref[...], flat_ref[...].astype(BF16)).astype(BF16)
    for k, ref in enumerate((t0, t1, t2, t3)):
        ref[...] = strips[k * STRIP : (k + 1) * STRIP]
    out_ref[...] = (emb_ref[...].astype(F32) + dot(active_ref[...], w_two_ref[...])).astype(BF16)


def collect_kernel(inner_ref, t0, t1, t2, t3, add_ref, grid_ref, out_ref, cells_ref):
    for k, ref in enumerate((t0, t1, t2, t3)):
        cells_ref[k * STRIP : (k + 1) * STRIP] = ref[...]
    d_round = (inner_ref[...] + dot(add_ref[...], cells_ref[...])).astype(BF16)
    out_ref[...] = dot(grid_ref[...], d_round, TN)


def turned(spin, x, y, last):
    row = jnp.where(spin == 0, x, jnp.where(spin == 1, last - y, jnp.where(spin == 2, last - x, y)))
    col = jnp.where(spin == 0, y, jnp.where(spin == 1, x, jnp.where(spin == 2, last - y, last - x)))
    return row, col


def selectors(spin):
    p = jnp.arange(FULL * PITCH, dtype=jnp.int32)
    x, y = p // PITCH, p % PITCH
    row, col = turned(spin, x, y, FULL - 1)
    end = SIDE + HALO
    in_row, in_col = (row >= HALO) & (row < end), (col >= HALO) & (col < end)
    strip = jnp.where(
        (row < HALO) & in_col, row * SIDE + col - HALO,
        jnp.where((row >= end) & in_col, STRIP + (row - end) * SIDE + col - HALO,
        jnp.where((col < HALO) & in_row, 2 * STRIP + col * SIDE + row - HALO,
        jnp.where((col >= end) & in_row, 3 * STRIP + (col - end) * SIDE + row - HALO, -1))),
    )
    strip = jnp.where(y < FULL, strip, -1)
    own = (x >= HALO) & (x < end) & (y >= HALO) & (y < end)
    source = jnp.where(own, (x - HALO) * SIDE + y - HALO, jnp.where(strip >= 0, strip + CELLS, -1))
    place = (source[:, None] == jnp.arange(CELLS + 4 * STRIP, dtype=jnp.int32)[None]).astype(BF16)
    back = (jnp.arange(4 * STRIP, dtype=jnp.int32)[:, None] == strip[None]).astype(BF16)

    q = jnp.arange(CELLS, dtype=jnp.int32)
    row, col = turned(spin, q // SIDE, q % SIDE, SIDE - 1)
    cut = SIDE - HALO
    by_row = jnp.where(row >= cut, (row - cut) * SIDE + col, jnp.where(row < HALO, STRIP + row * SIDE + col, -1))
    by_col = jnp.where(col >= cut, 2 * STRIP + (col - cut) * SIDE + row, jnp.where(col < HALO, 3 * STRIP + col * SIDE + row, -1))
    k = jnp.arange(4 * STRIP, dtype=jnp.int32)
    pick = ((k[:, None] == by_row[None]) | (k[:, None] == by_col[None])).astype(BF16)
    add = ((by_row[:, None] == k[None]) | (by_col[:, None] == k[None])).astype(BF16)
    return place, back, pick, add


def exchange(strips, forth):
    moves = (("face", 1), ("face", -1), ("tile", 1), ("tile", -1))
    out = []
    for strip, (axis, way) in zip(strips, moves):
        size, way = lax.axis_size(axis), way if forth else -way
        out.append(lax.ppermute(strip, axis, [(i, (i + way) % size) for i in range(size)]))
    return out


def on_device(
    obs_values, obs_tile, interp, tile_spin, w_embed, dw_kernel, norm_gain, w_one, w_two, cotangent
):
    tiles = lax.axis_size(BOTH)
    width, channels = w_embed.shape
    hidden = w_one.shape[1]
    slots = interp.shape[2]
    place, back, pick, add = selectors(tile_spin[0, 0])
    taps = jnp.broadcast_to(
        dw_kernel.astype(F32).reshape(TAPS * TAPS, 1, 4, LANE), (TAPS * TAPS, 2, 4, LANE)
    ).reshape(TAPS * TAPS * 8, LANE)
    gain = norm_gain.astype(F32)[None]
    weights = jnp.concatenate([interp[0], interp[0]], axis=1).reshape(tiles * 2 * slots, CELLS).T

    (leaving,) = call(
        route_kernel, [((tiles * 8, LANE), BF16)], [], 16,
        obs_tile, obs_tile.reshape(1, -1), obs_values,
    )
    arrived = lax.all_to_all(leaving.reshape(tiles, 8, LANE), BOTH, 0, 0, tiled=True)
    d_active = dot(cotangent, w_two, NT)

    strip = ((STRIP, channels), BF16)
    gridded, embedded, *strips = call(
        embed_kernel, [((CELLS, width), BF16), ((CELLS, channels), BF16)] + [strip] * 4, [], 16,
        arrived.reshape(tiles * 8, LANE), weights, w_embed, pick,
    )
    strips = exchange(strips, True)
    cells2 = ROWS2 * PITCH * 8
    field, normal, inverse, active, d_hidden, grad_one, grad_two = call(
        forward_kernel,
        [
            ((cells2, LANE), F32),
            ((CELLS, channels), F32),
            ((CELLS, LANE), F32),
            ((CELLS, hidden), BF16),
            ((CELLS, hidden), BF16),
            ((channels, hidden), BF16),
            ((hidden, channels), BF16),
        ],
        [
            ((CELLS + 4 * STRIP, channels), BF16),
            ((FULL * PITCH, channels), F32),
            ((CELLS * 4, LANE), F32),
            ((CELLS, channels), BF16),
        ],
        40,
        embedded, *strips, place, taps, gain, w_one, d_active, cotangent,
    )
    grad_one, grad_two = lax.psum((grad_one, grad_two), BOTH)

    output, grad_taps, grad_gain, inner, *strips = call(
        backward_kernel,
        [
            ((CELLS, channels), BF16),
            ((TAPS * TAPS * 8, LANE), F32),
            ((1, channels), F32),
            ((CELLS, channels), F32),
        ]
        + [strip] * 4,
        [
            ((CELLS, channels), F32),
            ((CELLS * 4, LANE), F32),
            ((cells2, LANE), F32),
            ((FULL * PITCH, channels), F32),
        ],
        40,
        embedded, field, normal, inverse, active, d_hidden, w_one, w_two, gain, taps, cotangent, back,
    )
    strips = exchange(strips, False)
    (grad_embed,) = call(
        collect_kernel, [((width, channels), F32)], [((4 * STRIP, channels), BF16)], 16,
        inner, *strips, add, gridded,
    )
    grad_kernel = jnp.sum(grad_taps.reshape(TAPS * TAPS, 2, 4 * LANE), axis=1)
    small = jnp.concatenate([grad_embed, grad_kernel, grad_gain], axis=0)
    small = lax.psum(small, BOTH)
    return (
        output,
        small[:width],
        small[width : width + TAPS * TAPS],
        small[width + TAPS * TAPS],
        grad_one.astype(F32),
        grad_two.astype(F32),
    )


def solution(mesh):
    split = P(BOTH, None)
    in_specs = (split, split, P(BOTH, None, None, None), split) + (P(),) * 5 + (split,)
    return jax.shard_map(
        on_device, mesh=mesh, in_specs=in_specs, out_specs=(split,) + (P(),) * 5, check_vma=False
    )
```

time: 479 us -> 395 us (0.82); the launches traced: 471 us -> 395 us
  waiting for transfers between devices: 108 us -> 312 us
  local copies, waits for them, and re-layouts: 139 us -> 13.2 us
  blocking collectives: 71.9 us -> 0 us
  other arithmetic: 57.9 us -> 9.73 us
  loops' own time: 30.4 us -> 0 us
  matrix products: 23.8 us -> 3.66 us
  Pallas kernels: 0 us -> 19.1 us
    psum x1 -> x2, waiting for transfers between devices: 94.1 us -> 299 us  [the longest x1 153 us: on_device(): grad_one, grad_two = lax.psum((grad_one, grad_two), BOTH)]
    add x49 -> x0, local copies, waits for them, and re-layouts: 95.8 us -> none
    psum x1 -> x0, blocking collectives: 71.9 us -> none  [on_device(): lax.psum((grad_embed, grad_kernel, grad_gain, grad_one, grad_two), ('face...]
    reduce_sum x6 -> x1, other arithmetic: 30.7 us -> 0.24 us  [on_device(): grad_kernel = jnp.sum(grad_taps.reshape(TAPS * TAPS, 2, 4 * LANE), axis=1)]
    another operation x4 -> x0, loops' own time: 30.4 us -> none  [quarter_turn(): lax.switch(quarter, [partial(jnp.rot90, k=turns, axes=(0, 1)) for turns i...]
    add x4 -> x0, other arithmetic: 21.2 us -> none  [the longest x1 20.4 us: tile_pass(): d_field + spread[6 - row_shift:12 - row_shift + side_len, 6 - col_shift:1...]
    dot_general x10 -> x1, matrix products: 23.8 us -> 3.66 us  [dot(): return lax.dot_general(a, b, dims, preferred_element_type=F32)]
    pallas_call x0 -> x5, Pallas kernels: none -> 19.1 us  [call(): pl.pallas_call(kernel, out_shape=[jax.ShapeDtypeStruct(s, d) for s, d in...]
  transfers between devices with their start and end apart: 10 -> 11, of which waited for: 7 -> 7; matrix products, arithmetic and copies ran while one was open for 5% -> 3% of each run, Pallas kernels for 0% -> 0%
where the time goes in v1:
time: 395 us
  waiting for transfers between devices  312 us (79%)
  starting transfers between devices  22.5 us (6%)
  Pallas kernels  19.1 us (5%)
  between operations  14.9 us (4%)
  local copies, waits for them, and re-layouts  13.2 us (3%)
  other arithmetic  9.73 us (2%)
    psum x1, waiting for transfers between devices, on_device(): grad_one, grad_two = lax.psum((grad_one, grad_two), BOTH)  153 us
    psum x1, waiting for transfers between devices, on_device(): small = lax.psum(small, BOTH)  146 us
    pallas_call x5, Pallas kernels, call(): pl.pallas_call(kernel, out_shape=[jax.ShapeDtypeStruct(s, d) for s, d in...  19.1 us
    all_to_all x1, starting transfers between devices, on_device(): lax.all_to_all(leaving.reshape(tiles, 8, LANE), BOTH, 0, 0, tiled=True)  12 us
    ppermute x8, starting transfers between devices, exchange(): lax.ppermute(strip, axis, [(i, (i + way) % size) for i in range(size)])  10.5 us
  transfers between devices with their start and end apart: 11, of which 7 were waited for; matrix products, arithmetic and copies ran while one was open for 3% of the time, Pallas kernels for 0%

profile of v1, /device:TPU:1, one launch (start us, length us, event | category | flops | bytes accessed | tf_op | source)
XLA Modules:
  0.0 394.7 jit_solution(4149422961225707682)
XLA Ops:
  9.6 1.1 shard_map.145
  10.7 12.0 %all-to-all-start = ((bf16[128,8,128]{2,1,0:T(8,128)(2,1)}), bf16[128,8,128]{2,1,0:T(8,128)(2,1)}, u32[]{:S(2)}, u32[]{:S(2)}) async-start(bf16[128,8,128]{2,1,0:T(8,128)(2,1)} %bitcast.1), calls=%async_computation | async-start | bytes 524288 | tf_op jit(solution)/shard_map/all_to_all | solution.py:297
  22.7 1.3 maximum_bitcast_fusion
  24.8 3.7 fusion.30.d_act_ref
  28.8 4.4 %all-to-all-done = bf16[128,8,128]{2,1,0:T(8,128)(2,1)} async-done(((bf16[128,8,128]{2,1,0:T(8,128)(2,1)}), bf16[128,8,128]{2,1,0:T(8,128)(2,1)}, u32[]{:S(2)}, u32[]{:S(2)}) %all-to-all-start) | async-done | bytes 262176 | tf_op jit(solution)/shard_map/all_to_all | solution.py:297
  33.2 0.9 copy-done.6
  34.1 2.3 shard_map.146
  38.0 3.5 collective-permute-start.1
  41.4 2.2 collective-permute-start.2
  45.1 4.3 %collective-permute-done.3.s3 = bf16[48,512]{1,0:T(8,128)(2,1)S(1)} collective-permute-done((bf16[48,512]{1,0:T(8,128)(2,1)}, bf16[48,512]{1,0:T(8,128)(2,1)S(1)}, u32[]{:S(2)}, u32[]{:S(2)}) %collective-permute-start.3) | collective-permute-done | bytes 49184 | tf_op jit(solution)/shard_map/ppermute | solution.py:275
  49.4 1.6 copy-done.2
  52.0 8.9 %shard_map.147 = (f32[2688,128]{1,0:T(8,128)S(1)}, f32[256,512]{1,0:T(8,128)S(1)}, f32[256,128]{1,0:T(8,128)S(1)}, bf16[256,2048]{1,0:T(8,128)(2,1)S(1)}, bf16[2...) custom-call(bf16[256,512]{1,0:T(8,128)(2,1)S(1)} %copy-done.5, ...), custom_call_target="tpu_custom_call" | custom-call | tf_op jit(solution)/shard_map/pallas_call | solution.py:35
  60.9 6.4 %shard_map.148 = (bf16[256,512]{1,0:T(8,128)(2,1)}, f32[392,128]{1,0:T(8,128)S(1)}, f32[1,512]{1,0:T(1,128)S(1)}, f32[256,512]{1,0:T(8,128)S(1)}, bf16[48,512]{1...) custom-call(bf16[256,512]{1,0:T(8,128)(2,1)S(1)} %copy-done.5, ...), custom_call_target="tpu_custom_call" | custom-call | tf_op jit(solution)/shard_map/pallas_call | solution.py:35
  67.2 1.5 collective-permute-start.5
  68.7 1.0 collective-permute-start.6
  69.7 2.2 collective-permute-start.7
  72.5 2.0 collective-permute-done.6.t2
  77.2 146.4 %all-reduce.4.cloned.1.call-done = f32[306,512]{1,0:T(8,128)} async-done(((f32[306,512]{1,0:T(8,128)}), f32[306,512]{1,0:T(8,128)}) %all-reduce.4.cloned.1.call-update) | async-done | bytes 626704 | tf_op jit(solution)/shard_map/psum | solution.py:354
  223.7 1.9 slice.12
  225.5 1.6 slice.13
  227.1 1.3 slice.14
  228.4 152.6 %all-reduce.6.cloned.1.call-done = (bf16[512,2048]{1,0:T(8,128)(2,1)}, bf16[2048,512]{1,0:T(8,128)(2,1)}) async-done(((bf16[512,2048]{1,0:T(8,128)(2,1)}, bf16[2048,512]{1,0:T(8,128)(2,1)}), (bf16[512,2048]{1,0:T(8,128)(2,1)}, bf16[2048,512]{1,0:T(8,128)(2,1)})) %all-reduce.6.cloned.1.call-update) | async-done | bytes 4194320 | tf_op jit(solution)/shard_map/psum | solution.py:327
  380.9 4.3 %convert_element_type.24 = f32[512,2048]{1,0:T(8,128)} convert(bf16[512,2048]{1,0:T(8,128)(2,1)} %get-tuple-element.48) | non-fusion elementwise | flops 1048576 | bytes 6291456 | tf_op jit(solution)/shard_map/convert_element_type | solution.py:360
  385.2 2.6 convert_element_type.25
  (52 shorter events, 10.1 us)
Async XLA Ops:
  7.2 17.6 %copy-start.3 = (bf16[256,512]{1,0:T(8,128)(2,1)S(1)}, bf16[256,512]{1,0:T(8,128)(2,1)}, u32[]{:S(2)}) copy-start(bf16[256,512]{1,0:T(8,128)(2,1)} %cot_ref.3) | copy-start | bytes 786436
  8.0 0.9 copy-start.9
  8.9 0.7 copy-start.10
  10.7 22.5 %all-to-all-start = ((bf16[128,8,128]{2,1,0:T(8,128)(2,1)}), bf16[128,8,128]{2,1,0:T(8,128)(2,1)}, u32[]{:S(2)}, u32[]{:S(2)}) async-start(bf16[128,8,128]{2,1,0:T(8,128)(2,1)} %bitcast.1), calls=%async_computation | async-start | bytes 524288 | tf_op jit(solution)/shard_map/all_to_all | solution.py:297
  22.7 201.0 %all-reduce.4.cloned.1.call-start = ((), (), s32[]{:S(2)}) async-start(), calls=%async_computation.1 | async-start | bytes 1277952 | tf_op jit(solution)/shard_map/psum | solution.py:354
  24.8 19.8 %copy-start.12 = (bf16[512]{0:T(512)(128)(2,1)S(1)}, bf16[512]{0:T(512)(128)(2,1)}, u32[]{:S(2)}) copy-start(bf16[512]{0:T(512)(128)(2,1)} %param.16) | copy-start | bytes 3076
  28.4 21.0 %copy-start = (bf16[512,2048]{1,0:T(8,128)(2,1)S(1)}, bf16[512,2048]{1,0:T(8,128)(2,1)}, u32[]{:S(2)}) copy-start(bf16[512,2048]{1,0:T(8,128)(2,1)} %w_one_ref.3) | copy-start | bytes 6291460
  33.2 1.0 copy-start.6
  36.5 0.7 copy-start.4
  37.2 0.7 copy-start.7
  37.8 6.7 %collective-permute-start = (bf16[48,512]{1,0:T(8,128)(2,1)}, bf16[48,512]{1,0:T(8,128)(2,1)S(1)}, u32[]{:S(2)}, u32[]{:S(2)}) collective-permute-start(bf16[48,512]{1,0:T(8,128)(2,1)} %get-tuple-element.28), channel_id=1, source_target_pairs={{0,16},{16,32},{32,48},{48,64},{64,80},{80,96},{96,112},{112,0},{1... | collective-permute-start | bytes 147464 | tf_op jit(solution)/shard_map/ppermute | solution.py:275
  38.0 6.6 %collective-permute-start.1 = (bf16[48,512]{1,0:T(8,128)(2,1)}, bf16[48,512]{1,0:T(8,128)(2,1)S(1)}, u32[]{:S(2)}, u32[]{:S(2)}) collective-permute-start(bf16[48,512]{1,0:T(8,128)(2,1)} %get-tuple-element.29), channel_id=1, source_target_pairs={{0,112},{16,0},{32,16},{48,32},{64,48},{80,64},{96,80},{112,96},{1... | collective-permute-start | bytes 147464 | tf_op jit(solution)/shard_map/ppermute | solution.py:275
  41.4 3.7 collective-permute-start.2
  43.6 5.8 %collective-permute-start.3 = (bf16[48,512]{1,0:T(8,128)(2,1)}, bf16[48,512]{1,0:T(8,128)(2,1)S(1)}, u32[]{:S(2)}, u32[]{:S(2)}) collective-permute-start(bf16[48,512]{1,0:T(8,128)(2,1)} %get-tuple-element.31), channel_id=1, source_target_pairs={{0,15},{1,0},{2,1},{3,2},{4,3},{5,4},{6,5},{7,6},{8,7},{9,8},{10,9... | collective-permute-start | bytes 147464 | tf_op jit(solution)/shard_map/ppermute | solution.py:275
  49.4 1.6 copy-start.2
  51.0 0.9 copy-start.5
  52.0 8.9 %copy-start.1 = (bf16[2048,512]{1,0:T(8,128)(2,1)S(1)}, bf16[2048,512]{1,0:T(8,128)(2,1)}, u32[]{:S(2)}) copy-start(bf16[2048,512]{1,0:T(8,128)(2,1)} %w_two_ref.1) | copy-start | bytes 6291460
  60.9 14.3 %copy-start.8 = (bf16[256,256]{1,0:T(8,128)(2,1)S(1)}, bf16[256,256]{1,0:T(8,128)(2,1)}, u32[]{:S(2)}) copy-start(bf16[256,256]{1,0:T(8,128)(2,1)} %copy-done.7) | copy-start | bytes 393220
  67.2 5.2 %collective-permute-start.4 = (bf16[48,512]{1,0:T(8,128)(2,1)}, bf16[48,512]{1,0:T(8,128)(2,1)S(1)}, u32[]{:S(2)}, u32[]{:S(2)}) collective-permute-start(bf16[48,512]{1,0:T(8,128)(2,1)} %get-tuple-element.39), channel_id=1, source_target_pairs={{0,112},{16,0},{32,16},{48,32},{64,48},{80,64},{96,80},{112,96},{1... | collective-permute-start | bytes 147464 | tf_op jit(solution)/shard_map/ppermute | solution.py:275
  67.2 5.3 %collective-permute-start.5 = (bf16[48,512]{1,0:T(8,128)(2,1)}, bf16[48,512]{1,0:T(8,128)(2,1)S(1)}, u32[]{:S(2)}, u32[]{:S(2)}) collective-permute-start(bf16[48,512]{1,0:T(8,128)(2,1)} %get-tuple-element.40), channel_id=1, source_target_pairs={{0,16},{16,32},{32,48},{48,64},{64,80},{80,96},{96,112},{112,0},{1... | collective-permute-start | bytes 147464 | tf_op jit(solution)/shard_map/ppermute | solution.py:275
  68.7 5.8 %collective-permute-start.6 = (bf16[48,512]{1,0:T(8,128)(2,1)}, bf16[48,512]{1,0:T(8,128)(2,1)S(1)}, u32[]{:S(2)}, u32[]{:S(2)}) collective-permute-start(bf16[48,512]{1,0:T(8,128)(2,1)} %get-tuple-element.41), channel_id=1, source_target_pairs={{0,15},{1,0},{2,1},{3,2},{4,3},{5,4},{6,5},{7,6},{8,7},{9,8},{10,9... | collective-permute-start | bytes 147464 | tf_op jit(solution)/shard_map/ppermute | solution.py:275
  69.7 5.4 %collective-permute-start.7 = (bf16[48,512]{1,0:T(8,128)(2,1)S(1)}, bf16[48,512]{1,0:T(8,128)(2,1)S(1)}, u32[]{:S(2)}, u32[]{:S(2)}) collective-permute-start(bf16[48,512]{1,0:T(8,128)(2,1)S(1)} %get-tuple-element.42), channel_id=1, source_target_pairs={{0,1},{1,2},{2,3},{3,4},{4,5},{5,6},{6,7},{7,8},{8,9},{9,10},{10,1... | collective-permute-start | bytes 147464 | tf_op jit(solution)/shard_map/ppermute | solution.py:275
  76.5 304.5 %all-reduce.6.cloned.1.call-start = ((), (), s32[]{:S(2)}) async-start(), calls=%async_computation.2 | async-start | bytes 8388608 | tf_op jit(solution)/shard_map/psum | solution.py:327
  380.9 4.3 %copy-start.11 = (bf16[2048,512]{1,0:T(8,128)(2,1)S(1)}, bf16[2048,512]{1,0:T(8,128)(2,1)}, u32[]{:S(2)}) copy-start(bf16[2048,512]{1,0:T(8,128)(2,1)} %get-tuple-element.49) | copy-start | bytes 6291460
Sparse Core Ops, SparseCore 0:
  76.6 147.0 all-reduce.3
  229.4 151.5 all-reduce.5

commit v2 on v1

--- a/solution.py
+++ b/solution.py
@@ -17,7 +17,9 @@
 LANE = 128
 ROWS2 = HALF + TAPS - 1
 STRIP = HALO * SIDE
-BOTH = ("face", "tile")
+STEP = 256
+ALL = ("face", "col", "core")
+CHIPS = ("face", "col")
 ROOT = 0.7978845608028654
 CUBE = 0.044715
 
@@ -31,11 +33,11 @@
 
 
 def call(kernel, outs, scratch, limit, *args):
-    vmem = pl.BlockSpec(memory_space=pltpu.VMEM)
+    vmem, scalar = pl.BlockSpec(memory_space=pltpu.VMEM), pl.BlockSpec(memory_space=pltpu.SMEM)
     return pl.pallas_call(
         kernel,
         out_shape=[jax.ShapeDtypeStruct(s, d) for s, d in outs],
-        in_specs=[vmem] * len(args),
+        in_specs=[scalar if a.shape == (1,) else vmem for a in args],
         out_specs=[vmem] * len(outs),
         scratch_shapes=[pltpu.VMEM(s, d) for s, d in scratch],
         compiler_params=pltpu.CompilerParams(vmem_limit_bytes=limit * 2**20),
@@ -75,21 +77,30 @@
     ).astype(BF16)
     gridded = dot(weights_ref[...], spread).astype(BF16)
     grid_ref[...] = gridded
-    embedded = dot(gridded, w_embed_ref[...]).astype(BF16)
-    emb_ref[...] = embedded
-    strips = dot(pick_ref[...], embedded).astype(BF16)
+    emb_ref[...] = dot(gridded, w_embed_ref[...]).astype(BF16)
+    strips = dot(pick_ref[...], gridded).astype(BF16)
     for k, ref in enumerate(strip_refs):
         ref[...] = strips[k * STRIP : (k + 1) * STRIP]
 
 
+def tiles_of(part, two, one):
+    for k in range(64):
+        r, c = divmod(k, 4)
+        yield part * 128 + k, two, pl.ds(r * 16, 16), pl.ds(c * LANE, LANE)
+    for k in range(64):
+        r, c = divmod(k, 2)
+        yield part * 128 + 64 + k, one, pl.ds(r * 16, 16), pl.ds(c * LANE, LANE)
+
+
 def forward_kernel(
-    emb_ref, s0, s1, s2, s3, place_ref, kern_ref, gain_ref, w_one_ref, d_act_ref, cot_ref,
-    field_ref, normal_ref, inv_ref, active_ref, d_hid_ref, one_ref, two_ref,
-    cells_ref, flat_ref, conv_ref, scaled_ref,
+    core_ref, emb_ref, s0, s1, s2, s3, place_ref, kern_ref, gain_ref, w_embed_ref, w_one_ref, d_act_ref, cot_ref,
+    field_ref, normal_ref, inv_ref, scaled_ref, active_ref, d_hid_ref, theirs_ref,
+    strips_ref, cells_ref, flat_ref, conv_ref, two_ref, one_ref,
 ):
+    for k, ref in enumerate((s0, s1, s2, s3)):
+        strips_ref[k * STRIP : (k + 1) * STRIP] = ref[...]
     cells_ref[0:CELLS] = emb_ref[...]
-    for k, ref in enumerate((s0, s1, s2, s3)):
-        cells_ref[CELLS + k * STRIP : CELLS + (k + 1) * STRIP] = ref[...]
+    cells_ref[CELLS:] = dot(strips_ref[...], w_embed_ref[...]).astype(BF16)
     flat_ref[...] = dot(place_ref[...], cells_ref[...])
     for x in range(FULL):
         for g in range(3):
@@ -130,27 +141,30 @@
         inv_ref[rows, :] = jnp.broadcast_to(inverse, (SIDE, LANE))
         scaled_ref[rows, :] = (normal * gain_ref[...]).astype(BF16)
 
-    step = 256
-    for k in range(w_one_ref.shape[1] // step):
-        some = pl.ds(k * step, step)
+    for k in range(w_one_ref.shape[1] // STEP):
+        some = pl.ds(k * STEP, STEP)
         pre = dot(scaled_ref[...], w_one_ref[:, some])
         square = pre * pre
         tanh = jnp.tanh(pre * (ROOT + (ROOT * CUBE) * square))
         upper = 0.5 + 0.5 * tanh
-        active = (pre * upper).astype(BF16)
         slope = upper + (0.5 * pre) * (1.0 - tanh * tanh) * (ROOT + (3.0 * ROOT * CUBE) * square)
-        d_hid = (d_act_ref[:, some] * slope).astype(BF16)
-        active_ref[:, some] = active
-        d_hid_ref[:, some] = d_hid
-        two_ref[some, :] = dot(active, cot_ref[...], TN).astype(two_ref.dtype)
-        one_ref[:, some] = dot(scaled_ref[...], d_hid, TN).astype(one_ref.dtype)
+        active_ref[:, some] = (pre * upper).astype(BF16)
+        d_hid_ref[:, some] = (d_act_ref[:, some] * slope).astype(BF16)
+
+    steps = theirs_ref.shape[0] // 128
+    for k in range(steps):
+        some = pl.ds(pl.multiple_of(((1 - core_ref[0]) * steps + k) * STEP, STEP), STEP)
+        two_ref[...] = dot(active_ref[:, some], cot_ref[...], TN)
+        one_ref[...] = dot(scaled_ref[...], d_hid_ref[:, some], TN)
+        for t, ref, rows, lanes in tiles_of(k, two_ref, one_ref):
+            theirs_ref[t] = ref[rows, lanes].astype(BF16)
 
 
 def backward_kernel(
-    emb_ref, field_ref, normal_ref, inv_ref, active_ref, d_hid_ref, w_one_ref, w_two_ref,
-    gain_ref, kern_ref, cot_ref, back_ref,
-    out_ref, taps_ref, gain_out_ref, inner_ref, t0, t1, t2, t3,
-    d_scaled_ref, d_conv_ref, spread_ref, flat_ref,
+    core_ref, grid_ref, s0, s1, s2, s3, place_ref, field_ref, normal_ref, inv_ref, d_hid_ref, w_one_ref,
+    gain_ref, kern_ref, cot_ref,
+    mine_ref, theirs_ref,
+    d_scaled_ref, d_conv_ref, spread_ref, flat_ref, taps_ref, cells_ref, small_ref,
 ):
     d_scaled_ref[...] = dot(d_hid_ref[...], w_one_ref[...], NT)
     total = jnp.zeros((SIDE, normal_ref.shape[1]), F32)
@@ -168,7 +182,7 @@
                 d_conv_ref[comb(i, 8 * g, SIDE, h, cb), :] = d_conv[
                     8 * g : 8 * g + 8, cb * LANE : (cb + 1) * LANE
                 ]
-    gain_out_ref[...] = jnp.sum(total, axis=0, keepdims=True)
+    grad_gain = jnp.sum(total, axis=0, keepdims=True)
 
     spread_ref[...] = jnp.zeros_like(spread_ref)
     taps_ref[...] = jnp.zeros_like(taps_ref)
@@ -200,36 +214,102 @@
 
     lax.fori_loop(0, HALF, tap_row, 0)
 
-    def field_part(x, start, cb):
-        value = None
-        if x < ROWS2:
-            value = spread_ref[comb(x, start, PITCH, 0, cb), :]
-        if x >= HALF:
-            more = spread_ref[comb(x - HALF, start, PITCH, 1, cb), :]
-            value = more if value is None else value + more
-        return value
-
     for x in range(FULL):
-        for cb in range(4):
-            lanes = pl.ds(cb * LANE, LANE)
-            for g in range(3):
-                flat_ref[pl.ds(x * PITCH + 8 * g, 8), lanes] = field_part(x, 8 * g, cb)
-            if HALO <= x < SIDE + HALO:
-                for g in range(2):
-                    rows = pl.ds((x - HALO) * SIDE + 8 * g, 8)
-                    inner_ref[rows, lanes] = field_part(x, HALO + 8 * g, cb)
-    inner_ref[...] = inner_ref[...] + cot_ref[...].astype(F32)
-    strips = dot(back_ref[...], flat_ref[...].astype(BF16)).astype(BF16)
-    for k, ref in enumerate((t0, t1, t2, t3)):
-        ref[...] = strips[k * STRIP : (k + 1) * STRIP]
+        for g in range(3):
+            for cb in range(4):
+                value = None
+                if x < ROWS2:
+                    value = spread_ref[comb(x, 8 * g, PITCH, 0, cb), :]
+                if x >= HALF:
+                    more = spread_ref[comb(x - HALF, 8 * g, PITCH, 1, cb), :]
+                    value = more if value is None else value + more
+                flat_ref[pl.ds(x * PITCH + 8 * g, 8), pl.ds(cb * LANE, LANE)] = value
+
+    cells_ref[0:CELLS] = grid_ref[...]
+    for k, ref in enumerate((s0, s1, s2, s3)):
+        cells_ref[CELLS + k * STRIP : CELLS + (k + 1) * STRIP] = ref[...]
+    spots = dot(place_ref[...], cells_ref[...]).astype(BF16)
+    grad_embed = dot(spots, flat_ref[...].astype(BF16), TN) + dot(grid_ref[...], cot_ref[...], TN)
+
+    half = mine_ref.shape[0]
+    small_ref[...] = jnp.zeros_like(small_ref)
+    for t in range(half):
+        r, c = divmod(t, 4)
+        small_ref[t * 16 : (t + 1) * 16] = grad_embed[r * 16 : (r + 1) * 16, c * LANE : (c + 1) * LANE]
+    base = half * 16
+    for t in range(TAPS * TAPS):
+        both = taps_ref[t * 8 : (t + 1) * 8, :]
+        small_ref[base + t * 4 : base + (t + 1) * 4] = both[:4] + both[4:]
+    for c in range(4):
+        at = base + TAPS * TAPS * 4 + c
+        small_ref[at : at + 1] = grad_gain[:, c * LANE : (c + 1) * LANE]
+    core = core_ref[0]
+    for t in range(half):
+        mine_ref[t] = small_ref[pl.ds(pl.multiple_of((core * half + t) * 16, 16), 16), :]
+        theirs_ref[t] = small_ref[
+            pl.ds(pl.multiple_of(((1 - core) * half + t) * 16, 16), 16), :
+        ].astype(BF16)
+
+
+def pair_kernel(
+    core_ref, scaled_ref, active_ref, d_hid_ref, cot_ref, big_ref, mine_ref, small_ref, out_ref, two_ref, one_ref
+):
+    steps = big_ref.shape[0] // 128
+    for k in range(steps):
+        some = pl.ds(pl.multiple_of((core_ref[0] * steps + k) * STEP, STEP), STEP)
+        two_ref[...] = dot(active_ref[:, some], cot_ref[...], TN)
+        one_ref[...] = dot(scaled_ref[...], d_hid_ref[:, some], TN)
+        for t, ref, rows, lanes in tiles_of(k, two_ref, one_ref):
+            out_ref[t // 8, t % 8] = (ref[rows, lanes] + big_ref[t].astype(F32)).astype(BF16)
+    for t in range(out_ref.shape[0]):
+        out_ref[t, 8] = (mine_ref[t] + small_ref[t].astype(F32)).astype(BF16)
+
+
+def feature_kernel(emb_ref, active_ref, w_two_ref, out_ref):
     out_ref[...] = (emb_ref[...].astype(F32) + dot(active_ref[...], w_two_ref[...])).astype(BF16)
 
 
-def collect_kernel(inner_ref, t0, t1, t2, t3, add_ref, grid_ref, out_ref, cells_ref):
-    for k, ref in enumerate((t0, t1, t2, t3)):
-        cells_ref[k * STRIP : (k + 1) * STRIP] = ref[...]
-    d_round = (inner_ref[...] + dot(add_ref[...], cells_ref[...])).astype(BF16)
-    out_ref[...] = dot(grid_ref[...], d_round, TN)
+def sum_kernel(in_ref, out_ref):
+    parts, tiles = in_ref.shape[:2]
+
+    def add(d, sums):
+        return [s + in_ref[d, t].astype(F32) for t, s in enumerate(sums)]
+
+    sums = lax.fori_loop(0, parts, add, [jnp.zeros(in_ref.shape[2:], F32)] * tiles)
+    sums = [s.astype(BF16) for s in sums]
+
+    def spread(d, carry):
+        for t in range(tiles):
+            out_ref[d, t] = sums[t]
+        return carry
+
+    lax.fori_loop(0, parts, spread, 0)
+
+
+def assemble_kernel(core_ref, in_ref, *refs):
+    one_ref, two_ref = refs[-2:]
+    for t, ref, rows, lanes in tiles_of(0, two_ref, one_ref):
+        ref[rows, lanes] = in_ref[t // 8, t % 8].astype(F32)
+
+
+def assemble(core, gathered, shapes, before):
+    steps = shapes[0][1] // STEP // 2
+    whole = [pl.BlockSpec(memory_space=pl.ANY)] * len(before)
+    return pl.pallas_call(
+        assemble_kernel,
+        out_shape=[jax.ShapeDtypeStruct(s, F32) for s in shapes],
+        grid_spec=pltpu.PrefetchScalarGridSpec(
+            num_scalar_prefetch=1,
+            grid=(steps,),
+            in_specs=[pl.BlockSpec((16,) + gathered.shape[1:], lambda k, core: (k, 0, 0, 0))] + whole,
+            out_specs=[
+                pl.BlockSpec((shapes[0][0], STEP), lambda k, core: (0, core[0] * steps + k)),
+                pl.BlockSpec((STEP, shapes[1][1]), lambda k, core: (core[0] * steps + k, 0)),
+            ],
+        ),
+        input_output_aliases={2 + k: k for k in range(len(before))},
+        compiler_params=pltpu.CompilerParams(vmem_limit_bytes=24 * 2**20),
+    )(core, gathered, *before)
 
 
 def turned(spin, x, y, last):
@@ -254,7 +334,6 @@
     own = (x >= HALO) & (x < end) & (y >= HALO) & (y < end)
     source = jnp.where(own, (x - HALO) * SIDE + y - HALO, jnp.where(strip >= 0, strip + CELLS, -1))
     place = (source[:, None] == jnp.arange(CELLS + 4 * STRIP, dtype=jnp.int32)[None]).astype(BF16)
-    back = (jnp.arange(4 * STRIP, dtype=jnp.int32)[:, None] == strip[None]).astype(BF16)
 
     q = jnp.arange(CELLS, dtype=jnp.int32)
     row, col = turned(spin, q // SIDE, q % SIDE, SIDE - 1)
@@ -263,27 +342,31 @@
     by_col = jnp.where(col >= cut, 2 * STRIP + (col - cut) * SIDE + row, jnp.where(col < HALO, 3 * STRIP + col * SIDE + row, -1))
     k = jnp.arange(4 * STRIP, dtype=jnp.int32)
     pick = ((k[:, None] == by_row[None]) | (k[:, None] == by_col[None])).astype(BF16)
-    add = ((by_row[:, None] == k[None]) | (by_col[:, None] == k[None])).astype(BF16)
-    return place, back, pick, add
-
-
-def exchange(strips, forth):
-    moves = (("face", 1), ("face", -1), ("tile", 1), ("tile", -1))
+    return place, pick
+
+
+def exchange(strips):
+    moves = (("face", 1), ("face", -1), (("col", "core"), 1), (("col", "core"), -1))
     out = []
     for strip, (axis, way) in zip(strips, moves):
-        size, way = lax.axis_size(axis), way if forth else -way
+        size = lax.axis_size(axis)
         out.append(lax.ppermute(strip, axis, [(i, (i + way) % size) for i in range(size)]))
     return out
+
+
+def swap(value):
+    return lax.ppermute(value, "core", [(0, 1), (1, 0)])
 
 
 def on_device(
     obs_values, obs_tile, interp, tile_spin, w_embed, dw_kernel, norm_gain, w_one, w_two, cotangent
 ):
-    tiles = lax.axis_size(BOTH)
+    tiles, chips = lax.axis_size(ALL), lax.axis_size(CHIPS)
     width, channels = w_embed.shape
     hidden = w_one.shape[1]
     slots = interp.shape[2]
-    place, back, pick, add = selectors(tile_spin[0, 0])
+    core = lax.axis_index("core").reshape(1)
+    place, pick = selectors(tile_spin[0, 0])
     taps = jnp.broadcast_to(
         dw_kernel.astype(F32).reshape(TAPS * TAPS, 1, 4, LANE), (TAPS * TAPS, 2, 4, LANE)
     ).reshape(TAPS * TAPS * 8, LANE)
@@ -294,77 +377,86 @@
         route_kernel, [((tiles * 8, LANE), BF16)], [], 16,
         obs_tile, obs_tile.reshape(1, -1), obs_values,
     )
-    arrived = lax.all_to_all(leaving.reshape(tiles, 8, LANE), BOTH, 0, 0, tiled=True)
+    arrived = lax.all_to_all(leaving.reshape(tiles, 8, LANE), ALL, 0, 0, tiled=True)
     d_active = dot(cotangent, w_two, NT)
 
-    strip = ((STRIP, channels), BF16)
     gridded, embedded, *strips = call(
-        embed_kernel, [((CELLS, width), BF16), ((CELLS, channels), BF16)] + [strip] * 4, [], 16,
+        embed_kernel,
+        [((CELLS, width), BF16), ((CELLS, channels), BF16)] + [((STRIP, width), BF16)] * 4, [], 16,
         arrived.reshape(tiles * 8, LANE), weights, w_embed, pick,
     )
-    strips = exchange(strips, True)
+    strips = exchange(strips)
     cells2 = ROWS2 * PITCH * 8
-    field, normal, inverse, active, d_hidden, grad_one, grad_two = call(
+    flat = ((FULL * PITCH, channels), F32)
+    step_sums = [((STEP, channels), F32), ((channels, STEP), F32)]
+    half = hidden * channels // (16 * LANE)
+    field, normal, inverse, scaled, active, d_hidden, theirs = call(
         forward_kernel,
         [
             ((cells2, LANE), F32),
             ((CELLS, channels), F32),
             ((CELLS, LANE), F32),
+            ((CELLS, channels), BF16),
             ((CELLS, hidden), BF16),
             ((CELLS, hidden), BF16),
-            ((channels, hidden), BF16),
-            ((hidden, channels), BF16),
+            ((half, 16, LANE), BF16),
         ],
         [
+            ((4 * STRIP, width), BF16),
             ((CELLS + 4 * STRIP, channels), BF16),
-            ((FULL * PITCH, channels), F32),
+            flat,
             ((CELLS * 4, LANE), F32),
-            ((CELLS, channels), BF16),
-        ],
+        ]
+        + step_sums,
         40,
-        embedded, *strips, place, taps, gain, w_one, d_active, cotangent,
-    )
-    grad_one, grad_two = lax.psum((grad_one, grad_two), BOTH)
-
-    output, grad_taps, grad_gain, inner, *strips = call(
+        core, embedded, *strips, place, taps, gain, w_embed, w_one, d_active, cotangent,
+    )
+    big = swap(theirs)
+
+    mine, theirs = call(
         backward_kernel,
-        [
-            ((CELLS, channels), BF16),
-            ((TAPS * TAPS * 8, LANE), F32),
-            ((1, channels), F32),
-            ((CELLS, channels), F32),
-        ]
-        + [strip] * 4,
+        [((chips, 16, LANE), F32), ((chips, 16, LANE), BF16)],
         [
             ((CELLS, channels), F32),
             ((CELLS * 4, LANE), F32),
             ((cells2, LANE), F32),
-            ((FULL * PITCH, channels), F32),
+            flat,
+            ((TAPS * TAPS * 8, LANE), F32),
+            ((CELLS + 4 * STRIP, width), BF16),
+            ((2 * chips * 16, LANE), F32),
         ],
         40,
-        embedded, field, normal, inverse, active, d_hidden, w_one, w_two, gain, taps, cotangent, back,
-    )
-    strips = exchange(strips, False)
-    (grad_embed,) = call(
-        collect_kernel, [((width, channels), F32)], [((4 * STRIP, channels), BF16)], 16,
-        inner, *strips, add, gridded,
-    )
-    grad_kernel = jnp.sum(grad_taps.reshape(TAPS * TAPS, 2, 4 * LANE), axis=1)
-    small = jnp.concatenate([grad_embed, grad_kernel, grad_gain], axis=0)
-    small = lax.psum(small, BOTH)
-    return (
-        output,
-        small[:width],
-        small[width : width + TAPS * TAPS],
-        small[width + TAPS * TAPS],
-        grad_one.astype(F32),
-        grad_two.astype(F32),
-    )
+        core, gridded, *strips, place, field, normal, inverse, d_hidden, w_one, gain, taps, cotangent,
+    )
+    small = swap(theirs)
+    (paired,) = call(
+        pair_kernel, [((chips, 9, 16, LANE), BF16)], step_sums, 40,
+        core, scaled, active, d_hidden, cotangent, big, mine, small,
+    )
+    (output,) = call(
+        feature_kernel, [((CELLS, channels), BF16)], [], 16, embedded, active, w_two
+    )
+    paired = lax.all_to_all(paired, CHIPS, 0, 0, tiled=True)
+    (summed,) = call(sum_kernel, [((chips, 9, 16, LANE), BF16)], [], 16, paired)
+    here = lax.all_to_all(summed, CHIPS, 0, 0, tiled=True)
+    there = swap(here)
+    shapes = [(channels, hidden), (hidden, channels)]
+    grads = assemble(core, here, shapes, [])
+    grad_one, grad_two = assemble(1 - core, there, shapes, grads)
+
+    first = jnp.where(core[0] == 0, here[:, 8], there[:, 8]).astype(F32)
+    last = jnp.where(core[0] == 0, there[:, 8], here[:, 8]).astype(F32)
+    grad_embed = first.reshape(16, 4, 16, LANE).transpose(0, 2, 1, 3).reshape(width, channels)
+    count = TAPS * TAPS
+    rows = last.reshape(chips * 16, LANE)[: (count + 1) * 4].reshape(count + 1, channels)
+    return output, grad_embed, rows[:count], rows[count], grad_one, grad_two
 
 
 def solution(mesh):
-    split = P(BOTH, None)
-    in_specs = (split, split, P(BOTH, None, None, None), split) + (P(),) * 5 + (split,)
+    faces, tiles = mesh.shape["face"], mesh.shape["tile"]
+    fine = jax.sharding.Mesh(mesh.devices.reshape(faces, tiles // 2, 2), ALL)
+    split = P(ALL, None)
+    in_specs = (split, split, P(ALL, None, None, None), split) + (P(),) * 5 + (split,)
     return jax.shard_map(
-        on_device, mesh=mesh, in_specs=in_specs, out_specs=(split,) + (P(),) * 5, check_vma=False
-    )
+        on_device, mesh=fine, in_specs=in_specs, out_specs=(split,) + (P(),) * 5, check_vma=False
+    )

time: 395 us -> 152 us (0.38)
  waiting for transfers between devices: 312 us -> 7.71 us
  blocking collectives: 0 us -> 74.8 us
  between operations: 14.9 us -> 1.49 us
  other arithmetic: 9.73 us -> 3.4 us
  Pallas kernels: 19.1 us -> 23.4 us
    psum x2 -> x0, waiting for transfers between devices: 299 us -> none  [the longest x1 153 us: on_device(): grad_one, grad_two = lax.psum((grad_one, grad_two), BOTH)]
    all_to_all x0 -> x2, blocking collectives: none -> 74.8 us  [the longest x1 39 us: on_device(): paired = lax.all_to_all(paired, CHIPS, 0, 0, tiled=True)]
    convert_element_type x4 -> x1, other arithmetic: 7.07 us -> 0.05 us  [on_device(): last = jnp.where(core[0] == 0, there[:, 8], here[:, 8]).astype(F32)]
    pallas_call x0 -> x2, Pallas kernels: none -> 6.56 us  [assemble(): pl.pallas_call(assemble_kernel, out_shape=[jax.ShapeDtypeStruct(s, F32) f...]
    ppermute x8 -> x4, starting transfers between devices: 10.5 us -> 5.73 us  [exchange(): lax.ppermute(strip, axis, [(i, (i + way) % size) for i in range(size)])]
    ppermute x0 -> x3, starting transfers between devices: none -> 4.18 us  [swap(): return lax.ppermute(value, 'core', [(0, 1), (1, 0)])]
    ppermute x8 -> x4, waiting for transfers between devices: 7.47 us -> 3.36 us  [exchange(): lax.ppermute(strip, axis, [(i, (i + way) % size) for i in range(size)])]
    slice x3 -> x2, local copies, waits for them, and re-layouts: 4.72 us -> 0.67 us  [on_device(): return (output, grad_embed, rows[:count], rows[count], grad_one, grad_two)]
  transfers between devices with their start and end apart: 11 -> 8, of which waited for: 7 -> 3; matrix products, arithmetic and copies ran while one was open for 3% -> 6% of each run, Pallas kernels for 0% -> 6%
where the time goes in v2:
time: 152 us; the launch traced here: 151 us
  blocking collectives  74.8 us (49%)
  Pallas kernels  23.4 us (15%)
  starting transfers between devices  21.4 us (14%)
  local copies, waits for them, and re-layouts  15 us (10%)
  waiting for transfers between devices  7.71 us (5%)
  matrix products  3.69 us (2%)
  other arithmetic  3.4 us (2%)
    all_to_all x1, blocking collectives, on_device(): paired = lax.all_to_all(paired, CHIPS, 0, 0, tiled=True)  39 us
    all_to_all x1, blocking collectives, on_device(): here = lax.all_to_all(summed, CHIPS, 0, 0, tiled=True)  35.8 us
    pallas_call x7, Pallas kernels, call(): pl.pallas_call(kernel, out_shape=[jax.ShapeDtypeStruct(s, d) for s, d in...  16.8 us
    all_to_all x1, starting transfers between devices, on_device(): lax.all_to_all(leaving.reshape(tiles, 8, LANE), ALL, 0, 0, tiled=True)  11.5 us
    unnamed x34, local copies, waits for them, and re-layouts  9.73 us
    pallas_call x2, Pallas kernels, assemble(): pl.pallas_call(assemble_kernel, out_shape=[jax.ShapeDtypeStruct(s, F32) f...  6.56 us
    ppermute x4, starting transfers between devices, exchange(): lax.ppermute(strip, axis, [(i, (i + way) % size) for i in range(size)])  5.73 us
    ppermute x3, starting transfers between devices, swap(): return lax.ppermute(value, 'core', [(0, 1), (1, 0)])  4.18 us
  transfers between devices with their start and end apart: 8, of which 3 were waited for; matrix products, arithmetic and copies ran while one was open for 6% of the time, Pallas kernels for 6%

profile of v2, /device:TPU:1, one launch (start us, length us, event | category | flops | bytes accessed | tf_op | source)
XLA Modules:
  0.0 150.9 jit_solution(17485698038008762538)
XLA Ops:
  3.1 1.1 shard_map.145
  4.2 11.5 %all-to-all-start = ((bf16[128,8,128]{2,1,0:T(8,128)(2,1)}), bf16[128,8,128]{2,1,0:T(8,128)(2,1)S(1)}, u32[]{:S(2)}, u32[]{:S(2)}) async-start(bf16[128,8,128]{2,1,0:T(8,128)(2,1)} %bitcast.1), calls=%async_computation | async-start | bytes 524288 | tf_op jit(solution)/shard_map/all_to_all | solution.py:380
  16.3 2.1 %maximum_bitcast_fusion = bf16[1024,256]{1,0:T(8,128)(2,1)} fusion(bf16[128,4,256]{2,1,0:T(4,128)(2,1)} %bitcast.41), kind=kLoop, calls=%fused_computation.3 | loop fusion | flops 1048576 | bytes 786432 | tf_op jit(solution)/shard_map/reshape | solution.py:374
  18.4 3.7 %fusion.27.d_act_ref = f32[256,2048]{1,0:T(8,128)} fusion(bf16[256,512]{1,0:T(8,128)(2,1)S(1)} %copy-done.5, bf16[2048,512]{1,0:T(8,128)(2,1)} %w_two_ref.1), kind=kOutput, calls=%fused_computation.53 | convolution fusion | flops 536870912 | bytes 4456448 | tf_op jit(solution)/shard_map/dot_general | solution.py:32
  22.2 1.4 copy.22
  23.6 2.8 %all-to-all-done = bf16[128,8,128]{2,1,0:T(8,128)(2,1)S(1)} async-done(((bf16[128,8,128]{2,1,0:T(8,128)(2,1)}), bf16[128,8,128]{2,1,0:T(8,128)(2,1)S(1)}, u32[]{:S(2)}, u32[]{:S(2)}) %all-to-all-start) | async-done | bytes 262176 | tf_op jit(solution)/shard_map/all_to_all | solution.py:380
  28.1 1.3 shard_map.146
  30.3 3.4 %collective-permute-start.1 = (bf16[48,256]{1,0:T(8,128)(2,1)}, bf16[48,256]{1,0:T(8,128)(2,1)S(1)}, u32[]{:S(2)}, u32[]{:S(2)}) collective-permute-start(bf16[48,256]{1,0:T(8,128)(2,1)} %get-tuple-element.27), channel_id=1, source_target_pairs={{0,112},{16,0},{32,16},{48,32},{64,48},{80,64},{96,80},{112,96},{1... | collective-permute-start | bytes 73736 | tf_op jit(solution)/shard_map/ppermute | solution.py:353
  33.6 2.2 %collective-permute-start.2 = (bf16[48,256]{1,0:T(8,128)(2,1)}, bf16[48,256]{1,0:T(8,128)(2,1)S(1)}, u32[]{:S(2)}, u32[]{:S(2)}) collective-permute-start(bf16[48,256]{1,0:T(8,128)(2,1)} %get-tuple-element.28), channel_id=1, source_target_pairs={{0,1},{1,2},{2,3},{3,4},{4,5},{5,6},{6,7},{7,8},{8,9},{9,10},{10,1... | collective-permute-start | bytes 73736 | tf_op jit(solution)/shard_map/ppermute | solution.py:353
  36.0 1.5 reshape.198
  37.5 3.4 %collective-permute-done.3.s3 = bf16[48,256]{1,0:T(8,128)(2,1)S(1)} collective-permute-done((bf16[48,256]{1,0:T(8,128)(2,1)S(1)}, bf16[48,256]{1,0:T(8,128)(2,1)S(1)}, u32[]{:S(2)}, u32[]{:S(2)}) %collective-permute-start.3) | collective-permute-done | bytes 24608 | tf_op jit(solution)/shard_map/ppermute | solution.py:353
  41.8 1.6 %copy-done.1 = f32[256,2048]{1,0:T(8,128)S(1)} copy-done((f32[256,2048]{1,0:T(8,128)S(1)}, f32[256,2048]{1,0:T(8,128)}, u32[]{:S(2)}) %copy-start.1) | copy-done | bytes 2097176
  43.4 5.6 %shard_map.147 = (f32[2688,128]{1,0:T(8,128)S(1)}, f32[256,512]{1,0:T(8,128)S(1)}, f32[256,128]{1,0:T(8,128)S(1)}, bf16[256,512]{1,0:T(8,128)(2,1)S(1)}, bf16[25...) custom-call(s32[1]{0:T(128)} %bitcast.9.core_ref, ...), custom_call_target="tpu_custom_call" | custom-call | tf_op jit(solution)/shard_map/pallas_call | solution.py:37
  49.9 5.6 %shard_map.149 = (f32[64,16,128]{2,1,0:T(8,128)S(1)}, bf16[64,16,128]{2,1,0:T(8,128)(2,1)S(1)}) custom-call(s32[1]{0:T(128)} %bitcast.9.core_ref, bf16[256,256]{1,0:T(8,128)(2,1)S(1)} %copy-done.12, bf16[48,256]{1,0:T(8,128)(2,1)S(1)} %collective-permute-done.s0, bf16[48,256]{1,0:T(8,128)(2,1)S(1)} %collective-permute-done.1.s1, ...), custom_call_target="tpu_custom_call" | custom-call | tf_op jit(solution)/shard_map/pallas_call | solution.py:37
  55.6 1.5 collective-permute-done.5.small_ref
  57.9 39.0 %all_to_all.15.in_ref = bf16[64,9,16,128]{3,2,1,0:T(8,128)(2,1)S(1)} all-to-all(bf16[64,9,16,128]{3,2,1,0:T(8,128)(2,1)S(1)} %shard_map.150), channel_id=1, replica_groups=mesh['face'=8,'col'=8,'core'=2] {'face','col'}, dimensions={0} | all-to-all | bytes 4718592 | tf_op jit(solution)/shard_map/all_to_all | solution.py:439
  96.9 1.0 shard_map.151
  98.0 35.8 %all_to_all.16.in_ref = bf16[64,9,16,128]{3,2,1,0:T(8,128)(2,1)S(1)} all-to-all(bf16[64,9,16,128]{3,2,1,0:T(8,128)(2,1)S(1)} %shard_map.151), channel_id=1, replica_groups=mesh['face'=8,'col'=8,'core'=2] {'face','col'}, dimensions={0} | all-to-all | bytes 4718592 | tf_op jit(solution)/shard_map/all_to_all | solution.py:441
  133.8 3.2 %collective-permute-start.6 = (bf16[64,9,16,128]{3,2,1,0:T(8,128)(2,1)S(1)}, bf16[64,9,16,128]{3,2,1,0:T(8,128)(2,1)}, u32[]{:S(2)}, u32[]{:S(2)}) collective-permute-start(bf16[64,9,16,128]{3,2,1,0:T(8,128)(2,1)S(1)} %all_to_all.16.in_ref), channel_id=1, source_target_pairs={{0,1},{1,0},{2,3},{3,2},{4,5},{5,4},{6,7},{7,6},{8,9},{9,8},{10,11... | collective-permute-start | bytes 7077896 | tf_op jit(solution)/shard_map/ppermute | solution.py:358
  137.0 1.6 %copy-done.2 = bf16[2048,512]{1,0:T(8,128)(2,1)S(1)} copy-done((bf16[2048,512]{1,0:T(8,128)(2,1)S(1)}, bf16[2048,512]{1,0:T(8,128)(2,1)}, u32[]{:S(2)}) %copy-start.2) | copy-done | bytes 2097176
  139.5 1.4 shard_map.148
  140.9 2.4 %shard_map.152 = (f32[512,2048]{1,0:T(8,128)}, f32[2048,512]{1,0:T(8,128)}) custom-call(s32[1]{0:T(128)} %bitcast.9.core_ref, bf16[64,9,16,128]{3,2,1,0:T(8,128)(2,1)S(1)} %all_to_all.16.in_ref), custom_call_target="tpu_custom_call" | custom-call | tf_op jit(solution)/shard_map/pallas_call | solution.py:298
  143.3 1.0 broadcast_select_fusion
  146.7 4.2 %shard_map.153 = (f32[512,2048]{1,0:T(8,128)}, f32[2048,512]{1,0:T(8,128)}) custom-call(s32[1]{0:T(128)S(6)} %sub.123.core_ref, bf16[64,9,16,128]{3,2,1,0:T(8,128)(2,1)} %collective-permute-done.6.in_ref, f32[512,2048]{1,0:T(8,128)} %get-tuple-element.40.refs_0_, f32[2048,512]{1,0:T(8,128)} %get-tuple-element.41.refs_1_), custom_call_target="tpu_custom_call", output_to_operand_aliasing={{0}: (2, {}), {1}: (3, {})} | custom-call | tf_op jit(solution)/shard_map/pallas_call | solution.py:298
  (54 shorter events, 11.4 us)
Async XLA Ops:
  0.6 17.8 %copy-start.5 = (bf16[256,512]{1,0:T(8,128)(2,1)S(1)}, bf16[256,512]{1,0:T(8,128)(2,1)}, u32[]{:S(2)}) copy-start(bf16[256,512]{1,0:T(8,128)(2,1)} %cot_ref.5) | copy-start | bytes 786436
  1.5 0.9 copy-start.13
  2.4 0.7 copy-start.14
  4.2 22.3 %all-to-all-start = ((bf16[128,8,128]{2,1,0:T(8,128)(2,1)}), bf16[128,8,128]{2,1,0:T(8,128)(2,1)S(1)}, u32[]{:S(2)}, u32[]{:S(2)}) async-start(bf16[128,8,128]{2,1,0:T(8,128)(2,1)} %bitcast.1), calls=%async_computation | async-start | bytes 524288 | tf_op jit(solution)/shard_map/all_to_all | solution.py:380
  18.4 8.7 %copy-start.8 = (bf16[256,512]{1,0:T(8,128)(2,1)S(1)}, bf16[256,512]{1,0:T(8,128)(2,1)}, u32[]{:S(2)}) copy-start(bf16[256,512]{1,0:T(8,128)(2,1)} %w_embed_ref.3) | copy-start | bytes 786436
  18.4 17.5 %copy-start.15 = (bf16[512]{0:T(512)(128)(2,1)S(1)}, bf16[512]{0:T(512)(128)(2,1)}, u32[]{:S(2)}) copy-start(bf16[512]{0:T(512)(128)(2,1)} %param.16) | copy-start | bytes 3076
  22.1 19.6 %copy-start = (bf16[512,2048]{1,0:T(8,128)(2,1)S(1)}, bf16[512,2048]{1,0:T(8,128)(2,1)}, u32[]{:S(2)}) copy-start(bf16[512,2048]{1,0:T(8,128)(2,1)} %w_one_ref.3) | copy-start | bytes 6291460
  26.5 0.7 copy-start.9
  27.2 1.0 copy-start.10
  29.4 0.7 copy-start.11
  30.1 18.9 %copy-start.6 = (bf16[256,512]{1,0:T(8,128)(2,1)}, bf16[256,512]{1,0:T(8,128)(2,1)S(1)}, u32[]{:S(2)}) copy-start(bf16[256,512]{1,0:T(8,128)(2,1)S(1)} %get-tuple-element.25.emb_ref) | copy-start | bytes 786436
  30.1 7.4 %collective-permute-start = (bf16[48,256]{1,0:T(8,128)(2,1)}, bf16[48,256]{1,0:T(8,128)(2,1)S(1)}, u32[]{:S(2)}, u32[]{:S(2)}) collective-permute-start(bf16[48,256]{1,0:T(8,128)(2,1)} %get-tuple-element.26), channel_id=1, source_target_pairs={{0,16},{16,32},{32,48},{48,64},{64,80},{80,96},{96,112},{112,0},{1... | collective-permute-start | bytes 73736 | tf_op jit(solution)/shard_map/ppermute | solution.py:353
  30.3 7.2 %collective-permute-start.1 = (bf16[48,256]{1,0:T(8,128)(2,1)}, bf16[48,256]{1,0:T(8,128)(2,1)S(1)}, u32[]{:S(2)}, u32[]{:S(2)}) collective-permute-start(bf16[48,256]{1,0:T(8,128)(2,1)} %get-tuple-element.27), channel_id=1, source_target_pairs={{0,112},{16,0},{32,16},{48,32},{64,48},{80,64},{96,80},{112,96},{1... | collective-permute-start | bytes 73736 | tf_op jit(solution)/shard_map/ppermute | solution.py:353
  33.6 3.8 %collective-permute-start.2 = (bf16[48,256]{1,0:T(8,128)(2,1)}, bf16[48,256]{1,0:T(8,128)(2,1)S(1)}, u32[]{:S(2)}, u32[]{:S(2)}) collective-permute-start(bf16[48,256]{1,0:T(8,128)(2,1)} %get-tuple-element.28), channel_id=1, source_target_pairs={{0,1},{1,2},{2,3},{3,4},{4,5},{5,6},{6,7},{7,8},{8,9},{9,10},{10,1... | collective-permute-start | bytes 73736 | tf_op jit(solution)/shard_map/ppermute | solution.py:353
  35.8 5.1 %collective-permute-start.3 = (bf16[48,256]{1,0:T(8,128)(2,1)S(1)}, bf16[48,256]{1,0:T(8,128)(2,1)S(1)}, u32[]{:S(2)}, u32[]{:S(2)}) collective-permute-start(bf16[48,256]{1,0:T(8,128)(2,1)S(1)} %get-tuple-element.29), channel_id=1, source_target_pairs={{0,15},{1,0},{2,1},{3,2},{4,3},{5,4},{6,5},{7,6},{8,7},{9,8},{10,9... | collective-permute-start | bytes 73736 | tf_op jit(solution)/shard_map/ppermute | solution.py:353
  41.8 1.6 %copy-start.1 = (f32[256,2048]{1,0:T(8,128)S(1)}, f32[256,2048]{1,0:T(8,128)}, u32[]{:S(2)}) copy-start(f32[256,2048]{1,0:T(8,128)} %fusion.27.d_act_ref) | copy-start | bytes 6291460
  43.4 6.5 %copy-start.12 = (bf16[256,256]{1,0:T(8,128)(2,1)S(1)}, bf16[256,256]{1,0:T(8,128)(2,1)}, u32[]{:S(2)}) copy-start(bf16[256,256]{1,0:T(8,128)(2,1)} %copy-done.11) | copy-start | bytes 393220
  49.0 8.1 %copy-start.3 = (bf16[256,2048]{1,0:T(8,128)(2,1)}, bf16[256,2048]{1,0:T(8,128)(2,1)S(1)}, u32[]{:S(2)}) copy-start(bf16[256,2048]{1,0:T(8,128)(2,1)S(1)} %get-tuple-element.30.active_ref) | copy-start | bytes 3145732
  49.0 8.1 %collective-permute-start.4 = (bf16[512,16,128]{2,1,0:T(8,128)(2,1)S(1)}, bf16[512,16,128]{2,1,0:T(8,128)(2,1)S(1)}, u32[]{:S(2)}, u32[]{:S(2)}) collective-permute-start(bf16[512,16,128]{2,1,0:T(8,128)(2,1)S(1)} %get-tuple-element.33), channel_id=1, source_target_pairs={{0,1},{1,0},{2,3},{3,2},{4,5},{5,4},{6,7},{7,6},{8,9},{9,8},{10,11... | collective-permute-start | bytes 6291464 | tf_op jit(solution)/shard_map/ppermute | solution.py:358
  55.5 1.6 %collective-permute-start.5 = (bf16[64,16,128]{2,1,0:T(8,128)(2,1)S(1)}, bf16[64,16,128]{2,1,0:T(8,128)(2,1)S(1)}, u32[]{:S(2)}, u32[]{:S(2)}) collective-permute-start(bf16[64,16,128]{2,1,0:T(8,128)(2,1)S(1)} %get-tuple-element.39), channel_id=1, source_target_pairs={{0,1},{1,0},{2,3},{3,2},{4,5},{5,4},{6,7},{7,6},{8,9},{9,8},{10,11... | collective-permute-start | bytes 786440 | tf_op jit(solution)/shard_map/ppermute | solution.py:358
  98.0 39.0 %copy-start.4 = (bf16[256,2048]{1,0:T(8,128)(2,1)S(1)}, bf16[256,2048]{1,0:T(8,128)(2,1)}, u32[]{:S(2)}) copy-start(bf16[256,2048]{1,0:T(8,128)(2,1)} %copy-done.3) | copy-start | bytes 3145732
  133.8 9.5 %collective-permute-start.6 = (bf16[64,9,16,128]{3,2,1,0:T(8,128)(2,1)S(1)}, bf16[64,9,16,128]{3,2,1,0:T(8,128)(2,1)}, u32[]{:S(2)}, u32[]{:S(2)}) collective-permute-start(bf16[64,9,16,128]{3,2,1,0:T(8,128)(2,1)S(1)} %all_to_all.16.in_ref), channel_id=1, source_target_pairs={{0,1},{1,0},{2,3},{3,2},{4,5},{5,4},{6,7},{7,6},{8,9},{9,8},{10,11... | collective-permute-start | bytes 7077896 | tf_op jit(solution)/shard_map/ppermute | solution.py:358
  137.0 1.6 %copy-start.2 = (bf16[2048,512]{1,0:T(8,128)(2,1)S(1)}, bf16[2048,512]{1,0:T(8,128)(2,1)}, u32[]{:S(2)}) copy-start(bf16[2048,512]{1,0:T(8,128)(2,1)} %w_two_ref.1) | copy-start | bytes 6291460
  138.6 0.9 copy-start.7

commit v3 on v2

--- a/solution.py
+++ b/solution.py
@@ -32,18 +32,30 @@
     return lax.dot_general(a, b, dims, preferred_element_type=F32)
 
 
-def call(kernel, outs, scratch, limit, *args):
+def call(kernel, outs, scratch, limit, *args, far=(), far_outs=(), copies=0, aliases=None):
     vmem, scalar = pl.BlockSpec(memory_space=pltpu.VMEM), pl.BlockSpec(memory_space=pltpu.SMEM)
+    away = pl.BlockSpec(memory_space=pl.ANY)
     return pl.pallas_call(
         kernel,
         out_shape=[jax.ShapeDtypeStruct(s, d) for s, d in outs],
-        in_specs=[scalar if a.shape == (1,) else vmem for a in args],
-        out_specs=[vmem] * len(outs),
-        scratch_shapes=[pltpu.VMEM(s, d) for s, d in scratch],
+        in_specs=[
+            scalar if a.shape == (1,) else away if k in far else vmem for k, a in enumerate(args)
+        ],
+        out_specs=[away if k in far_outs else vmem for k in range(len(outs))],
+        scratch_shapes=[pltpu.VMEM(s, d) for s, d in scratch]
+        + [pltpu.SemaphoreType.DMA((copies,))] * bool(copies),
+        input_output_aliases=aliases or {},
         compiler_params=pltpu.CompilerParams(vmem_limit_bytes=limit * 2**20),
     )(*args)
 
 
+def start(sem, *pairs):
+    moves = [pltpu.make_async_copy(a, b, sem.at[k]) for k, (a, b) in enumerate(pairs)]
+    for move in moves:
+        move.start()
+    return moves
+
+
 def block(i, j, pitch):
     return pl.ds(pl.multiple_of((i * pitch + j) * 8, 8), 8)
 
@@ -52,35 +64,57 @@
     return pl.ds((i * pitch + j) * 8 + h * 4 + cb, 8, stride=8)
 
 
-def route_kernel(col_ref, row_ref, obs_ref, out_ref):
+def route_kernel(row_far, obs_far, out_ref, row_ref, obs_ref, sem):
+    fetch_row, fetch_obs = start(sem, (row_far, row_ref), (obs_far, obs_ref))
+    fetch_row.wait()
     row = row_ref[...]
     count = row.shape[1]
+    across = jnp.broadcast_to(row, (count, count)).astype(F32)
     earlier = lax.broadcasted_iota(jnp.int32, (count, count), 0) < lax.broadcasted_iota(
         jnp.int32, (count, count), 1
     )
-    same = jnp.where((col_ref[...] == row) & earlier, 1.0, 0.0)
+    same = jnp.where((across.T == across) & earlier, 1.0, 0.0)
     rank = jnp.sum(same, axis=0, keepdims=True).astype(jnp.int32)
     place = row * 8 + rank
     lines = out_ref.shape[0]
     line = lax.broadcasted_iota(jnp.int32, (lines, count), 0)
     chosen = jnp.where((line - (line & 4)) == place, 1.0, 0.0).astype(BF16)
+    fetch_obs.wait()
     moved = dot(chosen, obs_ref[...])
     first = (lax.broadcasted_iota(jnp.int32, (lines, LANE), 0) & 4) == 0
     out_ref[...] = jnp.where(first, moved[:, :LANE], moved[:, LANE:]).astype(BF16)
 
 
-def embed_kernel(got_ref, weights_ref, w_embed_ref, pick_ref, grid_ref, emb_ref, *strip_refs):
-    got = got_ref[...].astype(F32)
-    first = (lax.broadcasted_iota(jnp.int32, got.shape, 0) & 4) == 0
-    spread = jnp.concatenate(
-        [jnp.where(first, got, 0.0), jnp.where(first, 0.0, got)], axis=1
-    ).astype(BF16)
-    gridded = dot(weights_ref[...], spread).astype(BF16)
+def prepare_kernel(interp_ref, cot_ref, w_two_ref, weights_ref, d_act_ref):
+    weights = interp_ref[...].astype(F32)
+    tiles, slots = weights.shape[:2]
+    for k in range(slots):
+        weights_ref[:, k * tiles : (k + 1) * tiles] = weights[:, k, :].T.astype(BF16)
+    for k in range(w_two_ref.shape[0] // STEP):
+        some = pl.ds(k * STEP, STEP)
+        d_act_ref[:, some] = dot(cot_ref[...], w_two_ref[some, :], NT)
+
+
+def embed_kernel(
+    got_ref, weights_ref, w_embed_ref, pick_ref, grid_ref, emb_ref, s0, s1, s2, s3, wide_ref, rows_ref
+):
+    wide_ref[...] = got_ref[...].astype(F32)
+    tiles = got_ref.shape[0] // 8
+    for k in range(4):
+        for half in range(2):
+            for g in range(0, tiles, 16):
+                two = [
+                    wide_ref[pl.ds((g + e) * 8 + half * 4 + k, 8, stride=8), :] for e in (0, 8)
+                ]
+                rows_ref[pl.ds(k * tiles + g, 16), pl.ds(half * LANE, LANE)] = jnp.concatenate(
+                    two, axis=0
+                ).astype(BF16)
+    gridded = dot(weights_ref[...], rows_ref[...]).astype(BF16)
     grid_ref[...] = gridded
+    strips = dot(pick_ref[...], gridded).astype(BF16)
+    for k, ref in enumerate((s0, s1, s2, s3)):
+        ref[...] = strips[k * STRIP : (k + 1) * STRIP]
     emb_ref[...] = dot(gridded, w_embed_ref[...]).astype(BF16)
-    strips = dot(pick_ref[...], gridded).astype(BF16)
-    for k, ref in enumerate(strip_refs):
-        ref[...] = strips[k * STRIP : (k + 1) * STRIP]
 
 
 def tiles_of(part, two, one):
@@ -93,10 +127,19 @@
 
 
 def forward_kernel(
-    core_ref, emb_ref, s0, s1, s2, s3, place_ref, kern_ref, gain_ref, w_embed_ref, w_one_ref, d_act_ref, cot_ref,
-    field_ref, normal_ref, inv_ref, scaled_ref, active_ref, d_hid_ref, theirs_ref,
-    strips_ref, cells_ref, flat_ref, conv_ref, two_ref, one_ref,
+    core_ref, emb_ref, s0, s1, s2, s3, place_ref, dw_ref, gain_ref, w_embed_ref, w_one_ref, d_act_far, cot_ref,
+    field_ref, normal_ref, inv_ref, scaled_ref, active_ref, d_hid_ref, kern_ref, theirs_ref,
+    strips_ref, cells_ref, flat_ref, conv_ref, two_ref, one_ref, d_act_ref, sem,
 ):
+    (fetch,) = start(sem, (d_act_far, d_act_ref))
+    taps = dw_ref[...].astype(F32)
+    last = taps.shape[0] - 1
+    for h in range(2):
+        for cb in range(4):
+            lanes = slice(cb * LANE, (cb + 1) * LANE)
+            for g in range(0, last, 8):
+                kern_ref[pl.ds(g * 8 + h * 4 + cb, 8, stride=8), :] = taps[g : g + 8, lanes]
+            kern_ref[pl.ds(last * 8 + h * 4 + cb, 1), :] = taps[last:, lanes]
     for k, ref in enumerate((s0, s1, s2, s3)):
         strips_ref[k * STRIP : (k + 1) * STRIP] = ref[...]
     cells_ref[0:CELLS] = emb_ref[...]
@@ -139,8 +182,9 @@
         rows = pl.ds(r * SIDE, SIDE)
         normal_ref[rows, :] = normal
         inv_ref[rows, :] = jnp.broadcast_to(inverse, (SIDE, LANE))
-        scaled_ref[rows, :] = (normal * gain_ref[...]).astype(BF16)
-
+        scaled_ref[rows, :] = (normal * gain_ref[...].astype(F32)).astype(BF16)
+
+    fetch.wait()
     for k in range(w_one_ref.shape[1] // STEP):
         some = pl.ds(k * STEP, STEP)
         pre = dot(scaled_ref[...], w_one_ref[:, some])
@@ -173,7 +217,7 @@
         rows = pl.ds(r * SIDE, SIDE)
         normal, d_scaled = normal_ref[rows, :], d_scaled_ref[rows, :]
         total = total + d_scaled * normal
-        d_normal = d_scaled * gain_ref[...]
+        d_normal = d_scaled * gain_ref[...].astype(F32)
         mean = jnp.mean(d_normal, axis=1, keepdims=True)
         along = jnp.mean(d_normal * normal, axis=1, keepdims=True)
         d_conv = (d_normal - mean - normal * along) * inv_ref[rows, 0:1]
@@ -252,8 +296,11 @@
 
 
 def pair_kernel(
-    core_ref, scaled_ref, active_ref, d_hid_ref, cot_ref, big_ref, mine_ref, small_ref, out_ref, two_ref, one_ref
+    core_ref, scaled_ref, active_ref, d_hid_ref, cot_ref, big_ref, emb_ref, w_two_far,
+    out_ref, feature_far,
+    two_ref, one_ref, w_two_ref, feature_ref, sem,
 ):
+    (fetch,) = start(sem, (w_two_far, w_two_ref))
     steps = big_ref.shape[0] // 128
     for k in range(steps):
         some = pl.ds(pl.multiple_of((core_ref[0] * steps + k) * STEP, STEP), STEP)
@@ -261,12 +308,18 @@
         one_ref[...] = dot(scaled_ref[...], d_hid_ref[:, some], TN)
         for t, ref, rows, lanes in tiles_of(k, two_ref, one_ref):
             out_ref[t // 8, t % 8] = (ref[rows, lanes] + big_ref[t].astype(F32)).astype(BF16)
-    for t in range(out_ref.shape[0]):
-        out_ref[t, 8] = (mine_ref[t] + small_ref[t].astype(F32)).astype(BF16)
-
-
-def feature_kernel(emb_ref, active_ref, w_two_ref, out_ref):
-    out_ref[...] = (emb_ref[...].astype(F32) + dot(active_ref[...], w_two_ref[...])).astype(BF16)
+    fetch.wait()
+    feature_ref[...] = (emb_ref[...].astype(F32) + dot(active_ref[...], w_two_ref[...])).astype(BF16)
+    put = pltpu.make_async_copy(feature_ref, feature_far, sem.at[1])
+    put.start()
+    put.wait()
+
+
+def join_kernel(mine_ref, small_ref, paired_far, out_far, tile_ref, sem):
+    tile_ref[...] = (mine_ref[...] + small_ref[...].astype(F32)).astype(BF16)
+    put = pltpu.make_async_copy(tile_ref, out_far.at[:, 8], sem.at[0])
+    put.start()
+    put.wait()
 
 
 def sum_kernel(in_ref, out_ref):
@@ -286,30 +339,63 @@
     lax.fori_loop(0, parts, spread, 0)
 
 
-def assemble_kernel(core_ref, in_ref, *refs):
-    one_ref, two_ref = refs[-2:]
-    for t, ref, rows, lanes in tiles_of(0, two_ref, one_ref):
-        ref[rows, lanes] = in_ref[t // 8, t % 8].astype(F32)
-
-
-def assemble(core, gathered, shapes, before):
-    steps = shapes[0][1] // STEP // 2
-    whole = [pl.BlockSpec(memory_space=pl.ANY)] * len(before)
-    return pl.pallas_call(
-        assemble_kernel,
-        out_shape=[jax.ShapeDtypeStruct(s, F32) for s in shapes],
-        grid_spec=pltpu.PrefetchScalarGridSpec(
-            num_scalar_prefetch=1,
-            grid=(steps,),
-            in_specs=[pl.BlockSpec((16,) + gathered.shape[1:], lambda k, core: (k, 0, 0, 0))] + whole,
-            out_specs=[
-                pl.BlockSpec((shapes[0][0], STEP), lambda k, core: (0, core[0] * steps + k)),
-                pl.BlockSpec((STEP, shapes[1][1]), lambda k, core: (core[0] * steps + k, 0)),
-            ],
-        ),
-        input_output_aliases={2 + k: k for k in range(len(before))},
-        compiler_params=pltpu.CompilerParams(vmem_limit_bytes=24 * 2**20),
-    )(core, gathered, *before)
+def assemble_half(core, in_ref, one_far, two_far, one_ref, two_ref, sem):
+    steps = one_ref.shape[0]
+    puts = []
+    for k in range(steps):
+        for t, ref, rows, lanes in tiles_of(k, two_ref, one_ref):
+            ref[k, rows, lanes] = in_ref[t // 8, t % 8].astype(F32)
+        some = pl.ds(pl.multiple_of((core * steps + k) * STEP, STEP), STEP)
+        puts += [
+            pltpu.make_async_copy(one_ref.at[k], one_far.at[:, some], sem.at[2 * k]),
+            pltpu.make_async_copy(two_ref.at[k], two_far.at[some, :], sem.at[2 * k + 1]),
+        ]
+        puts[-2].start()
+        puts[-1].start()
+    return puts
+
+
+def first_kernel(core_ref, in_ref, one_far, two_far, one_ref, two_ref, sem):
+    for put in assemble_half(core_ref[0], in_ref, one_far, two_far, one_ref, two_ref, sem):
+        put.wait()
+
+
+def second_kernel(
+    core_ref, in_ref, mine_ref, one_old, two_old,
+    one_far, two_far, embed_far, taps_far, gain_far,
+    one_ref, two_ref, rows_ref, embed_ref, taps_ref, gain_ref, sem,
+):
+    core = core_ref[0]
+    puts = assemble_half(1 - core, in_ref, one_far, two_far, one_ref, two_ref, sem)
+    count = taps_ref.shape[0]
+
+    def place(first, last):
+        for t in range(in_ref.shape[0]):
+            r, c = divmod(t, 4)
+            embed_ref[r * 16 : (r + 1) * 16, c * LANE : (c + 1) * LANE] = first[t, 8].astype(F32)
+        for t in range(rows_ref.shape[0] // 16):
+            rows_ref[t * 16 : (t + 1) * 16, :] = last[t, 8].astype(F32)
+
+    @pl.when(core == 0)
+    def _():
+        place(mine_ref, in_ref)
+
+    @pl.when(core == 1)
+    def _():
+        place(in_ref, mine_ref)
+
+    for cb in range(4):
+        lanes = pl.ds(cb * LANE, LANE)
+        for g in range(0, count - 1, 8):
+            taps_ref[pl.ds(g, 8), lanes] = rows_ref[pl.ds(g * 4 + cb, 8, stride=4), :]
+        taps_ref[pl.ds(count - 1, 1), lanes] = rows_ref[pl.ds((count - 1) * 4 + cb, 1), :]
+        gain_ref[:, lanes] = rows_ref[pl.ds(count * 4 + cb, 1), :]
+    base = len(puts)
+    for k, pair in enumerate(((embed_ref, embed_far), (taps_ref, taps_far), (gain_ref, gain_far))):
+        puts.append(pltpu.make_async_copy(*pair, sem.at[base + k]))
+        puts[-1].start()
+    for put in puts:
+        put.wait()
 
 
 def turned(spin, x, y, last):
@@ -367,30 +453,33 @@
     slots = interp.shape[2]
     core = lax.axis_index("core").reshape(1)
     place, pick = selectors(tile_spin[0, 0])
-    taps = jnp.broadcast_to(
-        dw_kernel.astype(F32).reshape(TAPS * TAPS, 1, 4, LANE), (TAPS * TAPS, 2, 4, LANE)
-    ).reshape(TAPS * TAPS * 8, LANE)
-    gain = norm_gain.astype(F32)[None]
-    weights = jnp.concatenate([interp[0], interp[0]], axis=1).reshape(tiles * 2 * slots, CELLS).T
+    gain = norm_gain[None]
 
     (leaving,) = call(
-        route_kernel, [((tiles * 8, LANE), BF16)], [], 16,
-        obs_tile, obs_tile.reshape(1, -1), obs_values,
+        route_kernel,
+        [((tiles * 8, LANE), BF16)],
+        [((1, obs_values.shape[0]), jnp.int32), (obs_values.shape, BF16)],
+        16, obs_tile.reshape(1, -1), obs_values, far=(0, 1), copies=2,
     )
     arrived = lax.all_to_all(leaving.reshape(tiles, 8, LANE), ALL, 0, 0, tiled=True)
-    d_active = dot(cotangent, w_two, NT)
+    weights, d_active = call(
+        prepare_kernel, [((CELLS, tiles * slots), BF16), ((CELLS, hidden), F32)], [], 16,
+        interp[0], cotangent, w_two,
+    )
 
     gridded, embedded, *strips = call(
         embed_kernel,
-        [((CELLS, width), BF16), ((CELLS, channels), BF16)] + [((STRIP, width), BF16)] * 4, [], 16,
-        arrived.reshape(tiles * 8, LANE), weights, w_embed, pick,
+        [((CELLS, width), BF16), ((CELLS, channels), BF16)] + [((STRIP, width), BF16)] * 4,
+        [((tiles * 8, LANE), F32), ((tiles * slots, width), BF16)],
+        12, arrived.reshape(tiles * 8, LANE), weights, w_embed, pick,
     )
     strips = exchange(strips)
     cells2 = ROWS2 * PITCH * 8
     flat = ((FULL * PITCH, channels), F32)
+    kernel = ((TAPS * TAPS * 8, LANE), F32)
     step_sums = [((STEP, channels), F32), ((channels, STEP), F32)]
     half = hidden * channels // (16 * LANE)
-    field, normal, inverse, scaled, active, d_hidden, theirs = call(
+    field, normal, inverse, scaled, active, d_hidden, taps, theirs = call(
         forward_kernel,
         [
             ((cells2, LANE), F32),
@@ -399,6 +488,7 @@
             ((CELLS, channels), BF16),
             ((CELLS, hidden), BF16),
             ((CELLS, hidden), BF16),
+            kernel,
             ((half, 16, LANE), BF16),
         ],
         [
@@ -407,9 +497,11 @@
             flat,
             ((CELLS * 4, LANE), F32),
         ]
-        + step_sums,
-        40,
-        core, embedded, *strips, place, taps, gain, w_embed, w_one, d_active, cotangent,
+        + step_sums
+        + [((CELLS, hidden), F32)],
+        20,
+        core, embedded, *strips, place, dw_kernel, gain, w_embed, w_one, d_active, cotangent,
+        far=(11,), copies=1,
     )
     big = swap(theirs)
 
@@ -421,35 +513,44 @@
             ((CELLS * 4, LANE), F32),
             ((cells2, LANE), F32),
             flat,
-            ((TAPS * TAPS * 8, LANE), F32),
+            kernel,
             ((CELLS + 4 * STRIP, width), BF16),
             ((2 * chips * 16, LANE), F32),
         ],
-        40,
+        20,
         core, gridded, *strips, place, field, normal, inverse, d_hidden, w_one, gain, taps, cotangent,
     )
     small = swap(theirs)
+    whole = ((chips, 9, 16, LANE), BF16)
+    paired, output = call(
+        pair_kernel, [whole, ((CELLS, channels), BF16)],
+        step_sums + [((hidden, channels), BF16), ((CELLS, channels), BF16)], 20,
+        core, scaled, active, d_hidden, cotangent, big, embedded, w_two, far=(7,), far_outs=(1,), copies=2,
+    )
     (paired,) = call(
-        pair_kernel, [((chips, 9, 16, LANE), BF16)], step_sums, 40,
-        core, scaled, active, d_hidden, cotangent, big, mine, small,
-    )
-    (output,) = call(
-        feature_kernel, [((CELLS, channels), BF16)], [], 16, embedded, active, w_two
+        join_kernel, [whole], [((chips, 16, LANE), BF16)], 4,
+        mine, small, paired, far=(2,), far_outs=(0,), copies=1, aliases={2: 0},
     )
     paired = lax.all_to_all(paired, CHIPS, 0, 0, tiled=True)
-    (summed,) = call(sum_kernel, [((chips, 9, 16, LANE), BF16)], [], 16, paired)
+    (summed,) = call(sum_kernel, [whole], [], 4, paired)
     here = lax.all_to_all(summed, CHIPS, 0, 0, tiled=True)
     there = swap(here)
-    shapes = [(channels, hidden), (hidden, channels)]
-    grads = assemble(core, here, shapes, [])
-    grad_one, grad_two = assemble(1 - core, there, shapes, grads)
-
-    first = jnp.where(core[0] == 0, here[:, 8], there[:, 8]).astype(F32)
-    last = jnp.where(core[0] == 0, there[:, 8], here[:, 8]).astype(F32)
-    grad_embed = first.reshape(16, 4, 16, LANE).transpose(0, 2, 1, 3).reshape(width, channels)
+
+    large = [((channels, hidden), F32), ((hidden, channels), F32)]
+    steps = hidden // STEP // 2
+    buffers = [((steps, channels, STEP), F32), ((steps, STEP, channels), F32)]
+    grads = call(
+        first_kernel, large, buffers, 12, core, here, far_outs=(0, 1), copies=2 * steps
+    )
     count = TAPS * TAPS
-    rows = last.reshape(chips * 16, LANE)[: (count + 1) * 4].reshape(count + 1, channels)
-    return output, grad_embed, rows[:count], rows[count], grad_one, grad_two
+    minor = [((width, channels), F32), ((count, channels), F32), ((1, channels), F32)]
+    grad_one, grad_two, grad_embed, grad_kernel, grad_gain = call(
+        second_kernel, large + minor,
+        buffers + [((-(-(count + 1) * 4 // 16) * 16, LANE), F32)] + minor, 16,
+        core, there, here, *grads,
+        far=(3, 4), far_outs=range(5), copies=2 * steps + 3, aliases={3: 0, 4: 1},
+    )
+    return output, grad_embed, grad_kernel, grad_gain[0], grad_one, grad_two
 
 
 def solution(mesh):

time: 152 us -> 145 us (0.954)
  local copies, waits for them, and re-layouts: 15 us -> 11.2 us
  matrix products: 3.69 us -> 0 us
  other arithmetic: 3.4 us -> 1.49 us
    pallas_call x7 -> x10, Pallas kernels: 16.8 us -> 24.2 us  [call(): pl.pallas_call(kernel, out_shape=[jax.ShapeDtypeStruct(s, d) for s, d in...]
    pallas_call x2 -> x0, Pallas kernels: 6.56 us -> none  [assemble(): pl.pallas_call(assemble_kernel, out_shape=[jax.ShapeDtypeStruct(s, F32) f...]
    dot_general x1 -> x0, matrix products: 3.69 us -> none  [dot(): return lax.dot_general(a, b, dims, preferred_element_type=F32)]
    reshape x2 -> x0, other arithmetic: 2.12 us -> none  [the longest x1 2.08 us: on_device(): jnp.concatenate([interp[0], interp[0]], axis=1)]
    broadcast_in_dim x2 -> x1, local copies, waits for them, and re-layouts: 2.42 us -> 0.68 us  [on_device(): gain = norm_gain[None]]
    reshape x2 -> x0, local copies, waits for them, and re-layouts: 1.6 us -> none  [the longest x1 1.39 us: on_device(): jnp.concatenate([interp[0], interp[0]], axis=1)]
    unnamed x34 -> x28, local copies, waits for them, and re-layouts: 9.73 us -> 10.5 us
  transfers between devices with their start and end apart: 8 -> 8, of which waited for: 3 -> 3; matrix products, arithmetic and copies ran while one was open for 6% -> 2% of each run, Pallas kernels for 6% -> 8%
where the time goes in v3:
time: 145 us; the launch traced here: 144 us
  blocking collectives  75.8 us (52%)
  Pallas kernels  24.2 us (17%)
  starting transfers between devices  20.9 us (14%)
  local copies, waits for them, and re-layouts  11.2 us (8%)
  waiting for transfers between devices  9.01 us (6%)
  between operations  1.61 us (1%)
  other arithmetic  1.49 us (1%)
    all_to_all x1, blocking collectives, on_device(): paired = lax.all_to_all(paired, CHIPS, 0, 0, tiled=True)  39.8 us
    all_to_all x1, blocking collectives, on_device(): here = lax.all_to_all(summed, CHIPS, 0, 0, tiled=True)  36 us
    pallas_call x10, Pallas kernels, call(): pl.pallas_call(kernel, out_shape=[jax.ShapeDtypeStruct(s, d) for s, d in...  24.2 us
    all_to_all x1, starting transfers between devices, on_device(): lax.all_to_all(leaving.reshape(tiles, 8, LANE), ALL, 0, 0, tiled=True)  11.5 us
    unnamed x28, local copies, waits for them, and re-layouts  10.5 us
    ppermute x4, starting transfers between devices, exchange(): lax.ppermute(strip, axis, [(i, (i + way) % size) for i in range(size)])  5.73 us
    ppermute x4, waiting for transfers between devices, exchange(): lax.ppermute(strip, axis, [(i, (i + way) % size) for i in range(size)])  3.84 us
    ppermute x3, starting transfers between devices, swap(): return lax.ppermute(value, 'core', [(0, 1), (1, 0)])  3.65 us
  transfers between devices with their start and end apart: 8, of which 3 were waited for; matrix products, arithmetic and copies ran while one was open for 2% of the time, Pallas kernels for 8%

profile of v3, /device:TPU:1, one launch (start us, length us, event | category | flops | bytes accessed | tf_op | source)
XLA Modules:
  0.0 144.2 jit_solution(10086018370083870034)
XLA Ops:
  0.7 0.9 copy-done.11
  2.3 1.3 shard_map.145
  3.6 11.5 %all-to-all-start = ((bf16[128,8,128]{2,1,0:T(8,128)(2,1)}), bf16[128,8,128]{2,1,0:T(8,128)(2,1)S(1)}, u32[]{:S(2)}, u32[]{:S(2)}) async-start(bf16[128,8,128]{2,1,0:T(8,128)(2,1)} %bitcast.2), calls=%async_computation | async-start | bytes 524288 | tf_op jit(solution)/shard_map/all_to_all | solution.py:464
  16.4 1.6 %copy-done = bf16[2048,512]{1,0:T(8,128)(2,1)S(1)} copy-done((bf16[2048,512]{1,0:T(8,128)(2,1)S(1)}, bf16[2048,512]{1,0:T(8,128)(2,1)}, u32[]{:S(2)}) %copy-start) | copy-done | bytes 2097176
  18.0 0.9 copy-done.3
  18.9 0.9 copy-done.8
  20.7 1.3 copy-done.5
  22.8 3.1 %all-to-all-done = bf16[128,8,128]{2,1,0:T(8,128)(2,1)S(1)} async-done(((bf16[128,8,128]{2,1,0:T(8,128)(2,1)}), bf16[128,8,128]{2,1,0:T(8,128)(2,1)S(1)}, u32[]{:S(2)}, u32[]{:S(2)}) %all-to-all-start) | async-done | bytes 262176 | tf_op jit(solution)/shard_map/all_to_all | solution.py:464
  25.9 0.9 copy-done.10
  26.8 1.1 shard_map.147
  28.2 3.4 %collective-permute-start.1 = (bf16[48,256]{1,0:T(8,128)(2,1)}, bf16[48,256]{1,0:T(8,128)(2,1)}, u32[]{:S(2)}, u32[]{:S(2)}) collective-permute-start(bf16[48,256]{1,0:T(8,128)(2,1)} %get-tuple-element.36), channel_id=1, source_target_pairs={{0,112},{16,0},{32,16},{48,32},{64,48},{80,64},{96,80},{112,96},{1... | collective-permute-start | bytes 73736 | tf_op jit(solution)/shard_map/ppermute | solution.py:439
  31.6 2.2 %collective-permute-start.2 = (bf16[48,256]{1,0:T(8,128)(2,1)}, bf16[48,256]{1,0:T(8,128)(2,1)}, u32[]{:S(2)}, u32[]{:S(2)}) collective-permute-start(bf16[48,256]{1,0:T(8,128)(2,1)} %get-tuple-element.37), channel_id=1, source_target_pairs={{0,1},{1,2},{2,3},{3,4},{4,5},{5,6},{6,7},{7,8},{8,9},{9,10},{10,1... | collective-permute-start | bytes 73736 | tf_op jit(solution)/shard_map/ppermute | solution.py:439
  35.3 3.8 %collective-permute-done.3.s3 = bf16[48,256]{1,0:T(8,128)(2,1)} collective-permute-done((bf16[48,256]{1,0:T(8,128)(2,1)}, bf16[48,256]{1,0:T(8,128)(2,1)}, u32[]{:S(2)}, u32[]{:S(2)}) %collective-permute-start.3) | collective-permute-done | bytes 24608 | tf_op jit(solution)/shard_map/ppermute | solution.py:439
  39.1 1.6 %copy-done.6 = f32[256,2048]{1,0:T(8,128)S(1)} copy-done((f32[256,2048]{1,0:T(8,128)S(1)}, f32[256,2048]{1,0:T(8,128)}, u32[]{:S(2)}) %copy-start.6) | copy-done | bytes 2097176
  41.5 6.6 %shard_map.148 = (f32[2688,128]{1,0:T(8,128)S(1)}, f32[256,512]{1,0:T(8,128)S(1)}, f32[256,128]{1,0:T(8,128)S(1)}, bf16[256,512]{1,0:T(8,128)(2,1)S(1)}, bf16[25...) custom-call(s32[1]{0:T(128)} %bitcast.core_ref, ...), custom_call_target="tpu_custom_call" | custom-call | tf_op jit(solution)/shard_map/pallas_call | solution.py:38
  48.9 6.4 %shard_map.150 = (f32[64,16,128]{2,1,0:T(8,128)S(1)}, bf16[64,16,128]{2,1,0:T(8,128)(2,1)S(1)}) custom-call(s32[1]{0:T(128)} %bitcast.core_ref, bf16[256,256]{1,0:T(8,128)(2,1)S(1)} %get-tuple-element.45.grid_ref, bf16[48,256]{1,0:T(8,128)(2,1)} %collective-permute-done.s0, bf16[48,256]{1,0:T(8,128)(2,1)} %collective-permute-done.1.s1, ...), custom_call_target="tpu_custom_call" | custom-call | tf_op jit(solution)/shard_map/pallas_call | solution.py:38
  55.4 2.4 %shard_map.149 = (bf16[64,9,16,128]{3,2,1,0:T(8,128)(2,1)S(1)}, bf16[256,512]{1,0:T(8,128)(2,1)}) custom-call(s32[1]{0:T(128)} %bitcast.core_ref, bf16[256,512]{1,0:T(8,128)(2,1)S(1)} %get-tuple-element.40.scaled_ref, bf16[256,2048]{1,0:T(8,128)(2,1)S(1)} %get-tuple-element.41.active_ref, bf16[256,2048]{1,0:T(8,128)(2,1)S(1)} %get-tuple-element.42.d_hid_ref, ...), custom_call_target="tpu_custom_call" | custom-call | tf_op jit(solution)/shard_map/pallas_call | solution.py:38
  57.9 39.8 %all_to_all.15.in_ref = bf16[64,9,16,128]{3,2,1,0:T(8,128)(2,1)S(1)} all-to-all(bf16[64,9,16,128]{3,2,1,0:T(8,128)(2,1)S(1)} %shard_map.151), channel_id=1, replica_groups=mesh['face'=8,'col'=8,'core'=2] {'face','col'}, dimensions={0} | all-to-all | bytes 4718592 | tf_op jit(solution)/shard_map/all_to_all | solution.py:534
  97.7 1.0 shard_map.152
  98.7 36.0 %all_to_all.16.in_ref.mine_ref = bf16[64,9,16,128]{3,2,1,0:T(8,128)(2,1)S(1)} all-to-all(bf16[64,9,16,128]{3,2,1,0:T(8,128)(2,1)S(1)} %shard_map.152), channel_id=1, replica_groups=mesh['face'=8,'col'=8,'core'=2] {'face','col'}, dimensions={0} | all-to-all | bytes 4718592 | tf_op jit(solution)/shard_map/all_to_all | solution.py:536
  134.8 2.8 %collective-permute-start.6 = (bf16[64,9,16,128]{3,2,1,0:T(8,128)(2,1)S(1)}, bf16[64,9,16,128]{3,2,1,0:T(8,128)(2,1)S(1)}, u32[]{:S(2)}, u32[]{:S(2)}) collective-permute-start(bf16[64,9,16,128]{3,2,1,0:T(8,128)(2,1)S(1)} %all_to_all.16.in_ref.mine_ref), channel_id=1, source_target_pairs={{0,1},{1,0},{2,3},{3,2},{4,5},{5,4},{6,7},{7,6},{8,9},{9,8},{10,11... | collective-permute-start | bytes 7077896 | tf_op jit(solution)/shard_map/ppermute | solution.py:444
  137.6 2.1 %shard_map.153 = (f32[512,2048]{1,0:T(8,128)}, f32[2048,512]{1,0:T(8,128)}) custom-call(s32[1]{0:T(128)} %bitcast.core_ref, bf16[64,9,16,128]{3,2,1,0:T(8,128)(2,1)S(1)} %all_to_all.16.in_ref.mine_ref), custom_call_target="tpu_custom_call" | custom-call | tf_op jit(solution)/shard_map/pallas_call | solution.py:38
  139.7 2.1 %collective-permute-done.6.in_ref = bf16[64,9,16,128]{3,2,1,0:T(8,128)(2,1)S(1)} collective-permute-done((bf16[64,9,16,128]{3,2,1,0:T(8,128)(2,1)S(1)}, bf16[64,9,16,128]{3,2,1,0:T(8,128)(2,1)S(1)}, u32[]{:S(2)}, u32[]{:S(2)}) %collective-permute-start.6) | collective-permute-done | bytes 2359328 | tf_op jit(solution)/shard_map/ppermute | solution.py:444
  141.7 2.3 %shard_map.154 = (f32[512,2048]{1,0:T(8,128)}, f32[2048,512]{1,0:T(8,128)}, f32[256,512]{1,0:T(8,128)}, f32[49,512]{1,0:T(8,128)}, f32[1,512]{1,0:T(1,128)}) custom-call(s32[1]{0:T(128)} %bitcast.core_ref, bf16[64,9,16,128]{3,2,1,0:T(8,128)(2,1)S(1)} %collective-permute-done.6.in_ref, ...), custom_call_target="tpu_custom_call", output_to_operand_aliasing={{0}: (3, {}), {1}: (4, {})} | custom-call | tf_op jit(solution)/shard_map/pallas_call | solution.py:38
  (37 shorter events, 6.4 us)
Async XLA Ops:
  0.6 25.2 %copy-start.7 = (bf16[256,512]{1,0:T(8,128)(2,1)S(1)}, bf16[256,512]{1,0:T(8,128)(2,1)}, u32[]{:S(2)}) copy-start(bf16[256,512]{1,0:T(8,128)(2,1)} %w_embed_ref.3) | copy-start | bytes 786436
  0.6 0.9 copy-start.11
  1.6 0.7 copy-start.13
  3.6 35.5 %copy-start.4 = (bf16[256,512]{1,0:T(8,128)(2,1)S(1)}, bf16[256,512]{1,0:T(8,128)(2,1)}, u32[]{:S(2)}) copy-start(bf16[256,512]{1,0:T(8,128)(2,1)} %cot_ref.7) | copy-start | bytes 786436
  3.6 22.3 %all-to-all-start = ((bf16[128,8,128]{2,1,0:T(8,128)(2,1)}), bf16[128,8,128]{2,1,0:T(8,128)(2,1)S(1)}, u32[]{:S(2)}, u32[]{:S(2)}) async-start(bf16[128,8,128]{2,1,0:T(8,128)(2,1)} %bitcast.2), calls=%async_computation | async-start | bytes 524288 | tf_op jit(solution)/shard_map/all_to_all | solution.py:464
  16.4 1.6 %copy-start = (bf16[2048,512]{1,0:T(8,128)(2,1)S(1)}, bf16[2048,512]{1,0:T(8,128)(2,1)}, u32[]{:S(2)}) copy-start(bf16[2048,512]{1,0:T(8,128)(2,1)} %w_two_far.1) | copy-start | bytes 6291460
  18.0 0.9 copy-start.3
  18.9 0.9 copy-start.8
  19.9 19.2 %copy-start.2 = (bf16[512,2048]{1,0:T(8,128)(2,1)S(1)}, bf16[512,2048]{1,0:T(8,128)(2,1)}, u32[]{:S(2)}) copy-start(bf16[512,2048]{1,0:T(8,128)(2,1)} %w_one_ref.3) | copy-start | bytes 6291460
  20.7 1.3 copy-start.5
  22.0 0.7 copy-start.9
  25.9 1.0 copy-start.10
  28.0 7.3 %collective-permute-start = (bf16[48,256]{1,0:T(8,128)(2,1)}, bf16[48,256]{1,0:T(8,128)(2,1)}, u32[]{:S(2)}, u32[]{:S(2)}) collective-permute-start(bf16[48,256]{1,0:T(8,128)(2,1)} %get-tuple-element.35), channel_id=1, source_target_pairs={{0,16},{16,32},{32,48},{48,64},{64,80},{80,96},{96,112},{112,0},{1... | collective-permute-start | bytes 73736 | tf_op jit(solution)/shard_map/ppermute | solution.py:439
  28.2 7.0 %collective-permute-start.1 = (bf16[48,256]{1,0:T(8,128)(2,1)}, bf16[48,256]{1,0:T(8,128)(2,1)}, u32[]{:S(2)}, u32[]{:S(2)}) collective-permute-start(bf16[48,256]{1,0:T(8,128)(2,1)} %get-tuple-element.36), channel_id=1, source_target_pairs={{0,112},{16,0},{32,16},{48,32},{64,48},{80,64},{96,80},{112,96},{1... | collective-permute-start | bytes 73736 | tf_op jit(solution)/shard_map/ppermute | solution.py:439
  31.6 3.7 %collective-permute-start.2 = (bf16[48,256]{1,0:T(8,128)(2,1)}, bf16[48,256]{1,0:T(8,128)(2,1)}, u32[]{:S(2)}, u32[]{:S(2)}) collective-permute-start(bf16[48,256]{1,0:T(8,128)(2,1)} %get-tuple-element.37), channel_id=1, source_target_pairs={{0,1},{1,2},{2,3},{3,4},{4,5},{5,6},{6,7},{7,8},{8,9},{9,10},{10,1... | collective-permute-start | bytes 73736 | tf_op jit(solution)/shard_map/ppermute | solution.py:439
  33.7 5.4 %collective-permute-start.3 = (bf16[48,256]{1,0:T(8,128)(2,1)}, bf16[48,256]{1,0:T(8,128)(2,1)}, u32[]{:S(2)}, u32[]{:S(2)}) collective-permute-start(bf16[48,256]{1,0:T(8,128)(2,1)} %get-tuple-element.38), channel_id=1, source_target_pairs={{0,15},{1,0},{2,1},{3,2},{4,3},{5,4},{6,5},{7,6},{8,7},{9,8},{10,9... | collective-permute-start | bytes 73736 | tf_op jit(solution)/shard_map/ppermute | solution.py:439
  39.1 1.6 %copy-start.6 = (f32[256,2048]{1,0:T(8,128)S(1)}, f32[256,2048]{1,0:T(8,128)}, u32[]{:S(2)}) copy-start(f32[256,2048]{1,0:T(8,128)} %copy-done.5) | copy-start | bytes 6291460
  40.7 0.8 copy-start.12
  48.1 7.3 %collective-permute-start.4 = (bf16[512,16,128]{2,1,0:T(8,128)(2,1)S(1)}, bf16[512,16,128]{2,1,0:T(8,128)(2,1)S(1)}, u32[]{:S(2)}, u32[]{:S(2)}) collective-permute-start(bf16[512,16,128]{2,1,0:T(8,128)(2,1)S(1)} %get-tuple-element.43), channel_id=1, source_target_pairs={{0,1},{1,0},{2,3},{3,2},{4,5},{5,4},{6,7},{7,6},{8,9},{9,8},{10,11... | collective-permute-start | bytes 6291464 | tf_op jit(solution)/shard_map/ppermute | solution.py:444
  48.9 6.5 %copy-start.1 = (bf16[2048,512]{1,0:T(8,128)(2,1)S(1)}, bf16[2048,512]{1,0:T(8,128)(2,1)}, u32[]{:S(2)}) copy-start(bf16[2048,512]{1,0:T(8,128)(2,1)} %w_two_far.1) | copy-start | bytes 6291460
  55.3 2.5 %collective-permute-start.5 = (bf16[64,16,128]{2,1,0:T(8,128)(2,1)S(1)}, bf16[64,16,128]{2,1,0:T(8,128)(2,1)S(1)}, u32[]{:S(2)}, u32[]{:S(2)}) collective-permute-start(bf16[64,16,128]{2,1,0:T(8,128)(2,1)S(1)} %get-tuple-element.51), channel_id=1, source_target_pairs={{0,1},{1,0},{2,3},{3,2},{4,5},{5,4},{6,7},{7,6},{8,9},{9,8},{10,11... | collective-permute-start | bytes 786440 | tf_op jit(solution)/shard_map/ppermute | solution.py:444
  134.8 7.0 %collective-permute-start.6 = (bf16[64,9,16,128]{3,2,1,0:T(8,128)(2,1)S(1)}, bf16[64,9,16,128]{3,2,1,0:T(8,128)(2,1)S(1)}, u32[]{:S(2)}, u32[]{:S(2)}) collective-permute-start(bf16[64,9,16,128]{3,2,1,0:T(8,128)(2,1)S(1)} %all_to_all.16.in_ref.mine_ref), channel_id=1, source_target_pairs={{0,1},{1,0},{2,3},{3,2},{4,5},{5,4},{6,7},{7,6},{8,9},{9,8},{10,11... | collective-permute-start | bytes 7077896 | tf_op jit(solution)/shard_map/ppermute | solution.py:444

commit v4 on v3

--- a/solution.py
+++ b/solution.py
@@ -17,6 +17,7 @@
 LANE = 128
 ROWS2 = HALF + TAPS - 1
 STRIP = HALO * SIDE
+SHELF = 65536
 STEP = 256
 ALL = ("face", "col", "core")
 CHIPS = ("face", "col")
@@ -34,7 +35,7 @@
 
 def call(kernel, outs, scratch, limit, *args, far=(), far_outs=(), copies=0, aliases=None):
     vmem, scalar = pl.BlockSpec(memory_space=pltpu.VMEM), pl.BlockSpec(memory_space=pltpu.SMEM)
-    away = pl.BlockSpec(memory_space=pl.ANY)
+    away = pl.BlockSpec(memory_space=pltpu.HBM)
     return pl.pallas_call(
         kernel,
         out_shape=[jax.ShapeDtypeStruct(s, d) for s, d in outs],
@@ -45,7 +46,7 @@
         scratch_shapes=[pltpu.VMEM(s, d) for s, d in scratch]
         + [pltpu.SemaphoreType.DMA((copies,))] * bool(copies),
         input_output_aliases=aliases or {},
-        compiler_params=pltpu.CompilerParams(vmem_limit_bytes=limit * 2**20),
+        compiler_params=pltpu.CompilerParams(vmem_limit_bytes=int(limit * 2**20)),
     )(*args)
 
 
@@ -64,7 +65,7 @@
     return pl.ds((i * pitch + j) * 8 + h * 4 + cb, 8, stride=8)
 
 
-def route_kernel(row_far, obs_far, out_ref, row_ref, obs_ref, sem):
+def route_kernel(core_ref, row_far, obs_far, out_ref, row_ref, obs_ref, sem):
     fetch_row, fetch_obs = start(sem, (row_far, row_ref), (obs_far, obs_ref))
     fetch_row.wait()
     row = row_ref[...]
@@ -85,19 +86,50 @@
     out_ref[...] = jnp.where(first, moved[:, :LANE], moved[:, LANE:]).astype(BF16)
 
 
-def prepare_kernel(interp_ref, cot_ref, w_two_ref, weights_ref, d_act_ref):
+def shelf(width, slots, hidden, channels):
+    rows = (CELLS, 4 * STRIP, width + 80, hidden)
+    lanes = (slots, CELLS, channels, channels)
+    ends = [sum(rows[: k + 1]) for k in range(len(rows))]
+    return [(pl.ds(e - r, r), pl.ds(0, n)) for e, r, n in zip(ends, rows, lanes)]
+
+
+def prepare_kernel(
+    interp_ref, pick_ref, w_embed_ref, dw_ref, gain_ref, w_two_far, shelf_far,
+    weights_ref, small_ref, near_ref, w_two_ref, sem,
+):
+    tiles, slots = interp_ref.shape[:2]
+    width, channels = w_embed_ref.shape
+    spots = shelf(width, tiles * slots, w_two_far.shape[0], channels)
+    fetch = pltpu.make_async_copy(w_two_far, w_two_ref, sem.at[4])
+    fetch.start()
+    moves = [
+        pltpu.make_async_copy(a, shelf_far.at[spot], sem.at[k])
+        for k, (a, spot) in enumerate(zip((weights_ref, pick_ref, near_ref, w_two_ref), spots))
+    ]
+    moves[1].start()
+    small_ref[...] = jnp.zeros_like(small_ref)
+    small_ref[0 : TAPS * TAPS] = dw_ref[...].astype(F32)
+    small_ref[64:] = jnp.broadcast_to(gain_ref[...].astype(F32), (16, channels))
+    near_ref[0:width] = w_embed_ref[...]
+    near_ref[width:] = small_ref[...].astype(BF16)
+    moves[2].start()
     weights = interp_ref[...].astype(F32)
-    tiles, slots = weights.shape[:2]
     for k in range(slots):
         weights_ref[:, k * tiles : (k + 1) * tiles] = weights[:, k, :].T.astype(BF16)
-    for k in range(w_two_ref.shape[0] // STEP):
-        some = pl.ds(k * STEP, STEP)
-        d_act_ref[:, some] = dot(cot_ref[...], w_two_ref[some, :], NT)
+    moves[0].start()
+    fetch.wait()
+    moves[3].start()
+    for move in moves:
+        move.wait()
 
 
 def embed_kernel(
-    got_ref, weights_ref, w_embed_ref, pick_ref, grid_ref, emb_ref, s0, s1, s2, s3, wide_ref, rows_ref
-):
+    got_ref, shelf_far, grid_ref, emb_ref, near_ref, s0, s1, s2, s3, wide_ref, rows_ref, weights_ref, pick_ref, sem
+):
+    width, channels = near_ref.shape[0] - 80, near_ref.shape[1]
+    spots = shelf(width, weights_ref.shape[1], 0, channels)
+    targets = (weights_ref, pick_ref, near_ref)
+    fetches = start(sem, *((shelf_far.at[spot], b) for spot, b in zip(spots, targets)))
     wide_ref[...] = got_ref[...].astype(F32)
     tiles = got_ref.shape[0] // 8
     for k in range(4):
@@ -109,12 +141,14 @@
                 rows_ref[pl.ds(k * tiles + g, 16), pl.ds(half * LANE, LANE)] = jnp.concatenate(
                     two, axis=0
                 ).astype(BF16)
+    for fetch in fetches:
+        fetch.wait()
     gridded = dot(weights_ref[...], rows_ref[...]).astype(BF16)
     grid_ref[...] = gridded
     strips = dot(pick_ref[...], gridded).astype(BF16)
     for k, ref in enumerate((s0, s1, s2, s3)):
         ref[...] = strips[k * STRIP : (k + 1) * STRIP]
-    emb_ref[...] = dot(gridded, w_embed_ref[...]).astype(BF16)
+    emb_ref[...] = dot(gridded, near_ref[0:width]).astype(BF16)
 
 
 def tiles_of(part, two, one):
@@ -127,23 +161,25 @@
 
 
 def forward_kernel(
-    core_ref, emb_ref, s0, s1, s2, s3, place_ref, dw_ref, gain_ref, w_embed_ref, w_one_ref, d_act_far, cot_ref,
+    core_ref, emb_ref, s0, s1, s2, s3, place_ref, near_ref, w_one_ref, shelf_far, cot_ref,
     field_ref, normal_ref, inv_ref, scaled_ref, active_ref, d_hid_ref, kern_ref, theirs_ref,
-    strips_ref, cells_ref, flat_ref, conv_ref, two_ref, one_ref, d_act_ref, sem,
-):
-    (fetch,) = start(sem, (d_act_far, d_act_ref))
-    taps = dw_ref[...].astype(F32)
-    last = taps.shape[0] - 1
+    strips_ref, cells_ref, flat_ref, conv_ref, two_ref, one_ref, w_two_ref, sem,
+):
+    width, channels = near_ref.shape[0] - 80, near_ref.shape[1]
+    spot = shelf(width, 0, w_two_ref.shape[0], channels)[3]
+    (fetch,) = start(sem, (shelf_far.at[spot], w_two_ref))
+    taps = near_ref[width : width + 64].astype(F32)
+    last = TAPS * TAPS - 1
     for h in range(2):
         for cb in range(4):
             lanes = slice(cb * LANE, (cb + 1) * LANE)
             for g in range(0, last, 8):
                 kern_ref[pl.ds(g * 8 + h * 4 + cb, 8, stride=8), :] = taps[g : g + 8, lanes]
-            kern_ref[pl.ds(last * 8 + h * 4 + cb, 1), :] = taps[last:, lanes]
+            kern_ref[pl.ds(last * 8 + h * 4 + cb, 1), :] = taps[last : last + 1, lanes]
     for k, ref in enumerate((s0, s1, s2, s3)):
         strips_ref[k * STRIP : (k + 1) * STRIP] = ref[...]
     cells_ref[0:CELLS] = emb_ref[...]
-    cells_ref[CELLS:] = dot(strips_ref[...], w_embed_ref[...]).astype(BF16)
+    cells_ref[CELLS:] = dot(strips_ref[...], near_ref[0:width]).astype(BF16)
     flat_ref[...] = dot(place_ref[...], cells_ref[...])
     for x in range(FULL):
         for g in range(3):
@@ -169,6 +205,7 @@
 
     lax.fori_loop(0, HALF, conv_row, 0)
 
+    gain = near_ref[width + 64 :].astype(F32)
     for r in range(SIDE):
         h, i = divmod(r, HALF)
         parts = [
@@ -182,7 +219,7 @@
         rows = pl.ds(r * SIDE, SIDE)
         normal_ref[rows, :] = normal
         inv_ref[rows, :] = jnp.broadcast_to(inverse, (SIDE, LANE))
-        scaled_ref[rows, :] = (normal * gain_ref[...].astype(F32)).astype(BF16)
+        scaled_ref[rows, :] = (normal * gain).astype(BF16)
 
     fetch.wait()
     for k in range(w_one_ref.shape[1] // STEP):
@@ -193,7 +230,8 @@
         upper = 0.5 + 0.5 * tanh
         slope = upper + (0.5 * pre) * (1.0 - tanh * tanh) * (ROOT + (3.0 * ROOT * CUBE) * square)
         active_ref[:, some] = (pre * upper).astype(BF16)
-        d_hid_ref[:, some] = (d_act_ref[:, some] * slope).astype(BF16)
+        d_act = dot(cot_ref[...], w_two_ref[some, :], NT)
+        d_hid_ref[:, some] = (d_act * slope).astype(BF16)
 
     steps = theirs_ref.shape[0] // 128
     for k in range(steps):
@@ -206,18 +244,19 @@
 
 def backward_kernel(
     core_ref, grid_ref, s0, s1, s2, s3, place_ref, field_ref, normal_ref, inv_ref, d_hid_ref, w_one_ref,
-    gain_ref, kern_ref, cot_ref,
+    near_ref, kern_ref, cot_ref,
     mine_ref, theirs_ref,
     d_scaled_ref, d_conv_ref, spread_ref, flat_ref, taps_ref, cells_ref, small_ref,
 ):
     d_scaled_ref[...] = dot(d_hid_ref[...], w_one_ref[...], NT)
     total = jnp.zeros((SIDE, normal_ref.shape[1]), F32)
+    gain = near_ref[near_ref.shape[0] - 16 :].astype(F32)
     for r in range(SIDE):
         h, i = divmod(r, HALF)
         rows = pl.ds(r * SIDE, SIDE)
         normal, d_scaled = normal_ref[rows, :], d_scaled_ref[rows, :]
         total = total + d_scaled * normal
-        d_normal = d_scaled * gain_ref[...].astype(F32)
+        d_normal = d_scaled * gain
         mean = jnp.mean(d_normal, axis=1, keepdims=True)
         along = jnp.mean(d_normal * normal, axis=1, keepdims=True)
         d_conv = (d_normal - mean - normal * along) * inv_ref[rows, 0:1]
@@ -295,12 +334,7 @@
         ].astype(BF16)
 
 
-def pair_kernel(
-    core_ref, scaled_ref, active_ref, d_hid_ref, cot_ref, big_ref, emb_ref, w_two_far,
-    out_ref, feature_far,
-    two_ref, one_ref, w_two_ref, feature_ref, sem,
-):
-    (fetch,) = start(sem, (w_two_far, w_two_ref))
+def pair_kernel(core_ref, scaled_ref, active_ref, d_hid_ref, cot_ref, big_ref, out_ref, two_ref, one_ref):
     steps = big_ref.shape[0] // 128
     for k in range(steps):
         some = pl.ds(pl.multiple_of((core_ref[0] * steps + k) * STEP, STEP), STEP)
@@ -308,11 +342,6 @@
         one_ref[...] = dot(scaled_ref[...], d_hid_ref[:, some], TN)
         for t, ref, rows, lanes in tiles_of(k, two_ref, one_ref):
             out_ref[t // 8, t % 8] = (ref[rows, lanes] + big_ref[t].astype(F32)).astype(BF16)
-    fetch.wait()
-    feature_ref[...] = (emb_ref[...].astype(F32) + dot(active_ref[...], w_two_ref[...])).astype(BF16)
-    put = pltpu.make_async_copy(feature_ref, feature_far, sem.at[1])
-    put.start()
-    put.wait()
 
 
 def join_kernel(mine_ref, small_ref, paired_far, out_far, tile_ref, sem):
@@ -355,8 +384,15 @@
     return puts
 
 
-def first_kernel(core_ref, in_ref, one_far, two_far, one_ref, two_ref, sem):
-    for put in assemble_half(core_ref[0], in_ref, one_far, two_far, one_ref, two_ref, sem):
+def first_kernel(
+    core_ref, in_ref, emb_ref, active_ref, w_two_ref,
+    one_far, two_far, feature_far, one_ref, two_ref, feature_ref, sem,
+):
+    puts = assemble_half(core_ref[0], in_ref, one_far, two_far, one_ref, two_ref, sem)
+    feature_ref[...] = (emb_ref[...].astype(F32) + dot(active_ref[...], w_two_ref[...])).astype(BF16)
+    puts.append(pltpu.make_async_copy(feature_ref, feature_far, sem.at[len(puts)]))
+    puts[-1].start()
+    for put in puts:
         put.wait()
 
 
@@ -453,25 +489,24 @@
     slots = interp.shape[2]
     core = lax.axis_index("core").reshape(1)
     place, pick = selectors(tile_spin[0, 0])
-    gain = norm_gain[None]
-
     (leaving,) = call(
         route_kernel,
         [((tiles * 8, LANE), BF16)],
         [((1, obs_values.shape[0]), jnp.int32), (obs_values.shape, BF16)],
-        16, obs_tile.reshape(1, -1), obs_values, far=(0, 1), copies=2,
+        60.5, core, obs_tile.reshape(1, -1), obs_values, far=(1, 2), copies=2,
     )
     arrived = lax.all_to_all(leaving.reshape(tiles, 8, LANE), ALL, 0, 0, tiled=True)
-    weights, d_active = call(
-        prepare_kernel, [((CELLS, tiles * slots), BF16), ((CELLS, hidden), F32)], [], 16,
-        interp[0], cotangent, w_two,
-    )
-
-    gridded, embedded, *strips = call(
+    stacked = ((CELLS, tiles * slots), BF16)
+    near = ((width + 80, channels), BF16)
+    (shelved,) = call(
+        prepare_kernel, [((SHELF, channels), BF16)], [stacked, ((80, channels), F32), near, (w_two.shape, BF16)],
+        60.5, interp[0], pick, w_embed, dw_kernel, norm_gain[None], w_two, far=(5,), far_outs=(0,), copies=5,
+    )
+    gridded, embedded, nearby, *strips = call(
         embed_kernel,
-        [((CELLS, width), BF16), ((CELLS, channels), BF16)] + [((STRIP, width), BF16)] * 4,
-        [((tiles * 8, LANE), F32), ((tiles * slots, width), BF16)],
-        12, arrived.reshape(tiles * 8, LANE), weights, w_embed, pick,
+        [((CELLS, width), BF16), ((CELLS, channels), BF16), near] + [((STRIP, width), BF16)] * 4,
+        [((tiles * 8, LANE), F32), ((tiles * slots, width), BF16), stacked, (pick.shape, BF16)],
+        16, arrived.reshape(tiles * 8, LANE), shelved, far=(1,), copies=3,
     )
     strips = exchange(strips)
     cells2 = ROWS2 * PITCH * 8
@@ -498,10 +533,9 @@
             ((CELLS * 4, LANE), F32),
         ]
         + step_sums
-        + [((CELLS, hidden), F32)],
+        + [((hidden, channels), BF16)],
         20,
-        core, embedded, *strips, place, dw_kernel, gain, w_embed, w_one, d_active, cotangent,
-        far=(11,), copies=1,
+        core, embedded, *strips, place, nearby, w_one, shelved, cotangent, far=(9,), copies=1,
     )
     big = swap(theirs)
 
@@ -518,14 +552,12 @@
             ((2 * chips * 16, LANE), F32),
         ],
         20,
-        core, gridded, *strips, place, field, normal, inverse, d_hidden, w_one, gain, taps, cotangent,
+        core, gridded, *strips, place, field, normal, inverse, d_hidden, w_one, nearby, taps, cotangent,
     )
     small = swap(theirs)
     whole = ((chips, 9, 16, LANE), BF16)
-    paired, output = call(
-        pair_kernel, [whole, ((CELLS, channels), BF16)],
-        step_sums + [((hidden, channels), BF16), ((CELLS, channels), BF16)], 20,
-        core, scaled, active, d_hidden, cotangent, big, embedded, w_two, far=(7,), far_outs=(1,), copies=2,
+    (paired,) = call(
+        pair_kernel, [whole], step_sums, 20, core, scaled, active, d_hidden, cotangent, big
     )
     (paired,) = call(
         join_kernel, [whole], [((chips, 16, LANE), BF16)], 4,
@@ -539,8 +571,9 @@
     large = [((channels, hidden), F32), ((hidden, channels), F32)]
     steps = hidden // STEP // 2
     buffers = [((steps, channels, STEP), F32), ((steps, STEP, channels), F32)]
-    grads = call(
-        first_kernel, large, buffers, 12, core, here, far_outs=(0, 1), copies=2 * steps
+    *grads, output = call(
+        first_kernel, large + [((CELLS, channels), BF16)], buffers + [((CELLS, channels), BF16)], 16,
+        core, here, embedded, active, w_two, far_outs=(0, 1, 2), copies=2 * steps + 1,
     )
     count = TAPS * TAPS
     minor = [((width, channels), F32), ((count, channels), F32), ((1, channels), F32)]

time: 145 us -> 137 us (0.945)
  local copies, waits for them, and re-layouts: 11.2 us -> 1.28 us
  Pallas kernels: 24.2 us -> 25.9 us
  waiting for transfers between devices: 9.01 us -> 10.7 us
    unnamed x28 -> x6, local copies, waits for them, and re-layouts: 10.5 us -> 0.01 us
    pallas_call x10, Pallas kernels: 24.2 us -> 25.9 us  [call(): pl.pallas_call(kernel, out_shape=[jax.ShapeDtypeStruct(s, d) for s, d in...]
  transfers between devices with their start and end apart: 8 -> 8, of which waited for: 3 -> 5; matrix products, arithmetic and copies ran while one was open for 2% -> 2% of each run, Pallas kernels for 8% -> 10%
where the time goes in v4:
time: 137 us; the launch traced here: 136 us
  blocking collectives  75 us (55%)
  Pallas kernels  25.9 us (19%)
  starting transfers between devices  21.3 us (16%)
  waiting for transfers between devices  10.7 us (8%)
  between operations  1.42 us (1%)
    all_to_all x1, blocking collectives, on_device(): paired = lax.all_to_all(paired, CHIPS, 0, 0, tiled=True)  39.1 us
    all_to_all x1, blocking collectives, on_device(): here = lax.all_to_all(summed, CHIPS, 0, 0, tiled=True)  35.8 us
    pallas_call x10, Pallas kernels, call(): pl.pallas_call(kernel, out_shape=[jax.ShapeDtypeStruct(s, d) for s, d in...  25.9 us
    all_to_all x1, starting transfers between devices, on_device(): lax.all_to_all(leaving.reshape(tiles, 8, LANE), ALL, 0, 0, tiled=True)  11.5 us
    ppermute x4, starting transfers between devices, exchange(): lax.ppermute(strip, axis, [(i, (i + way) % size) for i in range(size)])  5.8 us
    ppermute x4, waiting for transfers between devices, exchange(): lax.ppermute(strip, axis, [(i, (i + way) % size) for i in range(size)])  4.88 us
    ppermute x3, starting transfers between devices, swap(): return lax.ppermute(value, 'core', [(0, 1), (1, 0)])  3.99 us
    all_to_all x1, waiting for transfers between devices, on_device(): lax.all_to_all(leaving.reshape(tiles, 8, LANE), ALL, 0, 0, tiled=True)  3.77 us
  transfers between devices with their start and end apart: 8, of which 5 were waited for; matrix products, arithmetic and copies ran while one was open for 2% of the time, Pallas kernels for 10%

profile of v4, /device:TPU:1, one launch (start us, length us, event | category | flops | bytes accessed | tf_op | source)
XLA Modules:
  0.0 136.4 jit_solution(4292206856977796634)
XLA Ops:
  0.6 1.9 %shard_map.145 = bf16[1024,128]{1,0:T(8,128)(2,1)} custom-call(s32[1]{0:T(128)} %bitcast.core_ref, s32[1,256]{1,0:T(1,128)} %bitcast.12, bf16[256,256]{1,0:T(8,128)(2,1)} %obs_far.1), custom_call_target="tpu_custom_call" | custom-call | tf_op jit(solution)/shard_map/pallas_call | solution.py:39
  2.6 11.5 %all-to-all-start = ((bf16[128,8,128]{2,1,0:T(8,128)(2,1)}), bf16[128,8,128]{2,1,0:T(8,128)(2,1)S(1)}, u32[]{:S(2)}, u32[]{:S(2)}) async-start(bf16[128,8,128]{2,1,0:T(8,128)(2,1)} %bitcast.10), calls=%async_computation | async-start | bytes 524288 | tf_op jit(solution)/shard_map/all_to_all | solution.py:498
  14.7 1.3 broadcast_in_dim.9.gain_ref
  16.0 0.7 fusion.2.pick_ref
  16.7 4.3 %shard_map.146.shelf_far = bf16[65536,512]{1,0:T(8,128)(2,1)} custom-call(bf16[128,4,256]{2,1,0:T(4,128)(2,1)} %bitcast.11, bf16[192,256]{1,0:T(8,128)(2,1)} %fusion.2.pick_ref, bf16[256,512]{1,0:T(8,128)(2,1)} %w_embed_ref.1, bf16[49,512]{1,0:T(8,128)(2,1)} %dw_ref.1, bf16[1,512]{1,0:T(2,128)(2,1)} %broadcast_in_dim.9.gain_ref, bf16[2048,512]{1,0:T(8,128)(2,1)} %w_two_ref.1), custom_call_target="tpu_custom_call" | custom-call | tf_op jit(solution)/shard_map/pallas_call | solution.py:39
  21.1 3.8 %all-to-all-done = bf16[128,8,128]{2,1,0:T(8,128)(2,1)S(1)} async-done(((bf16[128,8,128]{2,1,0:T(8,128)(2,1)}), bf16[128,8,128]{2,1,0:T(8,128)(2,1)S(1)}, u32[]{:S(2)}, u32[]{:S(2)}) %all-to-all-start) | async-done | bytes 262176 | tf_op jit(solution)/shard_map/all_to_all | solution.py:498
  24.9 1.8 %shard_map.147 = (bf16[256,256]{1,0:T(8,128)(2,1)S(1)}, bf16[256,512]{1,0:T(8,128)(2,1)S(1)}, bf16[336,512]{1,0:T(8,128)(2,1)S(1)}, bf16[48,256]{1,0:T(8,128)(2,...) custom-call(bf16[1024,128]{1,0:T(8,128)(2,1)S(1)} %bitcast.9, ...), custom_call_target="tpu_custom_call" | custom-call | tf_op jit(solution)/shard_map/pallas_call | solution.py:39
  26.7 0.3 collective-permute-start
  27.0 3.4 %collective-permute-start.1 = (bf16[48,256]{1,0:T(8,128)(2,1)S(1)}, bf16[48,256]{1,0:T(8,128)(2,1)S(1)}, u32[]{:S(2)}, u32[]{:S(2)}) collective-permute-start(bf16[48,256]{1,0:T(8,128)(2,1)S(1)} %get-tuple-element.33), channel_id=1, source_target_pairs={{0,112},{16,0},{32,16},{48,32},{64,48},{80,64},{96,80},{112,96},{1... | collective-permute-start | bytes 73736 | tf_op jit(solution)/shard_map/ppermute | solution.py:475
  30.4 2.2 %collective-permute-start.2 = (bf16[48,256]{1,0:T(8,128)(2,1)S(1)}, bf16[48,256]{1,0:T(8,128)(2,1)S(1)}, u32[]{:S(2)}, u32[]{:S(2)}) collective-permute-start(bf16[48,256]{1,0:T(8,128)(2,1)S(1)} %get-tuple-element.34), channel_id=1, source_target_pairs={{0,1},{1,2},{2,3},{3,4},{4,5},{5,6},{6,7},{7,8},{8,9},{9,10},{10,1... | collective-permute-start | bytes 73736 | tf_op jit(solution)/shard_map/ppermute | solution.py:475
  32.7 0.8 collective-permute-done.2.s2
  33.5 4.1 %collective-permute-done.3.s3 = bf16[48,256]{1,0:T(8,128)(2,1)S(1)} collective-permute-done((bf16[48,256]{1,0:T(8,128)(2,1)S(1)}, bf16[48,256]{1,0:T(8,128)(2,1)S(1)}, u32[]{:S(2)}, u32[]{:S(2)}) %collective-permute-start.3) | collective-permute-done | bytes 24608 | tf_op jit(solution)/shard_map/ppermute | solution.py:475
  37.6 5.3 %shard_map.148 = (f32[2688,128]{1,0:T(8,128)S(1)}, f32[256,512]{1,0:T(8,128)S(1)}, f32[256,128]{1,0:T(8,128)S(1)}, bf16[256,512]{1,0:T(8,128)(2,1)S(1)}, bf16[25...) custom-call(s32[1]{0:T(128)} %bitcast.core_ref, ...), custom_call_target="tpu_custom_call" | custom-call | tf_op jit(solution)/shard_map/pallas_call | solution.py:39
  42.9 0.7 collective-permute-start.5
  43.7 5.4 %shard_map.149 = (f32[64,16,128]{2,1,0:T(8,128)S(1)}, bf16[64,16,128]{2,1,0:T(8,128)(2,1)S(1)}) custom-call(s32[1]{0:T(128)} %bitcast.core_ref, bf16[256,256]{1,0:T(8,128)(2,1)S(1)} %get-tuple-element.31.grid_ref, bf16[48,256]{1,0:T(8,128)(2,1)S(1)} %collective-permute-done.s0, bf16[48,256]{1,0:T(8,128)(2,1)S(1)} %collective-permute-done.1.s1, ...), custom_call_target="tpu_custom_call" | custom-call | tf_op jit(solution)/shard_map/pallas_call | solution.py:39
  49.2 0.8 shard_map.150.paired_far
  50.0 0.7 collective-permute-done.4.small_ref
  50.8 39.1 %all_to_all.15.in_ref = bf16[64,9,16,128]{3,2,1,0:T(8,128)(2,1)S(1)} all-to-all(bf16[64,9,16,128]{3,2,1,0:T(8,128)(2,1)S(1)} %shard_map.151), channel_id=1, replica_groups=mesh['face'=8,'col'=8,'core'=2] {'face','col'}, dimensions={0} | all-to-all | bytes 4718592 | tf_op jit(solution)/shard_map/all_to_all | solution.py:566
  89.9 1.0 shard_map.152
  91.0 35.8 %all_to_all.16.in_ref.mine_ref = bf16[64,9,16,128]{3,2,1,0:T(8,128)(2,1)S(1)} all-to-all(bf16[64,9,16,128]{3,2,1,0:T(8,128)(2,1)S(1)} %shard_map.152), channel_id=1, replica_groups=mesh['face'=8,'col'=8,'core'=2] {'face','col'}, dimensions={0} | all-to-all | bytes 4718592 | tf_op jit(solution)/shard_map/all_to_all | solution.py:568
  126.8 3.2 %collective-permute-start.6 = (bf16[64,9,16,128]{3,2,1,0:T(8,128)(2,1)S(1)}, bf16[64,9,16,128]{3,2,1,0:T(8,128)(2,1)S(1)}, u32[]{:S(2)}, u32[]{:S(2)}) collective-permute-start(bf16[64,9,16,128]{3,2,1,0:T(8,128)(2,1)S(1)} %all_to_all.16.in_ref.mine_ref), channel_id=1, source_target_pairs={{0,1},{1,0},{2,3},{3,2},{4,5},{5,4},{6,7},{7,6},{8,9},{9,8},{10,11... | collective-permute-start | bytes 7077896 | tf_op jit(solution)/shard_map/ppermute | solution.py:480
  130.0 2.8 %shard_map.153 = (f32[512,2048]{1,0:T(8,128)}, f32[2048,512]{1,0:T(8,128)}, bf16[256,512]{1,0:T(8,128)(2,1)}) custom-call(s32[1]{0:T(128)} %bitcast.core_ref, bf16[64,9,16,128]{3,2,1,0:T(8,128)(2,1)S(1)} %all_to_all.16.in_ref.mine_ref, bf16[256,512]{1,0:T(8,128)(2,1)S(1)} %get-tuple-element.36.emb_ref, bf16[256,2048]{1,0:T(8,128)(2,1)S(1)} %get-tuple-element.46.active_ref, ...), custom_call_target="tpu_custom_call" | custom-call | tf_op jit(solution)/shard_map/pallas_call | solution.py:39
  132.8 1.3 collective-permute-done.6.in_ref
  134.1 2.3 %shard_map.154 = (f32[512,2048]{1,0:T(8,128)}, f32[2048,512]{1,0:T(8,128)}, f32[256,512]{1,0:T(8,128)}, f32[49,512]{1,0:T(8,128)}, f32[1,512]{1,0:T(1,128)}) custom-call(s32[1]{0:T(128)} %bitcast.core_ref, bf16[64,9,16,128]{3,2,1,0:T(8,128)(2,1)S(1)} %collective-permute-done.6.in_ref, ...), custom_call_target="tpu_custom_call", output_to_operand_aliasing={{0}: (3, {}), {1}: (4, {})} | custom-call | tf_op jit(solution)/shard_map/pallas_call | solution.py:39
  (15 shorter events, 0.4 us)
Async XLA Ops:
  2.6 22.3 %all-to-all-start = ((bf16[128,8,128]{2,1,0:T(8,128)(2,1)}), bf16[128,8,128]{2,1,0:T(8,128)(2,1)S(1)}, u32[]{:S(2)}, u32[]{:S(2)}) async-start(bf16[128,8,128]{2,1,0:T(8,128)(2,1)} %bitcast.10), calls=%async_computation | async-start | bytes 524288 | tf_op jit(solution)/shard_map/all_to_all | solution.py:498
  24.9 12.7 %copy-start = (bf16[512,2048]{1,0:T(8,128)(2,1)S(1)}, bf16[512,2048]{1,0:T(8,128)(2,1)}, u32[]{:S(2)}) copy-start(bf16[512,2048]{1,0:T(8,128)(2,1)} %w_one_ref.3) | copy-start | bytes 6291460
  24.9 12.7 %copy-start.2 = (bf16[256,512]{1,0:T(8,128)(2,1)S(1)}, bf16[256,512]{1,0:T(8,128)(2,1)}, u32[]{:S(2)}) copy-start(bf16[256,512]{1,0:T(8,128)(2,1)} %cot_ref.5) | copy-start | bytes 786436
  26.7 6.0 %collective-permute-start = (bf16[48,256]{1,0:T(8,128)(2,1)S(1)}, bf16[48,256]{1,0:T(8,128)(2,1)S(1)}, u32[]{:S(2)}, u32[]{:S(2)}) collective-permute-start(bf16[48,256]{1,0:T(8,128)(2,1)S(1)} %get-tuple-element.32), channel_id=1, source_target_pairs={{0,16},{16,32},{32,48},{48,64},{64,80},{80,96},{96,112},{112,0},{1... | collective-permute-start | bytes 73736 | tf_op jit(solution)/shard_map/ppermute | solution.py:475
  27.0 5.7 %collective-permute-start.1 = (bf16[48,256]{1,0:T(8,128)(2,1)S(1)}, bf16[48,256]{1,0:T(8,128)(2,1)S(1)}, u32[]{:S(2)}, u32[]{:S(2)}) collective-permute-start(bf16[48,256]{1,0:T(8,128)(2,1)S(1)} %get-tuple-element.33), channel_id=1, source_target_pairs={{0,112},{16,0},{32,16},{48,32},{64,48},{80,64},{96,80},{112,96},{1... | collective-permute-start | bytes 73736 | tf_op jit(solution)/shard_map/ppermute | solution.py:475
  30.4 3.1 %collective-permute-start.2 = (bf16[48,256]{1,0:T(8,128)(2,1)S(1)}, bf16[48,256]{1,0:T(8,128)(2,1)S(1)}, u32[]{:S(2)}, u32[]{:S(2)}) collective-permute-start(bf16[48,256]{1,0:T(8,128)(2,1)S(1)} %get-tuple-element.34), channel_id=1, source_target_pairs={{0,1},{1,2},{2,3},{3,4},{4,5},{5,6},{6,7},{7,8},{8,9},{9,10},{10,1... | collective-permute-start | bytes 73736 | tf_op jit(solution)/shard_map/ppermute | solution.py:475
  32.5 5.1 %collective-permute-start.3 = (bf16[48,256]{1,0:T(8,128)(2,1)S(1)}, bf16[48,256]{1,0:T(8,128)(2,1)S(1)}, u32[]{:S(2)}, u32[]{:S(2)}) collective-permute-start(bf16[48,256]{1,0:T(8,128)(2,1)S(1)} %get-tuple-element.35), channel_id=1, source_target_pairs={{0,15},{1,0},{2,1},{3,2},{4,3},{5,4},{6,5},{7,6},{8,7},{9,8},{10,9... | collective-permute-start | bytes 73736 | tf_op jit(solution)/shard_map/ppermute | solution.py:475
  42.9 6.3 %collective-permute-start.5 = (bf16[512,16,128]{2,1,0:T(8,128)(2,1)S(1)}, bf16[512,16,128]{2,1,0:T(8,128)(2,1)S(1)}, u32[]{:S(2)}, u32[]{:S(2)}) collective-permute-start(bf16[512,16,128]{2,1,0:T(8,128)(2,1)S(1)} %get-tuple-element.47), channel_id=1, source_target_pairs={{0,1},{1,0},{2,3},{3,2},{4,5},{5,4},{6,7},{7,6},{8,9},{9,8},{10,11... | collective-permute-start | bytes 6291464 | tf_op jit(solution)/shard_map/ppermute | solution.py:480
  49.1 1.6 %collective-permute-start.4 = (bf16[64,16,128]{2,1,0:T(8,128)(2,1)S(1)}, bf16[64,16,128]{2,1,0:T(8,128)(2,1)S(1)}, u32[]{:S(2)}, u32[]{:S(2)}) collective-permute-start(bf16[64,16,128]{2,1,0:T(8,128)(2,1)S(1)} %get-tuple-element.44), channel_id=1, source_target_pairs={{0,1},{1,0},{2,3},{3,2},{4,5},{5,4},{6,7},{7,6},{8,9},{9,8},{10,11... | collective-permute-start | bytes 786440 | tf_op jit(solution)/shard_map/ppermute | solution.py:480
  90.9 39.0 %copy-start.1 = (bf16[2048,512]{1,0:T(8,128)(2,1)S(1)}, bf16[2048,512]{1,0:T(8,128)(2,1)}, u32[]{:S(2)}) copy-start(bf16[2048,512]{1,0:T(8,128)(2,1)} %w_two_ref.1) | copy-start | bytes 6291460
  126.8 7.3 %collective-permute-start.6 = (bf16[64,9,16,128]{3,2,1,0:T(8,128)(2,1)S(1)}, bf16[64,9,16,128]{3,2,1,0:T(8,128)(2,1)S(1)}, u32[]{:S(2)}, u32[]{:S(2)}) collective-permute-start(bf16[64,9,16,128]{3,2,1,0:T(8,128)(2,1)S(1)} %all_to_all.16.in_ref.mine_ref), channel_id=1, source_target_pairs={{0,1},{1,0},{2,3},{3,2},{4,5},{5,4},{6,7},{7,6},{8,9},{9,8},{10,11... | collective-permute-start | bytes 7077896 | tf_op jit(solution)/shard_map/ppermute | solution.py:480

commit v5 on v4

--- a/solution.py
+++ b/solution.py
@@ -55,6 +55,15 @@
     for move in moves:
         move.start()
     return moves
+
+
+def strip_at(k):
+    return pl.ds(pl.multiple_of(k * STRIP, 16), STRIP)
+
+
+def take_strips(core, refs, strips_ref):
+    for ref, k in zip(refs, (0, 1, 2 + core, 3 - core)):
+        strips_ref[strip_at(k), :] = ref[...]
 
 
 def block(i, j, pitch):
@@ -124,7 +133,8 @@
 
 
 def embed_kernel(
-    got_ref, shelf_far, grid_ref, emb_ref, near_ref, s0, s1, s2, s3, wide_ref, rows_ref, weights_ref, pick_ref, sem
+    core_ref, got_ref, shelf_far, grid_ref, emb_ref, near_ref, up_ref, down_ref, far_ref, by_ref,
+    wide_ref, rows_ref, weights_ref, pick_ref, strips_ref, sem,
 ):
     width, channels = near_ref.shape[0] - 80, near_ref.shape[1]
     spots = shelf(width, weights_ref.shape[1], 0, channels)
@@ -145,9 +155,10 @@
         fetch.wait()
     gridded = dot(weights_ref[...], rows_ref[...]).astype(BF16)
     grid_ref[...] = gridded
-    strips = dot(pick_ref[...], gridded).astype(BF16)
-    for k, ref in enumerate((s0, s1, s2, s3)):
-        ref[...] = strips[k * STRIP : (k + 1) * STRIP]
+    strips_ref[...] = dot(pick_ref[...], gridded).astype(BF16)
+    core = core_ref[0]
+    for ref, k in ((up_ref, 0), (down_ref, 1), (far_ref, 3 - core), (by_ref, 2 + core)):
+        ref[...] = strips_ref[strip_at(k), :]
     emb_ref[...] = dot(gridded, near_ref[0:width]).astype(BF16)
 
 
@@ -160,10 +171,8 @@
         yield part * 128 + 64 + k, one, pl.ds(r * 16, 16), pl.ds(c * LANE, LANE)
 
 
-def forward_kernel(
-    core_ref, emb_ref, s0, s1, s2, s3, place_ref, near_ref, w_one_ref, shelf_far, cot_ref,
-    field_ref, normal_ref, inv_ref, scaled_ref, active_ref, d_hid_ref, kern_ref, theirs_ref,
-    strips_ref, cells_ref, flat_ref, conv_ref, two_ref, one_ref, w_two_ref, sem,
+def inner_kernel(
+    emb_ref, near_ref, shelf_far, cot_ref, field_ref, conv_ref, kern_ref, d_act_ref, w_two_ref, sem
 ):
     width, channels = near_ref.shape[0] - 80, near_ref.shape[1]
     spot = shelf(width, 0, w_two_ref.shape[0], channels)[3]
@@ -176,34 +185,85 @@
             for g in range(0, last, 8):
                 kern_ref[pl.ds(g * 8 + h * 4 + cb, 8, stride=8), :] = taps[g : g + 8, lanes]
             kern_ref[pl.ds(last * 8 + h * 4 + cb, 1), :] = taps[last : last + 1, lanes]
-    for k, ref in enumerate((s0, s1, s2, s3)):
-        strips_ref[k * STRIP : (k + 1) * STRIP] = ref[...]
-    cells_ref[0:CELLS] = emb_ref[...]
-    cells_ref[CELLS:] = dot(strips_ref[...], near_ref[0:width]).astype(BF16)
-    flat_ref[...] = dot(place_ref[...], cells_ref[...])
-    for x in range(FULL):
-        for g in range(3):
+    for i in range(SIDE):
+        own = emb_ref[pl.ds(i * SIDE, SIDE), :].astype(F32)
+        x = i + HALO
+        for g in range(0, SIDE, 8):
             for cb in range(4):
-                value = flat_ref[pl.ds(x * PITCH + 8 * g, 8), pl.ds(cb * LANE, LANE)]
+                value = own[g : g + 8, cb * LANE : (cb + 1) * LANE]
                 if x < ROWS2:
-                    field_ref[comb(x, 8 * g, PITCH, 0, cb), :] = value
+                    field_ref[comb(x, HALO + g, PITCH, 0, cb), :] = value
                 if x >= HALF:
-                    field_ref[comb(x - HALF, 8 * g, PITCH, 1, cb), :] = value
-
-    def conv_row(i, carry):
+                    field_ref[comb(x - HALF, HALO + g, PITCH, 1, cb), :] = value
+    fetch.wait()
+    step = d_act_ref.shape[1] // HALF
+    for i in range(HALF):
+        some = pl.ds(i * step, step)
+        d_act_ref[:, some] = dot(cot_ref[...], w_two_ref[some, :], NT)
         sums = [jnp.zeros((8, LANE), F32)] * SIDE
-        for a in range(TAPS):
-            taps = [kern_ref[pl.ds((a * TAPS + b) * 8, 8), :] for b in range(TAPS)]
-            for y in range(FULL):
-                here = field_ref[block(i + a, y, PITCH), :]
+        for x in range(max(i, HALO), min(i + TAPS, HALF + HALO)):
+            taps = [kern_ref[block(x - i, b, TAPS), :] for b in range(TAPS)]
+            for y in range(HALO, SIDE + HALO):
+                here = field_ref[block(x, y, PITCH), :]
                 for b in range(TAPS):
                     if 0 <= y - b < SIDE:
                         sums[y - b] = sums[y - b] + here * taps[b]
         for j in range(SIDE):
             conv_ref[block(i, j, SIDE), :] = sums[j]
-        return carry
-
-    lax.fori_loop(0, HALF, conv_row, 0)
+
+
+OUTER = (0, 1, 2, 19, 20, 21)
+
+
+def ring():
+    at = 0
+    for x in OUTER:
+        for y in range(0, PITCH, 8):
+            yield at, x, y
+            at += 8
+    for x in range(HALO, SIDE + HALO):
+        for y in (0, PITCH - 8):
+            yield at, x, y
+            at += 8
+
+
+RING = 8 * len(list(ring()))
+
+
+def forward_kernel(
+    core_ref, s0, s1, s2, s3, place_ref, near_ref, w_one_ref, own_ref, part_ref, kern_ref, d_act_ref, cot_ref,
+    field_ref, normal_ref, inv_ref, scaled_ref, active_ref, d_hid_ref, theirs_ref,
+    strips_ref, ring_ref, conv_ref,
+):
+    width, channels = near_ref.shape[0] - 80, near_ref.shape[1]
+    take_strips(core_ref[0], (s0, s1, s2, s3), strips_ref)
+    halo = dot(strips_ref[...], near_ref[0:width]).astype(BF16)
+    ring_ref[...] = dot(place_ref[...], halo)
+    field_ref[...] = own_ref[...]
+    for at, x, y in ring():
+        skip, count = (0, 8) if x in OUTER else (0, HALO) if y == 0 else (HALO, HALO)
+        for cb in range(4):
+            value = ring_ref[pl.ds(at + skip, count), pl.ds(cb * LANE, LANE)]
+            if x < ROWS2:
+                field_ref[pl.ds((x * PITCH + y + skip) * 8 + cb, count, stride=8), :] = value
+            if x >= HALF:
+                row = ((x - HALF) * PITCH + y + skip) * 8 + 4 + cb
+                field_ref[pl.ds(row, count, stride=8), :] = value
+
+    for i in range(HALF):
+        sums = [part_ref[block(i, j, SIDE), :] for j in range(SIDE)]
+        for a in range(TAPS):
+            x = i + a
+            whole = x < HALO or x >= HALF + HALO
+            taps = [kern_ref[block(a, b, TAPS), :] for b in range(TAPS)]
+            for y in range(FULL):
+                if whole or y < HALO or y >= SIDE + HALO:
+                    here = field_ref[block(x, y, PITCH), :]
+                    for b in range(TAPS):
+                        if 0 <= y - b < SIDE:
+                            sums[y - b] = sums[y - b] + here * taps[b]
+        for j in range(SIDE):
+            conv_ref[block(i, j, SIDE), :] = sums[j]
 
     gain = near_ref[width + 64 :].astype(F32)
     for r in range(SIDE):
@@ -221,7 +281,6 @@
         inv_ref[rows, :] = jnp.broadcast_to(inverse, (SIDE, LANE))
         scaled_ref[rows, :] = (normal * gain).astype(BF16)
 
-    fetch.wait()
     for k in range(w_one_ref.shape[1] // STEP):
         some = pl.ds(k * STEP, STEP)
         pre = dot(scaled_ref[...], w_one_ref[:, some])
@@ -230,23 +289,21 @@
         upper = 0.5 + 0.5 * tanh
         slope = upper + (0.5 * pre) * (1.0 - tanh * tanh) * (ROOT + (3.0 * ROOT * CUBE) * square)
         active_ref[:, some] = (pre * upper).astype(BF16)
-        d_act = dot(cot_ref[...], w_two_ref[some, :], NT)
-        d_hid_ref[:, some] = (d_act * slope).astype(BF16)
-
-    steps = theirs_ref.shape[0] // 128
-    for k in range(steps):
-        some = pl.ds(pl.multiple_of(((1 - core_ref[0]) * steps + k) * STEP, STEP), STEP)
-        two_ref[...] = dot(active_ref[:, some], cot_ref[...], TN)
-        one_ref[...] = dot(scaled_ref[...], d_hid_ref[:, some], TN)
-        for t, ref, rows, lanes in tiles_of(k, two_ref, one_ref):
-            theirs_ref[t] = ref[rows, lanes].astype(BF16)
+        d_hid_ref[:, some] = (d_act_ref[:, some] * slope).astype(BF16)
+
+    half = w_one_ref.shape[1] // 2
+    away = pl.ds(pl.multiple_of((1 - core_ref[0]) * half, half), half)
+    theirs_ref[:, 0:half] = active_ref[:, away]
+    theirs_ref[:, half : 2 * half] = d_hid_ref[:, away]
+    theirs_ref[:, 2 * half : 2 * half + channels] = scaled_ref[...]
+    theirs_ref[:, 2 * half + channels :] = cot_ref[...]
 
 
 def backward_kernel(
     core_ref, grid_ref, s0, s1, s2, s3, place_ref, field_ref, normal_ref, inv_ref, d_hid_ref, w_one_ref,
     near_ref, kern_ref, cot_ref,
     mine_ref, theirs_ref,
-    d_scaled_ref, d_conv_ref, spread_ref, flat_ref, taps_ref, cells_ref, small_ref,
+    d_scaled_ref, d_conv_ref, spread_ref, own_ref, ring_ref, taps_ref, strips_ref, small_ref,
 ):
     d_scaled_ref[...] = dot(d_hid_ref[...], w_one_ref[...], NT)
     total = jnp.zeros((SIDE, normal_ref.shape[1]), F32)
@@ -271,48 +328,44 @@
     taps_ref[...] = jnp.zeros_like(taps_ref)
 
     def conv_row(i, carry):
+        d_conv = [d_conv_ref[block(i, j, SIDE), :] for j in range(SIDE)]
         for a in range(TAPS):
-            taps = [kern_ref[pl.ds((a * TAPS + b) * 8, 8), :] for b in range(TAPS)]
+            taps = [kern_ref[block(a, b, TAPS), :] for b in range(TAPS)]
+            sums = [taps_ref[block(a, b, TAPS), :] for b in range(TAPS)]
             for y in range(FULL):
+                here = field_ref[block(i + a, y, PITCH), :]
                 value = spread_ref[block(i + a, y, PITCH), :]
                 for b in range(TAPS):
                     if 0 <= y - b < SIDE:
-                        value = value + d_conv_ref[block(i, y - b, SIDE), :] * taps[b]
+                        value = value + d_conv[y - b] * taps[b]
+                        sums[b] = sums[b] + here * d_conv[y - b]
                 spread_ref[block(i + a, y, PITCH), :] = value
+            for b in range(TAPS):
+                taps_ref[block(a, b, TAPS), :] = sums[b]
         return carry
 
     lax.fori_loop(0, HALF, conv_row, 0)
 
-    def tap_row(i, carry):
-        for a in range(TAPS):
-            sums = [taps_ref[pl.ds((a * TAPS + b) * 8, 8), :] for b in range(TAPS)]
-            for y in range(FULL):
-                here = field_ref[block(i + a, y, PITCH), :]
-                for b in range(TAPS):
-                    if 0 <= y - b < SIDE:
-                        sums[b] = sums[b] + here * d_conv_ref[block(i, y - b, SIDE), :]
-            for b in range(TAPS):
-                taps_ref[pl.ds((a * TAPS + b) * 8, 8), :] = sums[b]
-        return carry
-
-    lax.fori_loop(0, HALF, tap_row, 0)
-
-    for x in range(FULL):
-        for g in range(3):
-            for cb in range(4):
-                value = None
-                if x < ROWS2:
-                    value = spread_ref[comb(x, 8 * g, PITCH, 0, cb), :]
-                if x >= HALF:
-                    more = spread_ref[comb(x - HALF, 8 * g, PITCH, 1, cb), :]
-                    value = more if value is None else value + more
-                flat_ref[pl.ds(x * PITCH + 8 * g, 8), pl.ds(cb * LANE, LANE)] = value
-
-    cells_ref[0:CELLS] = grid_ref[...]
-    for k, ref in enumerate((s0, s1, s2, s3)):
-        cells_ref[CELLS + k * STRIP : CELLS + (k + 1) * STRIP] = ref[...]
-    spots = dot(place_ref[...], cells_ref[...]).astype(BF16)
-    grad_embed = dot(spots, flat_ref[...].astype(BF16), TN) + dot(grid_ref[...], cot_ref[...], TN)
+    def part(x, y, cb):
+        value = None
+        if x < ROWS2:
+            value = spread_ref[comb(x, y, PITCH, 0, cb), :]
+        if x >= HALF:
+            more = spread_ref[comb(x - HALF, y, PITCH, 1, cb), :]
+            value = more if value is None else value + more
+        return value
+
+    for cb in range(4):
+        lanes = pl.ds(cb * LANE, LANE)
+        for at, x, y in ring():
+            ring_ref[pl.ds(at, 8), lanes] = part(x, y, cb)
+        for i in range(SIDE):
+            for g in range(0, SIDE, 8):
+                own_ref[pl.ds(i * SIDE + g, 8), lanes] = part(i + HALO, g + HALO, cb)
+    take_strips(core_ref[0], (s0, s1, s2, s3), strips_ref)
+    d_halo = dot(place_ref[...], ring_ref[...].astype(BF16), TN).astype(BF16)
+    d_own = (own_ref[...] + cot_ref[...].astype(F32)).astype(BF16)
+    grad_embed = dot(grid_ref[...], d_own, TN) + dot(strips_ref[...], d_halo, TN)
 
     half = mine_ref.shape[0]
     small_ref[...] = jnp.zeros_like(small_ref)
@@ -334,14 +387,20 @@
         ].astype(BF16)
 
 
-def pair_kernel(core_ref, scaled_ref, active_ref, d_hid_ref, cot_ref, big_ref, out_ref, two_ref, one_ref):
-    steps = big_ref.shape[0] // 128
-    for k in range(steps):
-        some = pl.ds(pl.multiple_of((core_ref[0] * steps + k) * STEP, STEP), STEP)
-        two_ref[...] = dot(active_ref[:, some], cot_ref[...], TN)
-        one_ref[...] = dot(scaled_ref[...], d_hid_ref[:, some], TN)
+def pair_kernel(core_ref, scaled_ref, active_ref, d_hid_ref, cot_ref, their_ref, out_ref, two_ref, one_ref):
+    half, channels = active_ref.shape[1] // 2, cot_ref.shape[1]
+    their_scaled = their_ref[:, 2 * half : 2 * half + channels]
+    their_cot = their_ref[:, 2 * half + channels :]
+    for k in range(half // STEP):
+        some = pl.ds(pl.multiple_of(core_ref[0] * half + k * STEP, STEP), STEP)
+        two_ref[...] = dot(active_ref[:, some], cot_ref[...], TN) + dot(
+            their_ref[:, k * STEP : (k + 1) * STEP], their_cot, TN
+        )
+        one_ref[...] = dot(scaled_ref[...], d_hid_ref[:, some], TN) + dot(
+            their_scaled, their_ref[:, half + k * STEP : half + (k + 1) * STEP], TN
+        )
         for t, ref, rows, lanes in tiles_of(k, two_ref, one_ref):
-            out_ref[t // 8, t % 8] = (ref[rows, lanes] + big_ref[t].astype(F32)).astype(BF16)
+            out_ref[t // 8, t % 8] = ref[rows, lanes].astype(BF16)
 
 
 def join_kernel(mine_ref, small_ref, paired_far, out_far, tile_ref, sem):
@@ -441,8 +500,8 @@
 
 
 def selectors(spin):
-    p = jnp.arange(FULL * PITCH, dtype=jnp.int32)
-    x, y = p // PITCH, p % PITCH
+    x = jnp.asarray([x for _, x, _ in ring() for _ in range(8)], jnp.int32)
+    y = jnp.asarray([y + k for _, _, y in ring() for k in range(8)], jnp.int32)
     row, col = turned(spin, x, y, FULL - 1)
     end = SIDE + HALO
     in_row, in_col = (row >= HALO) & (row < end), (col >= HALO) & (col < end)
@@ -453,27 +512,26 @@
         jnp.where((col >= end) & in_row, 3 * STRIP + (col - end) * SIDE + row - HALO, -1))),
     )
     strip = jnp.where(y < FULL, strip, -1)
-    own = (x >= HALO) & (x < end) & (y >= HALO) & (y < end)
-    source = jnp.where(own, (x - HALO) * SIDE + y - HALO, jnp.where(strip >= 0, strip + CELLS, -1))
-    place = (source[:, None] == jnp.arange(CELLS + 4 * STRIP, dtype=jnp.int32)[None]).astype(BF16)
+    k = jnp.arange(4 * STRIP, dtype=jnp.int32)
+    place = (strip[:, None] == k[None]).astype(BF16)
 
     q = jnp.arange(CELLS, dtype=jnp.int32)
     row, col = turned(spin, q // SIDE, q % SIDE, SIDE - 1)
     cut = SIDE - HALO
     by_row = jnp.where(row >= cut, (row - cut) * SIDE + col, jnp.where(row < HALO, STRIP + row * SIDE + col, -1))
     by_col = jnp.where(col >= cut, 2 * STRIP + (col - cut) * SIDE + row, jnp.where(col < HALO, 3 * STRIP + col * SIDE + row, -1))
-    k = jnp.arange(4 * STRIP, dtype=jnp.int32)
     pick = ((k[:, None] == by_row[None]) | (k[:, None] == by_col[None])).astype(BF16)
     return place, pick
 
 
-def exchange(strips):
-    moves = (("face", 1), ("face", -1), (("col", "core"), 1), (("col", "core"), -1))
-    out = []
-    for strip, (axis, way) in zip(strips, moves):
-        size = lax.axis_size(axis)
-        out.append(lax.ppermute(strip, axis, [(i, (i + way) % size) for i in range(size)]))
-    return out
+def exchange(up, down, far, by):
+    beside = ("col", "core")
+    tiles, faces = lax.axis_size(beside), lax.axis_size("face")
+    pairs = [(i, (i + 1) % tiles) for i in range(1, tiles, 2)]
+    far = lax.ppermute(far, beside, pairs + [(j, i) for i, j in pairs])
+    up = lax.ppermute(up, "face", [(i, (i + 1) % faces) for i in range(faces)])
+    down = lax.ppermute(down, "face", [((i + 1) % faces, i) for i in range(faces)])
+    return up, down, far, swap(by)
 
 
 def swap(value):
@@ -505,52 +563,40 @@
     gridded, embedded, nearby, *strips = call(
         embed_kernel,
         [((CELLS, width), BF16), ((CELLS, channels), BF16), near] + [((STRIP, width), BF16)] * 4,
-        [((tiles * 8, LANE), F32), ((tiles * slots, width), BF16), stacked, (pick.shape, BF16)],
-        16, arrived.reshape(tiles * 8, LANE), shelved, far=(1,), copies=3,
-    )
-    strips = exchange(strips)
-    cells2 = ROWS2 * PITCH * 8
-    flat = ((FULL * PITCH, channels), F32)
+        [((tiles * 8, LANE), F32), ((tiles * slots, width), BF16), stacked, (pick.shape, BF16), ((4 * STRIP, width), BF16)],
+        16, core, arrived.reshape(tiles * 8, LANE), shelved, far=(2,), copies=3,
+    )
+    strips = exchange(*strips)
+    cells2 = ((ROWS2 * PITCH * 8, LANE), F32)
     kernel = ((TAPS * TAPS * 8, LANE), F32)
+    blocks, cells = ((CELLS * 4, LANE), F32), ((CELLS, channels), F32)
+    around = ((RING, channels), F32)
     step_sums = [((STEP, channels), F32), ((channels, STEP), F32)]
-    half = hidden * channels // (16 * LANE)
-    field, normal, inverse, scaled, active, d_hidden, taps, theirs = call(
+    field, conv, taps, d_active = call(
+        inner_kernel, [cells2, blocks, kernel, ((CELLS, hidden), F32)], [((hidden, channels), BF16)], 20,
+        embedded, nearby, shelved, cotangent, far=(2,), copies=1,
+    )
+    field, normal, inverse, scaled, active, d_hidden, theirs = call(
         forward_kernel,
         [
-            ((cells2, LANE), F32),
-            ((CELLS, channels), F32),
+            cells2,
+            cells,
             ((CELLS, LANE), F32),
             ((CELLS, channels), BF16),
             ((CELLS, hidden), BF16),
             ((CELLS, hidden), BF16),
-            kernel,
-            ((half, 16, LANE), BF16),
+            ((CELLS, hidden + 2 * channels), BF16),
         ],
-        [
-            ((4 * STRIP, width), BF16),
-            ((CELLS + 4 * STRIP, channels), BF16),
-            flat,
-            ((CELLS * 4, LANE), F32),
-        ]
-        + step_sums
-        + [((hidden, channels), BF16)],
+        [((4 * STRIP, width), BF16), around, blocks],
         20,
-        core, embedded, *strips, place, nearby, w_one, shelved, cotangent, far=(9,), copies=1,
+        core, *strips, place, nearby, w_one, field, conv, taps, d_active, cotangent,
     )
     big = swap(theirs)
 
     mine, theirs = call(
         backward_kernel,
         [((chips, 16, LANE), F32), ((chips, 16, LANE), BF16)],
-        [
-            ((CELLS, channels), F32),
-            ((CELLS * 4, LANE), F32),
-            ((cells2, LANE), F32),
-            flat,
-            kernel,
-            ((CELLS + 4 * STRIP, width), BF16),
-            ((2 * chips * 16, LANE), F32),
-        ],
+        [cells, blocks, cells2, cells, around, kernel, ((4 * STRIP, width), BF16), ((2 * chips * 16, LANE), F32)],
         20,
         core, gridded, *strips, place, field, normal, inverse, d_hidden, w_one, nearby, taps, cotangent,
     )

time: 137 us -> 131 us (0.956)
  waiting for transfers between devices: 10.7 us -> 5.19 us
  blocking collectives: 75 us -> 72.4 us
  starting transfers between devices: 21.3 us -> 22.8 us
    ppermute x4 -> x3, waiting for transfers between devices: 4.88 us -> 0.01 us  [the longest x1 0.01 us: exchange(): lax.ppermute(down, 'face', [((i + 1) % faces, i) for i in range(faces)])]
    all_to_all x1, blocking collectives: 39.1 us -> 36.2 us  [on_device(): paired = lax.all_to_all(paired, CHIPS, 0, 0, tiled=True)]
    ppermute x3 -> x4, starting transfers between devices: 3.99 us -> 5.5 us  [swap(): return lax.ppermute(value, 'core', [(0, 1), (1, 0)])]
    pallas_call x10 -> x11, Pallas kernels: 25.9 us -> 26.7 us  [call(): pl.pallas_call(kernel, out_shape=[jax.ShapeDtypeStruct(s, d) for s, d in...]
    ppermute x4 -> x3, starting transfers between devices: 5.8 us -> 5.8 us  [the longest x1 3.36 us: exchange(): lax.ppermute(down, 'face', [((i + 1) % faces, i) for i in range(faces)])]
  transfers between devices with their start and end apart: 8 -> 8, of which waited for: 5 -> 3; matrix products, arithmetic and copies ran while one was open for 2% -> 2% of each run, Pallas kernels for 10% -> 13%
where the time goes in v5:
time: 131 us
  blocking collectives  72.4 us (55%)
  Pallas kernels  26.7 us (20%)
  starting transfers between devices  22.8 us (17%)
  waiting for transfers between devices  5.19 us (4%)
  between operations  1.68 us (1%)
    all_to_all x1, blocking collectives, on_device(): here = lax.all_to_all(summed, CHIPS, 0, 0, tiled=True)  36.3 us
    all_to_all x1, blocking collectives, on_device(): paired = lax.all_to_all(paired, CHIPS, 0, 0, tiled=True)  36.2 us
    pallas_call x11, Pallas kernels, call(): pl.pallas_call(kernel, out_shape=[jax.ShapeDtypeStruct(s, d) for s, d in...  26.7 us
    all_to_all x1, starting transfers between devices, on_device(): lax.all_to_all(leaving.reshape(tiles, 8, LANE), ALL, 0, 0, tiled=True)  11.5 us
    ppermute x4, starting transfers between devices, swap(): return lax.ppermute(value, 'core', [(0, 1), (1, 0)])  5.5 us
    all_to_all x1, waiting for transfers between devices, on_device(): lax.all_to_all(leaving.reshape(tiles, 8, LANE), ALL, 0, 0, tiled=True)  3.67 us
    ppermute x1, starting transfers between devices, exchange(): lax.ppermute(down, 'face', [((i + 1) % faces, i) for i in range(faces)])  3.36 us
  transfers between devices with their start and end apart: 8, of which 3 were waited for; matrix products, arithmetic and copies ran while one was open for 2% of the time, Pallas kernels for 13%

profile of v5, /device:TPU:1, one launch (start us, length us, event | category | flops | bytes accessed | tf_op | source)
XLA Modules:
  0.0 131.0 jit_solution(9528067911104679003)
XLA Ops:
  0.6 1.9 %shard_map.163 = bf16[1024,128]{1,0:T(8,128)(2,1)} custom-call(s32[1]{0:T(128)} %bitcast.core_ref, s32[1,256]{1,0:T(1,128)} %bitcast.12, bf16[256,256]{1,0:T(8,128)(2,1)} %obs_far.1), custom_call_target="tpu_custom_call" | custom-call | tf_op jit(solution)/shard_map/pallas_call | solution.py:39
  2.6 11.5 %all-to-all-start = ((bf16[128,8,128]{2,1,0:T(8,128)(2,1)}), bf16[128,8,128]{2,1,0:T(8,128)(2,1)S(1)}, u32[]{:S(2)}, u32[]{:S(2)}) async-start(bf16[128,8,128]{2,1,0:T(8,128)(2,1)} %bitcast.10), calls=%async_computation | async-start | bytes 524288 | tf_op jit(solution)/shard_map/all_to_all | solution.py:556
  14.8 0.7 fusion.2.pick_ref
  15.4 1.3 broadcast_in_dim.10.gain_ref
  16.7 4.4 %shard_map.164.shelf_far = bf16[65536,512]{1,0:T(8,128)(2,1)} custom-call(bf16[128,4,256]{2,1,0:T(4,128)(2,1)} %bitcast.11, bf16[192,256]{1,0:T(8,128)(2,1)} %fusion.2.pick_ref, bf16[256,512]{1,0:T(8,128)(2,1)} %w_embed_ref.1, bf16[49,512]{1,0:T(8,128)(2,1)} %dw_ref.1, bf16[1,512]{1,0:T(2,128)(2,1)} %broadcast_in_dim.10.gain_ref, bf16[2048,512]{1,0:T(8,128)(2,1)} %w_two_ref.1), custom_call_target="tpu_custom_call" | custom-call | tf_op jit(solution)/shard_map/pallas_call | solution.py:39
  21.2 3.7 %all-to-all-done = bf16[128,8,128]{2,1,0:T(8,128)(2,1)S(1)} async-done(((bf16[128,8,128]{2,1,0:T(8,128)(2,1)}), bf16[128,8,128]{2,1,0:T(8,128)(2,1)S(1)}, u32[]{:S(2)}, u32[]{:S(2)}) %all-to-all-start) | async-done | bytes 262176 | tf_op jit(solution)/shard_map/all_to_all | solution.py:556
  24.9 1.7 %shard_map.165 = (bf16[256,256]{1,0:T(8,128)(2,1)S(1)}, bf16[256,512]{1,0:T(8,128)(2,1)S(1)}, bf16[336,512]{1,0:T(8,128)(2,1)S(1)}, bf16[48,256]{1,0:T(8,128)(2,...) custom-call(s32[1]{0:T(128)} %bitcast.core_ref, ...), custom_call_target="tpu_custom_call" | custom-call | tf_op jit(solution)/shard_map/pallas_call | solution.py:39
  26.6 0.3 collective-permute-start
  26.9 3.4 %collective-permute-start.1 = (bf16[48,256]{1,0:T(8,128)(2,1)S(1)}, bf16[48,256]{1,0:T(8,128)(2,1)S(1)}, u32[]{:S(2)}, u32[]{:S(2)}) collective-permute-start(bf16[48,256]{1,0:T(8,128)(2,1)S(1)} %get-tuple-element.36), channel_id=1, source_target_pairs={{16,0},{32,16},{48,32},{64,48},{80,64},{96,80},{112,96},{0,112},{1... | collective-permute-start | bytes 73736 | tf_op jit(solution)/shard_map/ppermute | solution.py:533
  30.2 2.2 %collective-permute-start.2 = (bf16[48,256]{1,0:T(8,128)(2,1)S(1)}, bf16[48,256]{1,0:T(8,128)(2,1)S(1)}, u32[]{:S(2)}, u32[]{:S(2)}) collective-permute-start(bf16[48,256]{1,0:T(8,128)(2,1)S(1)} %get-tuple-element.37), channel_id=1, source_target_pairs={{1,2},{3,4},{5,6},{7,8},{9,10},{11,12},{13,14},{15,0},{2,1},{4,3},... | collective-permute-start | bytes 73736 | tf_op jit(solution)/shard_map/ppermute | solution.py:531
  32.4 0.7 collective-permute-start.3
  33.2 3.0 %shard_map.166 = (f32[2688,128]{1,0:T(8,128)S(1)}, f32[1024,128]{1,0:T(8,128)S(1)}, f32[392,128]{1,0:T(8,128)S(1)}, f32[256,2048]{1,0:T(8,128)S(1)}) custom-call(bf16[256,512]{1,0:T(8,128)(2,1)S(1)} %get-tuple-element.40.emb_ref, bf16[336,512]{1,0:T(8,128)(2,1)S(1)} %get-tuple-element.39.near_ref, bf16[65536,512]{1,0:T(8,128)(2,1)} %shard_map.164.shelf_far, ...), custom_call_target="tpu_custom_call" | custom-call | tf_op jit(solution)/shard_map/pallas_call | solution.py:39
  36.2 2.9 %shard_map.167 = (f32[2688,128]{1,0:T(8,128)S(1)}, f32[256,512]{1,0:T(8,128)S(1)}, f32[256,128]{1,0:T(8,128)S(1)}, bf16[256,512]{1,0:T(8,128)(2,1)S(1)}, bf16[25...) custom-call(s32[1]{0:T(128)} %bitcast.core_ref, ...), custom_call_target="tpu_custom_call" | custom-call | tf_op jit(solution)/shard_map/pallas_call | solution.py:39
  39.1 1.9 %collective-permute-start.5 = (bf16[256,3072]{1,0:T(8,128)(2,1)S(1)}, bf16[256,3072]{1,0:T(8,128)(2,1)S(1)}, u32[]{:S(2)}, u32[]{:S(2)}) collective-permute-start(bf16[256,3072]{1,0:T(8,128)(2,1)S(1)} %get-tuple-element.53), channel_id=1, source_target_pairs={{0,1},{1,0},{2,3},{3,2},{4,5},{5,4},{6,7},{7,6},{8,9},{9,8},{10,11... | collective-permute-start | bytes 4718600 | tf_op jit(solution)/shard_map/ppermute | solution.py:538
  41.1 5.2 %shard_map.168 = (f32[64,16,128]{2,1,0:T(8,128)S(1)}, bf16[64,16,128]{2,1,0:T(8,128)(2,1)S(1)}) custom-call(s32[1]{0:T(128)} %bitcast.core_ref, bf16[256,256]{1,0:T(8,128)(2,1)S(1)} %get-tuple-element.34.grid_ref, bf16[48,256]{1,0:T(8,128)(2,1)S(1)} %collective-permute-done.s0, bf16[48,256]{1,0:T(8,128)(2,1)S(1)} %collective-permute-done.1.s1, ...), custom_call_target="tpu_custom_call" | custom-call | tf_op jit(solution)/shard_map/pallas_call | solution.py:39
  46.4 1.3 shard_map.169.paired_far
  47.7 0.2 collective-permute-done.4.small_ref
  48.0 36.2 %all_to_all.15.in_ref = bf16[64,9,16,128]{3,2,1,0:T(8,128)(2,1)S(1)} all-to-all(bf16[64,9,16,128]{3,2,1,0:T(8,128)(2,1)S(1)} %shard_map.170), channel_id=1, replica_groups=mesh['face'=8,'col'=8,'core'=2] {'face','col'}, dimensions={0} | all-to-all | bytes 4718592 | tf_op jit(solution)/shard_map/all_to_all | solution.py:612
  84.2 1.0 shard_map.171
  85.2 36.3 %all_to_all.16.in_ref.mine_ref = bf16[64,9,16,128]{3,2,1,0:T(8,128)(2,1)S(1)} all-to-all(bf16[64,9,16,128]{3,2,1,0:T(8,128)(2,1)S(1)} %shard_map.171), channel_id=1, replica_groups=mesh['face'=8,'col'=8,'core'=2] {'face','col'}, dimensions={0} | all-to-all | bytes 4718592 | tf_op jit(solution)/shard_map/all_to_all | solution.py:614
  121.5 2.8 %collective-permute-start.6 = (bf16[64,9,16,128]{3,2,1,0:T(8,128)(2,1)S(1)}, bf16[64,9,16,128]{3,2,1,0:T(8,128)(2,1)S(1)}, u32[]{:S(2)}, u32[]{:S(2)}) collective-permute-start(bf16[64,9,16,128]{3,2,1,0:T(8,128)(2,1)S(1)} %all_to_all.16.in_ref.mine_ref), channel_id=1, source_target_pairs={{0,1},{1,0},{2,3},{3,2},{4,5},{5,4},{6,7},{7,6},{8,9},{9,8},{10,11... | collective-permute-start | bytes 7077896 | tf_op jit(solution)/shard_map/ppermute | solution.py:538
  124.3 2.8 %shard_map.172 = (f32[512,2048]{1,0:T(8,128)}, f32[2048,512]{1,0:T(8,128)}, bf16[256,512]{1,0:T(8,128)(2,1)}) custom-call(s32[1]{0:T(128)} %bitcast.core_ref, bf16[64,9,16,128]{3,2,1,0:T(8,128)(2,1)S(1)} %all_to_all.16.in_ref.mine_ref, bf16[256,512]{1,0:T(8,128)(2,1)S(1)} %get-tuple-element.40.emb_ref, bf16[256,2048]{1,0:T(8,128)(2,1)S(1)} %get-tuple-element.52.active_ref, ...), custom_call_target="tpu_custom_call" | custom-call | tf_op jit(solution)/shard_map/pallas_call | solution.py:39
  127.2 1.3 collective-permute-done.6.in_ref
  128.5 2.3 %shard_map.173 = (f32[512,2048]{1,0:T(8,128)}, f32[2048,512]{1,0:T(8,128)}, f32[256,512]{1,0:T(8,128)}, f32[49,512]{1,0:T(8,128)}, f32[1,512]{1,0:T(1,128)}) custom-call(s32[1]{0:T(128)} %bitcast.core_ref, bf16[64,9,16,128]{3,2,1,0:T(8,128)(2,1)S(1)} %collective-permute-done.6.in_ref, ...), custom_call_target="tpu_custom_call", output_to_operand_aliasing={{0}: (3, {}), {1}: (4, {})} | custom-call | tf_op jit(solution)/shard_map/pallas_call | solution.py:39
  (26 shorter events, 0.4 us)
Async XLA Ops:
  2.6 22.3 %all-to-all-start = ((bf16[128,8,128]{2,1,0:T(8,128)(2,1)}), bf16[128,8,128]{2,1,0:T(8,128)(2,1)S(1)}, u32[]{:S(2)}, u32[]{:S(2)}) async-start(bf16[128,8,128]{2,1,0:T(8,128)(2,1)} %bitcast.10), calls=%async_computation | async-start | bytes 524288 | tf_op jit(solution)/shard_map/all_to_all | solution.py:556
  16.7 4.4 %copy-start.3 = (s32[400]{0:T(512)S(1)}, s32[400]{0:T(512)}, u32[]{:S(2)}) copy-start(s32[400]{0:T(512)} %constant.85.clone) | copy-start | bytes 4804
  16.7 4.4 %copy-start.4 = (s32[400]{0:T(512)S(1)}, s32[400]{0:T(512)}, u32[]{:S(2)}) copy-start(s32[400]{0:T(512)} %constant.86.clone) | copy-start | bytes 4804
  16.7 4.4 %copy-start.5 = (s32[400]{0:T(512)S(1)}, s32[400]{0:T(512)}, u32[]{:S(2)}) copy-start(s32[400]{0:T(512)} %constant.91) | copy-start | bytes 4804
  16.7 4.4 %copy-start.6 = (s32[400]{0:T(512)S(1)}, s32[400]{0:T(512)}, u32[]{:S(2)}) copy-start(s32[400]{0:T(512)} %constant.93) | copy-start | bytes 4804
  16.7 4.4 %copy-start.7 = (pred[400]{0:T(512)(128)(4,1)S(1)}, pred[400]{0:T(512)(128)(4,1)}, u32[]{:S(2)}) copy-start(pred[400]{0:T(512)(128)(4,1)} %constant.89) | copy-start | bytes 1204
  24.9 8.3 %copy-start.2 = (bf16[256,512]{1,0:T(8,128)(2,1)S(1)}, bf16[256,512]{1,0:T(8,128)(2,1)}, u32[]{:S(2)}) copy-start(bf16[256,512]{1,0:T(8,128)(2,1)} %cot_ref.7) | copy-start | bytes 786436
  26.6 9.6 %collective-permute-start = (bf16[48,256]{1,0:T(8,128)(2,1)S(1)}, bf16[48,256]{1,0:T(8,128)(2,1)S(1)}, u32[]{:S(2)}, u32[]{:S(2)}) collective-permute-start(bf16[48,256]{1,0:T(8,128)(2,1)S(1)} %get-tuple-element.35), channel_id=1, source_target_pairs={{0,16},{16,32},{32,48},{48,64},{64,80},{80,96},{96,112},{112,0},{1... | collective-permute-start | bytes 73736 | tf_op jit(solution)/shard_map/ppermute | solution.py:532
  26.9 9.3 %collective-permute-start.1 = (bf16[48,256]{1,0:T(8,128)(2,1)S(1)}, bf16[48,256]{1,0:T(8,128)(2,1)S(1)}, u32[]{:S(2)}, u32[]{:S(2)}) collective-permute-start(bf16[48,256]{1,0:T(8,128)(2,1)S(1)} %get-tuple-element.36), channel_id=1, source_target_pairs={{16,0},{32,16},{48,32},{64,48},{80,64},{96,80},{112,96},{0,112},{1... | collective-permute-start | bytes 73736 | tf_op jit(solution)/shard_map/ppermute | solution.py:533
  30.2 6.0 %collective-permute-start.2 = (bf16[48,256]{1,0:T(8,128)(2,1)S(1)}, bf16[48,256]{1,0:T(8,128)(2,1)S(1)}, u32[]{:S(2)}, u32[]{:S(2)}) collective-permute-start(bf16[48,256]{1,0:T(8,128)(2,1)S(1)} %get-tuple-element.37), channel_id=1, source_target_pairs={{1,2},{3,4},{5,6},{7,8},{9,10},{11,12},{13,14},{15,0},{2,1},{4,3},... | collective-permute-start | bytes 73736 | tf_op jit(solution)/shard_map/ppermute | solution.py:531
  32.4 3.8 %collective-permute-start.3 = (bf16[48,256]{1,0:T(8,128)(2,1)S(1)}, bf16[48,256]{1,0:T(8,128)(2,1)S(1)}, u32[]{:S(2)}, u32[]{:S(2)}) collective-permute-start(bf16[48,256]{1,0:T(8,128)(2,1)S(1)} %get-tuple-element.38), channel_id=1, source_target_pairs={{0,1},{1,0},{2,3},{3,2},{4,5},{5,4},{6,7},{7,6},{8,9},{9,8},{10,11... | collective-permute-start | bytes 73736 | tf_op jit(solution)/shard_map/ppermute | solution.py:538
  33.2 3.0 %copy-start.1 = (bf16[512,2048]{1,0:T(8,128)(2,1)S(1)}, bf16[512,2048]{1,0:T(8,128)(2,1)}, u32[]{:S(2)}) copy-start(bf16[512,2048]{1,0:T(8,128)(2,1)} %w_one_ref.3) | copy-start | bytes 6291460
  39.1 7.3 %collective-permute-start.5 = (bf16[256,3072]{1,0:T(8,128)(2,1)S(1)}, bf16[256,3072]{1,0:T(8,128)(2,1)S(1)}, u32[]{:S(2)}, u32[]{:S(2)}) collective-permute-start(bf16[256,3072]{1,0:T(8,128)(2,1)S(1)} %get-tuple-element.53), channel_id=1, source_target_pairs={{0,1},{1,0},{2,3},{3,2},{4,5},{5,4},{6,7},{7,6},{8,9},{9,8},{10,11... | collective-permute-start | bytes 4718600 | tf_op jit(solution)/shard_map/ppermute | solution.py:538
  46.3 1.6 %collective-permute-start.4 = (bf16[64,16,128]{2,1,0:T(8,128)(2,1)S(1)}, bf16[64,16,128]{2,1,0:T(8,128)(2,1)S(1)}, u32[]{:S(2)}, u32[]{:S(2)}) collective-permute-start(bf16[64,16,128]{2,1,0:T(8,128)(2,1)S(1)} %get-tuple-element.50), channel_id=1, source_target_pairs={{0,1},{1,0},{2,3},{3,2},{4,5},{5,4},{6,7},{7,6},{8,9},{9,8},{10,11... | collective-permute-start | bytes 786440 | tf_op jit(solution)/shard_map/ppermute | solution.py:538
  85.2 39.1 %copy-start = (bf16[2048,512]{1,0:T(8,128)(2,1)S(1)}, bf16[2048,512]{1,0:T(8,128)(2,1)}, u32[]{:S(2)}) copy-start(bf16[2048,512]{1,0:T(8,128)(2,1)} %w_two_ref.1) | copy-start | bytes 6291460
  121.5 7.0 %collective-permute-start.6 = (bf16[64,9,16,128]{3,2,1,0:T(8,128)(2,1)S(1)}, bf16[64,9,16,128]{3,2,1,0:T(8,128)(2,1)S(1)}, u32[]{:S(2)}, u32[]{:S(2)}) collective-permute-start(bf16[64,9,16,128]{3,2,1,0:T(8,128)(2,1)S(1)} %all_to_all.16.in_ref.mine_ref), channel_id=1, source_target_pairs={{0,1},{1,0},{2,3},{3,2},{4,5},{5,4},{6,7},{7,6},{8,9},{9,8},{10,11... | collective-permute-start | bytes 7077896 | tf_op jit(solution)/shard_map/ppermute | solution.py:538

commit v6 on v5

--- a/solution.py
+++ b/solution.py
@@ -61,8 +61,8 @@
     return pl.ds(pl.multiple_of(k * STRIP, 16), STRIP)
 
 
-def take_strips(core, refs, strips_ref):
-    for ref, k in zip(refs, (0, 1, 2 + core, 3 - core)):
+def take_strips(core, odd, refs, strips_ref):
+    for ref, k in zip(refs, (2 + core, 1 - odd, odd, 3 - core)):
         strips_ref[strip_at(k), :] = ref[...]
 
 
@@ -74,7 +74,7 @@
     return pl.ds((i * pitch + j) * 8 + h * 4 + cb, 8, stride=8)
 
 
-def route_kernel(core_ref, row_far, obs_far, out_ref, row_ref, obs_ref, sem):
+def route_kernel(core_ref, odd_ref, row_far, obs_far, out_ref, row_ref, obs_ref, sem):
     fetch_row, fetch_obs = start(sem, (row_far, row_ref), (obs_far, obs_ref))
     fetch_row.wait()
     row = row_ref[...]
@@ -95,49 +95,62 @@
     out_ref[...] = jnp.where(first, moved[:, :LANE], moved[:, LANE:]).astype(BF16)
 
 
-def shelf(width, slots, hidden, channels):
-    rows = (CELLS, 4 * STRIP, width + 80, hidden)
-    lanes = (slots, CELLS, channels, channels)
+def shelf(width, slots, channels):
+    rows = (CELLS, 4 * STRIP, width + 80)
+    lanes = (slots, CELLS, channels)
     ends = [sum(rows[: k + 1]) for k in range(len(rows))]
     return [(pl.ds(e - r, r), pl.ds(0, n)) for e, r, n in zip(ends, rows, lanes)]
 
 
 def prepare_kernel(
-    interp_ref, pick_ref, w_embed_ref, dw_ref, gain_ref, w_two_far, shelf_far,
-    weights_ref, small_ref, near_ref, w_two_ref, sem,
+    spin_ref, interp_far, w_embed_far, dw_far, gain_far, w_two_far, cot_far, shelf_far, d_act_far,
+    interp_ref, w_embed_ref, dw_ref, gain_ref, w_two_ref, cot_ref, d_act_ref, weights_ref, pick_ref, small_ref, near_ref, sem,
 ):
     tiles, slots = interp_ref.shape[:2]
     width, channels = w_embed_ref.shape
-    spots = shelf(width, tiles * slots, w_two_far.shape[0], channels)
-    fetch = pltpu.make_async_copy(w_two_far, w_two_ref, sem.at[4])
-    fetch.start()
-    moves = [
-        pltpu.make_async_copy(a, shelf_far.at[spot], sem.at[k])
-        for k, (a, spot) in enumerate(zip((weights_ref, pick_ref, near_ref, w_two_ref), spots))
-    ]
-    moves[1].start()
+    spots = shelf(width, tiles * slots, channels)
+    fetches = start(
+        sem, (w_two_far, w_two_ref), (interp_far, interp_ref), (w_embed_far, w_embed_ref), (dw_far, dw_ref),
+        (gain_far, gain_ref), (cot_far, cot_ref),
+    )
+    put_weights, put_pick, put_near = (
+        pltpu.make_async_copy(a, shelf_far.at[spot], sem.at[6 + k])
+        for k, (a, spot) in enumerate(zip((weights_ref, pick_ref, near_ref), spots))
+    )
+    q = lax.broadcasted_iota(jnp.int32, (1, CELLS), 1)
+    by_row, by_col = leaving_strips(spin_ref[0], q // SIDE, q % SIDE)
+    k = lax.broadcasted_iota(jnp.int32, pick_ref.shape, 0)
+    pick_ref[...] = jnp.where((k == by_row) | (k == by_col), 1.0, 0.0).astype(BF16)
+    put_pick.start()
+    for fetch in fetches:
+        fetch.wait()
+    puts = []
+    for k in range(0, w_two_ref.shape[0], 2 * STEP):
+        some = pl.ds(k, 2 * STEP)
+        d_act_ref[:, some] = dot(cot_ref[...], w_two_ref[some, :], NT)
+        target = d_act_far.at[pl.ds(0, CELLS), some]
+        puts.append(pltpu.make_async_copy(d_act_ref.at[:, some], target, sem.at[9 + len(puts)]))
+        puts[-1].start()
     small_ref[...] = jnp.zeros_like(small_ref)
     small_ref[0 : TAPS * TAPS] = dw_ref[...].astype(F32)
-    small_ref[64:] = jnp.broadcast_to(gain_ref[...].astype(F32), (16, channels))
+    small_ref[64:] = jnp.broadcast_to(gain_ref[...], (16, channels))
     near_ref[0:width] = w_embed_ref[...]
     near_ref[width:] = small_ref[...].astype(BF16)
-    moves[2].start()
+    put_near.start()
     weights = interp_ref[...].astype(F32)
     for k in range(slots):
         weights_ref[:, k * tiles : (k + 1) * tiles] = weights[:, k, :].T.astype(BF16)
-    moves[0].start()
-    fetch.wait()
-    moves[3].start()
-    for move in moves:
-        move.wait()
+    put_weights.start()
+    for put in [put_pick, put_near, put_weights] + puts:
+        put.wait()
 
 
 def embed_kernel(
-    core_ref, got_ref, shelf_far, grid_ref, emb_ref, near_ref, up_ref, down_ref, far_ref, by_ref,
+    core_ref, odd_ref, got_ref, shelf_far, grid_ref, emb_ref, near_ref, far_ref, one_ref, two_ref, by_ref,
     wide_ref, rows_ref, weights_ref, pick_ref, strips_ref, sem,
 ):
     width, channels = near_ref.shape[0] - 80, near_ref.shape[1]
-    spots = shelf(width, weights_ref.shape[1], 0, channels)
+    spots = shelf(width, weights_ref.shape[1], channels)
     targets = (weights_ref, pick_ref, near_ref)
     fetches = start(sem, *((shelf_far.at[spot], b) for spot, b in zip(spots, targets)))
     wide_ref[...] = got_ref[...].astype(F32)
@@ -156,8 +169,8 @@
     gridded = dot(weights_ref[...], rows_ref[...]).astype(BF16)
     grid_ref[...] = gridded
     strips_ref[...] = dot(pick_ref[...], gridded).astype(BF16)
-    core = core_ref[0]
-    for ref, k in ((up_ref, 0), (down_ref, 1), (far_ref, 3 - core), (by_ref, 2 + core)):
+    core, odd = core_ref[0], odd_ref[0]
+    for ref, k in ((far_ref, 3 - core), (one_ref, odd), (two_ref, 1 - odd), (by_ref, 2 + core)):
         ref[...] = strips_ref[strip_at(k), :]
     emb_ref[...] = dot(gridded, near_ref[0:width]).astype(BF16)
 
@@ -172,11 +185,10 @@
 
 
 def inner_kernel(
-    emb_ref, near_ref, shelf_far, cot_ref, field_ref, conv_ref, kern_ref, d_act_ref, w_two_ref, sem
-):
-    width, channels = near_ref.shape[0] - 80, near_ref.shape[1]
-    spot = shelf(width, 0, w_two_ref.shape[0], channels)[3]
-    (fetch,) = start(sem, (shelf_far.at[spot], w_two_ref))
+    emb_ref, near_ref, d_act_far, field_ref, conv_ref, kern_ref, d_act_ref, sem
+):
+    width = near_ref.shape[0] - 80
+    (fetch,) = start(sem, (d_act_far.at[pl.ds(0, CELLS), :], d_act_ref))
     taps = near_ref[width : width + 64].astype(F32)
     last = TAPS * TAPS - 1
     for h in range(2):
@@ -195,11 +207,7 @@
                     field_ref[comb(x, HALO + g, PITCH, 0, cb), :] = value
                 if x >= HALF:
                     field_ref[comb(x - HALF, HALO + g, PITCH, 1, cb), :] = value
-    fetch.wait()
-    step = d_act_ref.shape[1] // HALF
     for i in range(HALF):
-        some = pl.ds(i * step, step)
-        d_act_ref[:, some] = dot(cot_ref[...], w_two_ref[some, :], NT)
         sums = [jnp.zeros((8, LANE), F32)] * SIDE
         for x in range(max(i, HALO), min(i + TAPS, HALF + HALO)):
             taps = [kern_ref[block(x - i, b, TAPS), :] for b in range(TAPS)]
@@ -210,6 +218,7 @@
                         sums[y - b] = sums[y - b] + here * taps[b]
         for j in range(SIDE):
             conv_ref[block(i, j, SIDE), :] = sums[j]
+    fetch.wait()
 
 
 OUTER = (0, 1, 2, 19, 20, 21)
@@ -231,12 +240,12 @@
 
 
 def forward_kernel(
-    core_ref, s0, s1, s2, s3, place_ref, near_ref, w_one_ref, own_ref, part_ref, kern_ref, d_act_ref, cot_ref,
+    core_ref, odd_ref, s0, s1, s2, s3, place_ref, near_ref, w_one_ref, own_ref, part_ref, kern_ref, d_act_ref, cot_ref,
     field_ref, normal_ref, inv_ref, scaled_ref, active_ref, d_hid_ref, theirs_ref,
     strips_ref, ring_ref, conv_ref,
 ):
     width, channels = near_ref.shape[0] - 80, near_ref.shape[1]
-    take_strips(core_ref[0], (s0, s1, s2, s3), strips_ref)
+    take_strips(core_ref[0], odd_ref[0], (s0, s1, s2, s3), strips_ref)
     halo = dot(strips_ref[...], near_ref[0:width]).astype(BF16)
     ring_ref[...] = dot(place_ref[...], halo)
     field_ref[...] = own_ref[...]
@@ -284,11 +293,11 @@
     for k in range(w_one_ref.shape[1] // STEP):
         some = pl.ds(k * STEP, STEP)
         pre = dot(scaled_ref[...], w_one_ref[:, some])
-        square = pre * pre
-        tanh = jnp.tanh(pre * (ROOT + (ROOT * CUBE) * square))
-        upper = 0.5 + 0.5 * tanh
-        slope = upper + (0.5 * pre) * (1.0 - tanh * tanh) * (ROOT + (3.0 * ROOT * CUBE) * square)
-        active_ref[:, some] = (pre * upper).astype(BF16)
+        cubic = (ROOT * CUBE) * (pre * pre)
+        upper = 0.5 + 0.5 * jnp.tanh(pre * (ROOT + cubic))
+        active = pre * upper
+        slope = upper + active * (1.0 - upper) * (2.0 * ROOT + 6.0 * cubic)
+        active_ref[:, some] = active.astype(BF16)
         d_hid_ref[:, some] = (d_act_ref[:, some] * slope).astype(BF16)
 
     half = w_one_ref.shape[1] // 2
@@ -300,7 +309,7 @@
 
 
 def backward_kernel(
-    core_ref, grid_ref, s0, s1, s2, s3, place_ref, field_ref, normal_ref, inv_ref, d_hid_ref, w_one_ref,
+    core_ref, odd_ref, grid_ref, s0, s1, s2, s3, place_ref, field_ref, normal_ref, inv_ref, d_hid_ref, w_one_ref,
     near_ref, kern_ref, cot_ref,
     mine_ref, theirs_ref,
     d_scaled_ref, d_conv_ref, spread_ref, own_ref, ring_ref, taps_ref, strips_ref, small_ref,
@@ -362,7 +371,7 @@
         for i in range(SIDE):
             for g in range(0, SIDE, 8):
                 own_ref[pl.ds(i * SIDE + g, 8), lanes] = part(i + HALO, g + HALO, cb)
-    take_strips(core_ref[0], (s0, s1, s2, s3), strips_ref)
+    take_strips(core_ref[0], odd_ref[0], (s0, s1, s2, s3), strips_ref)
     d_halo = dot(place_ref[...], ring_ref[...].astype(BF16), TN).astype(BF16)
     d_own = (own_ref[...] + cot_ref[...].astype(F32)).astype(BF16)
     grad_embed = dot(grid_ref[...], d_own, TN) + dot(strips_ref[...], d_halo, TN)
@@ -461,7 +470,6 @@
     one_ref, two_ref, rows_ref, embed_ref, taps_ref, gain_ref, sem,
 ):
     core = core_ref[0]
-    puts = assemble_half(1 - core, in_ref, one_far, two_far, one_ref, two_ref, sem)
     count = taps_ref.shape[0]
 
     def place(first, last):
@@ -485,10 +493,12 @@
             taps_ref[pl.ds(g, 8), lanes] = rows_ref[pl.ds(g * 4 + cb, 8, stride=4), :]
         taps_ref[pl.ds(count - 1, 1), lanes] = rows_ref[pl.ds((count - 1) * 4 + cb, 1), :]
         gain_ref[:, lanes] = rows_ref[pl.ds(count * 4 + cb, 1), :]
-    base = len(puts)
+    base = 2 * one_ref.shape[0]
+    puts = []
     for k, pair in enumerate(((embed_ref, embed_far), (taps_ref, taps_far), (gain_ref, gain_far))):
         puts.append(pltpu.make_async_copy(*pair, sem.at[base + k]))
         puts[-1].start()
+    puts += assemble_half(1 - core, in_ref, one_far, two_far, one_ref, two_ref, sem)
     for put in puts:
         put.wait()
 
@@ -499,7 +509,15 @@
     return row, col
 
 
-def selectors(spin):
+def leaving_strips(spin, x, y):
+    row, col = turned(spin, x, y, SIDE - 1)
+    cut = SIDE - HALO
+    by_row = jnp.where(row >= cut, (row - cut) * SIDE + col, jnp.where(row < HALO, STRIP + row * SIDE + col, -1))
+    by_col = jnp.where(col >= cut, 2 * STRIP + (col - cut) * SIDE + row, jnp.where(col < HALO, 3 * STRIP + col * SIDE + row, -1))
+    return by_row, by_col
+
+
+def arriving_strips(spin):
     x = jnp.asarray([x for _, x, _ in ring() for _ in range(8)], jnp.int32)
     y = jnp.asarray([y + k for _, _, y in ring() for k in range(8)], jnp.int32)
     row, col = turned(spin, x, y, FULL - 1)
@@ -515,23 +533,17 @@
     k = jnp.arange(4 * STRIP, dtype=jnp.int32)
     place = (strip[:, None] == k[None]).astype(BF16)
 
-    q = jnp.arange(CELLS, dtype=jnp.int32)
-    row, col = turned(spin, q // SIDE, q % SIDE, SIDE - 1)
-    cut = SIDE - HALO
-    by_row = jnp.where(row >= cut, (row - cut) * SIDE + col, jnp.where(row < HALO, STRIP + row * SIDE + col, -1))
-    by_col = jnp.where(col >= cut, 2 * STRIP + (col - cut) * SIDE + row, jnp.where(col < HALO, 3 * STRIP + col * SIDE + row, -1))
-    pick = ((k[:, None] == by_row[None]) | (k[:, None] == by_col[None])).astype(BF16)
-    return place, pick
-
-
-def exchange(up, down, far, by):
+    return place
+
+
+def exchange(far, one, two, by):
+    def between(value, axes, first):
+        size = lax.axis_size(axes)
+        pairs = [(i, (i + 1) % size) for i in range(first, size, 2)]
+        return lax.ppermute(value, axes, pairs + [(j, i) for i, j in pairs])
+
     beside = ("col", "core")
-    tiles, faces = lax.axis_size(beside), lax.axis_size("face")
-    pairs = [(i, (i + 1) % tiles) for i in range(1, tiles, 2)]
-    far = lax.ppermute(far, beside, pairs + [(j, i) for i, j in pairs])
-    up = lax.ppermute(up, "face", [(i, (i + 1) % faces) for i in range(faces)])
-    down = lax.ppermute(down, "face", [((i + 1) % faces, i) for i in range(faces)])
-    return up, down, far, swap(by)
+    return between(far, beside, 1), between(one, "face", 0), between(two, "face", 1), between(by, beside, 0)
 
 
 def swap(value):
@@ -545,26 +557,42 @@
     width, channels = w_embed.shape
     hidden = w_one.shape[1]
     slots = interp.shape[2]
-    core = lax.axis_index("core").reshape(1)
-    place, pick = selectors(tile_spin[0, 0])
+    core, odd = lax.axis_index("core").reshape(1), (lax.axis_index("face") % 2).reshape(1)
+    place = arriving_strips(tile_spin[0, 0])
     (leaving,) = call(
         route_kernel,
         [((tiles * 8, LANE), BF16)],
         [((1, obs_values.shape[0]), jnp.int32), (obs_values.shape, BF16)],
-        60.5, core, obs_tile.reshape(1, -1), obs_values, far=(1, 2), copies=2,
+        60.5, core, odd, obs_tile.reshape(1, -1), obs_values, far=(2, 3), copies=2,
     )
     arrived = lax.all_to_all(leaving.reshape(tiles, 8, LANE), ALL, 0, 0, tiled=True)
     stacked = ((CELLS, tiles * slots), BF16)
     near = ((width + 80, channels), BF16)
-    (shelved,) = call(
-        prepare_kernel, [((SHELF, channels), BF16)], [stacked, ((80, channels), F32), near, (w_two.shape, BF16)],
-        60.5, interp[0], pick, w_embed, dw_kernel, norm_gain[None], w_two, far=(5,), far_outs=(0,), copies=5,
+    picks = ((4 * STRIP, CELLS), BF16)
+    shelved, d_active = call(
+        prepare_kernel,
+        [((SHELF, channels), BF16), ((SHELF // 8, hidden), F32)],
+        [
+            (interp.shape[1:], BF16),
+            (w_embed.shape, BF16),
+            (dw_kernel.shape, BF16),
+            ((1, channels), F32),
+            (w_two.shape, BF16),
+            (cotangent.shape, BF16),
+            ((CELLS, hidden), F32),
+            stacked,
+            picks,
+            ((80, channels), F32),
+            near,
+        ],
+        60.5, tile_spin.reshape(1), interp[0], w_embed, dw_kernel, norm_gain.astype(F32)[None], w_two, cotangent,
+        far=(1, 2, 3, 4, 5, 6), far_outs=(0, 1), copies=9 + hidden // (2 * STEP),
     )
     gridded, embedded, nearby, *strips = call(
         embed_kernel,
         [((CELLS, width), BF16), ((CELLS, channels), BF16), near] + [((STRIP, width), BF16)] * 4,
-        [((tiles * 8, LANE), F32), ((tiles * slots, width), BF16), stacked, (pick.shape, BF16), ((4 * STRIP, width), BF16)],
-        16, core, arrived.reshape(tiles * 8, LANE), shelved, far=(2,), copies=3,
+        [((tiles * 8, LANE), F32), ((tiles * slots, width), BF16), stacked, picks, ((4 * STRIP, width), BF16)],
+        16, core, odd, arrived.reshape(tiles * 8, LANE), shelved, far=(3,), copies=3,
     )
     strips = exchange(*strips)
     cells2 = ((ROWS2 * PITCH * 8, LANE), F32)
@@ -573,8 +601,8 @@
     around = ((RING, channels), F32)
     step_sums = [((STEP, channels), F32), ((channels, STEP), F32)]
     field, conv, taps, d_active = call(
-        inner_kernel, [cells2, blocks, kernel, ((CELLS, hidden), F32)], [((hidden, channels), BF16)], 20,
-        embedded, nearby, shelved, cotangent, far=(2,), copies=1,
+        inner_kernel, [cells2, blocks, kernel, ((CELLS, hidden), F32)], [], 20,
+        embedded, nearby, d_active, far=(2,), copies=1,
     )
     field, normal, inverse, scaled, active, d_hidden, theirs = call(
         forward_kernel,
@@ -589,7 +617,7 @@
         ],
         [((4 * STRIP, width), BF16), around, blocks],
         20,
-        core, *strips, place, nearby, w_one, field, conv, taps, d_active, cotangent,
+        core, odd, *strips, place, nearby, w_one, field, conv, taps, d_active, cotangent,
     )
     big = swap(theirs)
 
@@ -598,7 +626,7 @@
         [((chips, 16, LANE), F32), ((chips, 16, LANE), BF16)],
         [cells, blocks, cells2, cells, around, kernel, ((4 * STRIP, width), BF16), ((2 * chips * 16, LANE), F32)],
         20,
-        core, gridded, *strips, place, field, normal, inverse, d_hidden, w_one, nearby, taps, cotangent,
+        core, odd, gridded, *strips, place, field, normal, inverse, d_hidden, w_one, nearby, taps, cotangent,
     )
     small = swap(theirs)
     whole = ((chips, 9, 16, LANE), BF16)

time: 131 us -> 130 us (level)
  Pallas kernels: 26.7 us -> 24.9 us
  waiting for transfers between devices: 5.19 us -> 6.61 us
    pallas_call x11, Pallas kernels: 26.7 us -> 24.9 us  [call(): pl.pallas_call(kernel, out_shape=[jax.ShapeDtypeStruct(s, d) for s, d in...]
    all_to_all x1, waiting for transfers between devices: 3.67 us -> 4.98 us  [on_device(): lax.all_to_all(leaving.reshape(tiles, 8, LANE), ALL, 0, 0, tiled=True)]
    ppermute x3 -> x4, starting transfers between devices: 5.8 us -> 4.88 us  [between(): return lax.ppermute(value, axes, pairs + [(j, i) for i, j in pairs])]
    ppermute x4 -> x3, starting transfers between devices: 5.5 us -> 5.27 us  [swap(): return lax.ppermute(value, 'core', [(0, 1), (1, 0)])]
  transfers between devices with their start and end apart: 8 -> 8, of which waited for: 3 -> 4; matrix products, arithmetic and copies ran while one was open for 2% -> 1% of each run, Pallas kernels for 13% -> 12%
where the time goes in v6:
time: 130 us
  blocking collectives  73 us (56%)
  Pallas kernels  24.9 us (19%)
  starting transfers between devices  21.7 us (17%)
  waiting for transfers between devices  6.61 us (5%)
  between operations  1.69 us (1%)
  other arithmetic  1.4 us (1%)
    all_to_all x1, blocking collectives, on_device(): paired = lax.all_to_all(paired, CHIPS, 0, 0, tiled=True)  36.8 us
    all_to_all x1, blocking collectives, on_device(): here = lax.all_to_all(summed, CHIPS, 0, 0, tiled=True)  36.2 us
    pallas_call x11, Pallas kernels, call(): pl.pallas_call(kernel, out_shape=[jax.ShapeDtypeStruct(s, d) for s, d in...  24.9 us
    all_to_all x1, starting transfers between devices, on_device(): lax.all_to_all(leaving.reshape(tiles, 8, LANE), ALL, 0, 0, tiled=True)  11.5 us
    ppermute x3, starting transfers between devices, swap(): return lax.ppermute(value, 'core', [(0, 1), (1, 0)])  5.27 us
    all_to_all x1, waiting for transfers between devices, on_device(): lax.all_to_all(leaving.reshape(tiles, 8, LANE), ALL, 0, 0, tiled=True)  4.98 us
    ppermute x4, starting transfers between devices, between(): return lax.ppermute(value, axes, pairs + [(j, i) for i, j in pairs])  4.88 us
  transfers between devices with their start and end apart: 8, of which 4 were waited for; matrix products, arithmetic and copies ran while one was open for 1% of the time, Pallas kernels for 12%

profile of v6, /device:TPU:1, one launch (start us, length us, event | category | flops | bytes accessed | tf_op | source)
XLA Modules:
  0.0 129.6 jit_solution(2535852559809904158)
XLA Ops:
  0.7 1.9 %shard_map.163 = bf16[1024,128]{1,0:T(8,128)(2,1)} custom-call(s32[1]{0:T(128)} %bitcast.core_ref, s32[1]{0:T(128)} %bitcast.1.odd_ref, s32[1,256]{1,0:T(1,128)} %bitcast.17, bf16[256,256]{1,0:T(8,128)(2,1)} %obs_far.1), custom_call_target="tpu_custom_call" | custom-call | tf_op jit(solution)/shard_map/pallas_call | solution.py:39
  2.7 11.5 %all-to-all-start = ((bf16[128,8,128]{2,1,0:T(8,128)(2,1)}), bf16[128,8,128]{2,1,0:T(8,128)(2,1)S(1)}, u32[]{:S(2)}, u32[]{:S(2)}) async-start(bf16[128,8,128]{2,1,0:T(8,128)(2,1)} %bitcast.14), calls=%async_computation | async-start | bytes 524288 | tf_op jit(solution)/shard_map/all_to_all | solution.py:568
  14.8 1.3 broadcast_in_dim.15
  16.1 3.8 %shard_map.164 = (bf16[65536,512]{1,0:T(8,128)(2,1)}, f32[8192,2048]{1,0:T(8,128)}) custom-call(s32[1]{0:T(128)} %bitcast.12.spin_ref, bf16[128,4,256]{2,1,0:T(4,128)(2,1)} %bitcast.15, bf16[256,512]{1,0:T(8,128)(2,1)} %w_embed_far.1, bf16[49,512]{1,0:T(8,128)(2,1)} %dw_far.1, f32[1,512]{1,0:T(1,128)} %bitcast.16, bf16[2048,512]{1,0:T(8,128)(2,1)} %w_two_ref.1, ...), custom_call_target="tpu_custom_call" | custom-call | tf_op jit(solution)/shard_map/pallas_call | solution.py:39
  19.9 5.0 %all-to-all-done = bf16[128,8,128]{2,1,0:T(8,128)(2,1)S(1)} async-done(((bf16[128,8,128]{2,1,0:T(8,128)(2,1)}), bf16[128,8,128]{2,1,0:T(8,128)(2,1)S(1)}, u32[]{:S(2)}, u32[]{:S(2)}) %all-to-all-start) | async-done | bytes 262176 | tf_op jit(solution)/shard_map/all_to_all | solution.py:568
  24.9 1.7 %shard_map.165 = (bf16[256,256]{1,0:T(8,128)(2,1)S(1)}, bf16[256,512]{1,0:T(8,128)(2,1)S(1)}, bf16[336,512]{1,0:T(8,128)(2,1)S(1)}, bf16[48,256]{1,0:T(8,128)(2,...) custom-call(s32[1]{0:T(128)} %bitcast.core_ref, s32[1]{0:T(128)} %bitcast.1.odd_ref, ...), custom_call_target="tpu_custom_call" | custom-call | tf_op jit(solution)/shard_map/pallas_call | solution.py:39
  26.6 1.7 %collective-permute-start = (bf16[48,256]{1,0:T(8,128)(2,1)S(1)}, bf16[48,256]{1,0:T(8,128)(2,1)S(1)}, u32[]{:S(2)}, u32[]{:S(2)}) collective-permute-start(bf16[48,256]{1,0:T(8,128)(2,1)S(1)} %get-tuple-element.38), channel_id=1, source_target_pairs={{1,2},{3,4},{5,6},{7,8},{9,10},{11,12},{13,14},{15,0},{2,1},{4,3},... | collective-permute-start | bytes 73736 | tf_op jit(solution)/shard_map/ppermute | solution.py:543
  28.3 0.3 collective-permute-start.1
  28.6 0.8 collective-permute-start.2
  29.5 2.0 %collective-permute-start.3 = (bf16[48,256]{1,0:T(8,128)(2,1)S(1)}, bf16[48,256]{1,0:T(8,128)(2,1)S(1)}, u32[]{:S(2)}, u32[]{:S(2)}) collective-permute-start(bf16[48,256]{1,0:T(8,128)(2,1)S(1)} %get-tuple-element.41), channel_id=1, source_target_pairs={{0,1},{2,3},{4,5},{6,7},{8,9},{10,11},{12,13},{14,15},{1,0},{3,2},... | collective-permute-start | bytes 73736 | tf_op jit(solution)/shard_map/ppermute | solution.py:543
  31.7 1.8 %shard_map.166 = (f32[2688,128]{1,0:T(8,128)S(1)}, f32[1024,128]{1,0:T(8,128)S(1)}, f32[392,128]{1,0:T(8,128)S(1)}, f32[256,2048]{1,0:T(8,128)S(1)}) custom-call(bf16[256,512]{1,0:T(8,128)(2,1)S(1)} %get-tuple-element.43.emb_ref, bf16[336,512]{1,0:T(8,128)(2,1)S(1)} %get-tuple-element.42.near_ref, f32[8192,2048]{1,0:T(8,128)} %get-tuple-element.44.d_act_far), custom_call_target="tpu_custom_call" | custom-call | tf_op jit(solution)/shard_map/pallas_call | solution.py:39
  33.6 0.3 copy-done.1
  33.9 2.8 %shard_map.167 = (f32[2688,128]{1,0:T(8,128)S(1)}, f32[256,512]{1,0:T(8,128)S(1)}, f32[256,128]{1,0:T(8,128)S(1)}, bf16[256,512]{1,0:T(8,128)(2,1)S(1)}, bf16[25...) custom-call(s32[1]{0:T(128)} %bitcast.core_ref, s32[1]{0:T(128)} %bitcast.1.odd_ref, ...), custom_call_target="tpu_custom_call" | custom-call | tf_op jit(solution)/shard_map/pallas_call | solution.py:39
  36.7 2.3 %collective-permute-start.5 = (bf16[256,3072]{1,0:T(8,128)(2,1)S(1)}, bf16[256,3072]{1,0:T(8,128)(2,1)S(1)}, u32[]{:S(2)}, u32[]{:S(2)}) collective-permute-start(bf16[256,3072]{1,0:T(8,128)(2,1)S(1)} %get-tuple-element.57), channel_id=1, source_target_pairs={{0,1},{1,0},{2,3},{3,2},{4,5},{5,4},{6,7},{7,6},{8,9},{9,8},{10,11... | collective-permute-start | bytes 4718600 | tf_op jit(solution)/shard_map/ppermute | solution.py:550
  39.0 5.3 %shard_map.168 = (f32[64,16,128]{2,1,0:T(8,128)S(1)}, bf16[64,16,128]{2,1,0:T(8,128)(2,1)S(1)}) custom-call(s32[1]{0:T(128)} %bitcast.core_ref, s32[1]{0:T(128)} %bitcast.1.odd_ref, bf16[256,256]{1,0:T(8,128)(2,1)S(1)} %get-tuple-element.37.grid_ref, bf16[48,256]{1,0:T(8,128)(2,1)S(1)} %collective-permute-done.s0, ...), custom_call_target="tpu_custom_call" | custom-call | tf_op jit(solution)/shard_map/pallas_call | solution.py:39
  44.4 1.3 %shard_map.169.paired_far = bf16[64,9,16,128]{3,2,1,0:T(8,128)(2,1)S(1)} custom-call(s32[1]{0:T(128)} %bitcast.core_ref, bf16[256,512]{1,0:T(8,128)(2,1)S(1)} %get-tuple-element.55.scaled_ref, bf16[256,2048]{1,0:T(8,128)(2,1)S(1)} %get-tuple-element.56.active_ref, bf16[256,2048]{1,0:T(8,128)(2,1)S(1)} %get-tuple-element.52.d_hid_ref, ...), custom_call_target="tpu_custom_call" | custom-call | tf_op jit(solution)/shard_map/pallas_call | solution.py:39
  45.8 0.2 collective-permute-done.4.small_ref
  46.0 36.8 %all_to_all.15.in_ref = bf16[64,9,16,128]{3,2,1,0:T(8,128)(2,1)S(1)} all-to-all(bf16[64,9,16,128]{3,2,1,0:T(8,128)(2,1)S(1)} %shard_map.170), channel_id=1, replica_groups=mesh['face'=8,'col'=8,'core'=2] {'face','col'}, dimensions={0} | all-to-all | bytes 4718592 | tf_op jit(solution)/shard_map/all_to_all | solution.py:640
  82.8 1.0 shard_map.171
  83.9 36.2 %all_to_all.16.in_ref.mine_ref = bf16[64,9,16,128]{3,2,1,0:T(8,128)(2,1)S(1)} all-to-all(bf16[64,9,16,128]{3,2,1,0:T(8,128)(2,1)S(1)} %shard_map.171), channel_id=1, replica_groups=mesh['face'=8,'col'=8,'core'=2] {'face','col'}, dimensions={0} | all-to-all | bytes 4718592 | tf_op jit(solution)/shard_map/all_to_all | solution.py:642
  120.1 2.9 %collective-permute-start.6 = (bf16[64,9,16,128]{3,2,1,0:T(8,128)(2,1)S(1)}, bf16[64,9,16,128]{3,2,1,0:T(8,128)(2,1)S(1)}, u32[]{:S(2)}, u32[]{:S(2)}) collective-permute-start(bf16[64,9,16,128]{3,2,1,0:T(8,128)(2,1)S(1)} %all_to_all.16.in_ref.mine_ref), channel_id=1, source_target_pairs={{0,1},{1,0},{2,3},{3,2},{4,5},{5,4},{6,7},{7,6},{8,9},{9,8},{10,11... | collective-permute-start | bytes 7077896 | tf_op jit(solution)/shard_map/ppermute | solution.py:550
  123.0 2.8 %shard_map.172 = (f32[512,2048]{1,0:T(8,128)}, f32[2048,512]{1,0:T(8,128)}, bf16[256,512]{1,0:T(8,128)(2,1)}) custom-call(s32[1]{0:T(128)} %bitcast.core_ref, bf16[64,9,16,128]{3,2,1,0:T(8,128)(2,1)S(1)} %all_to_all.16.in_ref.mine_ref, bf16[256,512]{1,0:T(8,128)(2,1)S(1)} %get-tuple-element.43.emb_ref, bf16[256,2048]{1,0:T(8,128)(2,1)S(1)} %get-tuple-element.56.active_ref, ...), custom_call_target="tpu_custom_call" | custom-call | tf_op jit(solution)/shard_map/pallas_call | solution.py:39
  125.8 1.3 %collective-permute-done.6.in_ref = bf16[64,9,16,128]{3,2,1,0:T(8,128)(2,1)S(1)} collective-permute-done((bf16[64,9,16,128]{3,2,1,0:T(8,128)(2,1)S(1)}, bf16[64,9,16,128]{3,2,1,0:T(8,128)(2,1)S(1)}, u32[]{:S(2)}, u32[]{:S(2)}) %collective-permute-start.6) | collective-permute-done | bytes 2359328 | tf_op jit(solution)/shard_map/ppermute | solution.py:550
  127.1 2.4 %shard_map.173 = (f32[512,2048]{1,0:T(8,128)}, f32[2048,512]{1,0:T(8,128)}, f32[256,512]{1,0:T(8,128)}, f32[49,512]{1,0:T(8,128)}, f32[1,512]{1,0:T(1,128)}) custom-call(s32[1]{0:T(128)} %bitcast.core_ref, bf16[64,9,16,128]{3,2,1,0:T(8,128)(2,1)S(1)} %collective-permute-done.6.in_ref, ...), custom_call_target="tpu_custom_call", output_to_operand_aliasing={{0}: (3, {}), {1}: (4, {})} | custom-call | tf_op jit(solution)/shard_map/pallas_call | solution.py:39
  (24 shorter events, 0.5 us)
Async XLA Ops:
  0.6 19.2 %copy-start.3 = (s32[400]{0:T(512)S(1)}, s32[400]{0:T(512)}, u32[]{:S(2)}) copy-start(s32[400]{0:T(512)} %constant.61.clone) | copy-start | bytes 4804
  0.6 19.2 %copy-start.4 = (s32[400]{0:T(512)S(1)}, s32[400]{0:T(512)}, u32[]{:S(2)}) copy-start(s32[400]{0:T(512)} %constant.62.clone) | copy-start | bytes 4804
  0.7 19.2 %copy-start.7 = (pred[400]{0:T(512)(128)(4,1)S(1)}, pred[400]{0:T(512)(128)(4,1)}, u32[]{:S(2)}) copy-start(pred[400]{0:T(512)(128)(4,1)} %constant.65) | copy-start | bytes 1204
  0.7 19.2 %copy-start.5 = (s32[400]{0:T(512)S(1)}, s32[400]{0:T(512)}, u32[]{:S(2)}) copy-start(s32[400]{0:T(512)} %constant.67) | copy-start | bytes 4804
  0.7 19.2 %copy-start.6 = (s32[400]{0:T(512)S(1)}, s32[400]{0:T(512)}, u32[]{:S(2)}) copy-start(s32[400]{0:T(512)} %constant.69) | copy-start | bytes 4804
  2.7 22.3 %all-to-all-start = ((bf16[128,8,128]{2,1,0:T(8,128)(2,1)}), bf16[128,8,128]{2,1,0:T(8,128)(2,1)S(1)}, u32[]{:S(2)}, u32[]{:S(2)}) async-start(bf16[128,8,128]{2,1,0:T(8,128)(2,1)} %bitcast.14), calls=%async_computation | async-start | bytes 524288 | tf_op jit(solution)/shard_map/all_to_all | solution.py:568
  26.6 6.8 %collective-permute-start = (bf16[48,256]{1,0:T(8,128)(2,1)S(1)}, bf16[48,256]{1,0:T(8,128)(2,1)S(1)}, u32[]{:S(2)}, u32[]{:S(2)}) collective-permute-start(bf16[48,256]{1,0:T(8,128)(2,1)S(1)} %get-tuple-element.38), channel_id=1, source_target_pairs={{1,2},{3,4},{5,6},{7,8},{9,10},{11,12},{13,14},{15,0},{2,1},{4,3},... | collective-permute-start | bytes 73736 | tf_op jit(solution)/shard_map/ppermute | solution.py:543
  28.3 5.1 %collective-permute-start.1 = (bf16[48,256]{1,0:T(8,128)(2,1)S(1)}, bf16[48,256]{1,0:T(8,128)(2,1)S(1)}, u32[]{:S(2)}, u32[]{:S(2)}) collective-permute-start(bf16[48,256]{1,0:T(8,128)(2,1)S(1)} %get-tuple-element.39), channel_id=1, source_target_pairs={{0,16},{32,48},{64,80},{96,112},{16,0},{48,32},{80,64},{112,96},{1... | collective-permute-start | bytes 73736 | tf_op jit(solution)/shard_map/ppermute | solution.py:543
  28.6 4.9 %collective-permute-start.2 = (bf16[48,256]{1,0:T(8,128)(2,1)S(1)}, bf16[48,256]{1,0:T(8,128)(2,1)S(1)}, u32[]{:S(2)}, u32[]{:S(2)}) collective-permute-start(bf16[48,256]{1,0:T(8,128)(2,1)S(1)} %get-tuple-element.40), channel_id=1, source_target_pairs={{16,32},{48,64},{80,96},{112,0},{32,16},{64,48},{96,80},{0,112},{1... | collective-permute-start | bytes 73736 | tf_op jit(solution)/shard_map/ppermute | solution.py:543
  29.5 4.1 %collective-permute-start.3 = (bf16[48,256]{1,0:T(8,128)(2,1)S(1)}, bf16[48,256]{1,0:T(8,128)(2,1)S(1)}, u32[]{:S(2)}, u32[]{:S(2)}) collective-permute-start(bf16[48,256]{1,0:T(8,128)(2,1)S(1)} %get-tuple-element.41), channel_id=1, source_target_pairs={{0,1},{2,3},{4,5},{6,7},{8,9},{10,11},{12,13},{14,15},{1,0},{3,2},... | collective-permute-start | bytes 73736 | tf_op jit(solution)/shard_map/ppermute | solution.py:543
  31.6 2.2 %copy-start.1 = (bf16[512,2048]{1,0:T(8,128)(2,1)S(1)}, bf16[512,2048]{1,0:T(8,128)(2,1)}, u32[]{:S(2)}) copy-start(bf16[512,2048]{1,0:T(8,128)(2,1)} %w_one_ref.3) | copy-start | bytes 6291460
  31.7 2.2 %copy-start.2 = (bf16[256,512]{1,0:T(8,128)(2,1)S(1)}, bf16[256,512]{1,0:T(8,128)(2,1)}, u32[]{:S(2)}) copy-start(bf16[256,512]{1,0:T(8,128)(2,1)} %cot_ref.5) | copy-start | bytes 786436
  36.7 7.7 %collective-permute-start.5 = (bf16[256,3072]{1,0:T(8,128)(2,1)S(1)}, bf16[256,3072]{1,0:T(8,128)(2,1)S(1)}, u32[]{:S(2)}, u32[]{:S(2)}) collective-permute-start(bf16[256,3072]{1,0:T(8,128)(2,1)S(1)} %get-tuple-element.57), channel_id=1, source_target_pairs={{0,1},{1,0},{2,3},{3,2},{4,5},{5,4},{6,7},{7,6},{8,9},{9,8},{10,11... | collective-permute-start | bytes 4718600 | tf_op jit(solution)/shard_map/ppermute | solution.py:550
  44.3 1.6 %collective-permute-start.4 = (bf16[64,16,128]{2,1,0:T(8,128)(2,1)S(1)}, bf16[64,16,128]{2,1,0:T(8,128)(2,1)S(1)}, u32[]{:S(2)}, u32[]{:S(2)}) collective-permute-start(bf16[64,16,128]{2,1,0:T(8,128)(2,1)S(1)} %get-tuple-element.54), channel_id=1, source_target_pairs={{0,1},{1,0},{2,3},{3,2},{4,5},{5,4},{6,7},{7,6},{8,9},{9,8},{10,11... | collective-permute-start | bytes 786440 | tf_op jit(solution)/shard_map/ppermute | solution.py:550
  83.9 39.1 %copy-start = (bf16[2048,512]{1,0:T(8,128)(2,1)S(1)}, bf16[2048,512]{1,0:T(8,128)(2,1)}, u32[]{:S(2)}) copy-start(bf16[2048,512]{1,0:T(8,128)(2,1)} %w_two_ref.1) | copy-start | bytes 6291460
  120.1 7.0 %collective-permute-start.6 = (bf16[64,9,16,128]{3,2,1,0:T(8,128)(2,1)S(1)}, bf16[64,9,16,128]{3,2,1,0:T(8,128)(2,1)S(1)}, u32[]{:S(2)}, u32[]{:S(2)}) collective-permute-start(bf16[64,9,16,128]{3,2,1,0:T(8,128)(2,1)S(1)} %all_to_all.16.in_ref.mine_ref), channel_id=1, source_target_pairs={{0,1},{1,0},{2,3},{3,2},{4,5},{5,4},{6,7},{7,6},{8,9},{9,8},{10,11... | collective-permute-start | bytes 7077896 | tf_op jit(solution)/shard_map/ppermute | solution.py:550

commit v7 on v6

--- a/solution.py
+++ b/solution.py
@@ -95,63 +95,95 @@
     out_ref[...] = jnp.where(first, moved[:, :LANE], moved[:, LANE:]).astype(BF16)
 
 
+OUTER = (0, 1, 2, 19, 20, 21)
+
+
+def ring():
+    at = 0
+    for x in OUTER:
+        for y in range(0, PITCH, 8):
+            yield at, x, y
+            at += 8
+    for x in range(HALO, SIDE + HALO):
+        for y in (0, PITCH - 8):
+            yield at, x, y
+            at += 8
+
+
+RING = 8 * len(list(ring()))
+
+
 def shelf(width, slots, channels):
-    rows = (CELLS, 4 * STRIP, width + 80)
-    lanes = (slots, CELLS, channels)
+    rows = (CELLS, 4 * STRIP, width + 80, RING)
+    lanes = (slots, CELLS, channels, CELLS)
     ends = [sum(rows[: k + 1]) for k in range(len(rows))]
     return [(pl.ds(e - r, r), pl.ds(0, n)) for e, r, n in zip(ends, rows, lanes)]
 
 
 def prepare_kernel(
     spin_ref, interp_far, w_embed_far, dw_far, gain_far, w_two_far, cot_far, shelf_far, d_act_far,
-    interp_ref, w_embed_ref, dw_ref, gain_ref, w_two_ref, cot_ref, d_act_ref, weights_ref, pick_ref, small_ref, near_ref, sem,
+    interp_ref, w_embed_ref, dw_ref, gain_ref, w_two_ref, cot_ref, d_act_ref, weights_ref, pick_ref, small_ref, near_ref,
+    place_ref, sem,
 ):
     tiles, slots = interp_ref.shape[:2]
     width, channels = w_embed_ref.shape
     spots = shelf(width, tiles * slots, channels)
     fetches = start(
-        sem, (w_two_far, w_two_ref), (interp_far, interp_ref), (w_embed_far, w_embed_ref), (dw_far, dw_ref),
-        (gain_far, gain_ref), (cot_far, cot_ref),
-    )
-    put_weights, put_pick, put_near = (
+        sem, (interp_far, interp_ref), (cot_far, cot_ref), (w_embed_far, w_embed_ref), (dw_far, dw_ref),
+        (gain_far, gain_ref), (w_two_far, w_two_ref),
+    )
+    put_weights, put_pick, put_near, put_place = (
         pltpu.make_async_copy(a, shelf_far.at[spot], sem.at[6 + k])
-        for k, (a, spot) in enumerate(zip((weights_ref, pick_ref, near_ref), spots))
-    )
+        for k, (a, spot) in enumerate(zip((weights_ref, pick_ref, near_ref, place_ref), spots))
+    )
+    spin = spin_ref[0]
     q = lax.broadcasted_iota(jnp.int32, (1, CELLS), 1)
-    by_row, by_col = leaving_strips(spin_ref[0], q // SIDE, q % SIDE)
+    by_row, by_col = leaving_strips(spin, q // SIDE, q % SIDE)
     k = lax.broadcasted_iota(jnp.int32, pick_ref.shape, 0)
     pick_ref[...] = jnp.where((k == by_row) | (k == by_col), 1.0, 0.0).astype(BF16)
     put_pick.start()
-    for fetch in fetches:
+    fetches[0].wait()
+    weights = interp_ref[...].astype(F32)
+    for k in range(slots):
+        weights_ref[:, k * tiles : (k + 1) * tiles] = weights[:, k, :].T.astype(BF16)
+    put_weights.start()
+    p = lax.broadcasted_iota(jnp.int32, (RING, 1), 0)
+    outer = len(OUTER) * PITCH
+    o, r = (p * 171) >> 12, p - outer
+    x = jnp.where(p < outer, jnp.where(o < HALO, o, o + SIDE), HALO + (r >> 4))
+    y = jnp.where(p < outer, p - o * PITCH, (r & 15) + (r & 8))
+    strip = arriving_strips(spin, x, y)
+    k = lax.broadcasted_iota(jnp.int32, place_ref.shape, 1)
+    place_ref[...] = jnp.where(strip == k, 1.0, 0.0).astype(BF16)
+    put_place.start()
+    for fetch in fetches[1:]:
         fetch.wait()
+    small_ref[...] = jnp.zeros_like(small_ref)
+    small_ref[0 : TAPS * TAPS] = dw_ref[...].astype(F32)
+    gain = gain_ref[...].astype(F32)
+    for c in range(channels // LANE):
+        small_ref[64:, c * LANE : (c + 1) * LANE] = jnp.broadcast_to(gain[c : c + 1], (16, LANE))
+    near_ref[0:width] = w_embed_ref[...]
+    near_ref[width:] = small_ref[...].astype(BF16)
+    put_near.start()
     puts = []
     for k in range(0, w_two_ref.shape[0], 2 * STEP):
         some = pl.ds(k, 2 * STEP)
         d_act_ref[:, some] = dot(cot_ref[...], w_two_ref[some, :], NT)
         target = d_act_far.at[pl.ds(0, CELLS), some]
-        puts.append(pltpu.make_async_copy(d_act_ref.at[:, some], target, sem.at[9 + len(puts)]))
+        puts.append(pltpu.make_async_copy(d_act_ref.at[:, some], target, sem.at[10 + len(puts)]))
         puts[-1].start()
-    small_ref[...] = jnp.zeros_like(small_ref)
-    small_ref[0 : TAPS * TAPS] = dw_ref[...].astype(F32)
-    small_ref[64:] = jnp.broadcast_to(gain_ref[...], (16, channels))
-    near_ref[0:width] = w_embed_ref[...]
-    near_ref[width:] = small_ref[...].astype(BF16)
-    put_near.start()
-    weights = interp_ref[...].astype(F32)
-    for k in range(slots):
-        weights_ref[:, k * tiles : (k + 1) * tiles] = weights[:, k, :].T.astype(BF16)
-    put_weights.start()
-    for put in [put_pick, put_near, put_weights] + puts:
+    for put in [put_pick, put_near, put_weights, put_place] + puts:
         put.wait()
 
 
 def embed_kernel(
-    core_ref, odd_ref, got_ref, shelf_far, grid_ref, emb_ref, near_ref, far_ref, one_ref, two_ref, by_ref,
+    core_ref, odd_ref, got_ref, shelf_far, grid_ref, emb_ref, near_ref, place_ref, far_ref, one_ref, two_ref, by_ref,
     wide_ref, rows_ref, weights_ref, pick_ref, strips_ref, sem,
 ):
     width, channels = near_ref.shape[0] - 80, near_ref.shape[1]
     spots = shelf(width, weights_ref.shape[1], channels)
-    targets = (weights_ref, pick_ref, near_ref)
+    targets = (weights_ref, pick_ref, near_ref, place_ref)
     fetches = start(sem, *((shelf_far.at[spot], b) for spot, b in zip(spots, targets)))
     wide_ref[...] = got_ref[...].astype(F32)
     tiles = got_ref.shape[0] // 8
@@ -221,24 +253,6 @@
     fetch.wait()
 
 
-OUTER = (0, 1, 2, 19, 20, 21)
-
-
-def ring():
-    at = 0
-    for x in OUTER:
-        for y in range(0, PITCH, 8):
-            yield at, x, y
-            at += 8
-    for x in range(HALO, SIDE + HALO):
-        for y in (0, PITCH - 8):
-            yield at, x, y
-            at += 8
-
-
-RING = 8 * len(list(ring()))
-
-
 def forward_kernel(
     core_ref, odd_ref, s0, s1, s2, s3, place_ref, near_ref, w_one_ref, own_ref, part_ref, kern_ref, d_act_ref, cot_ref,
     field_ref, normal_ref, inv_ref, scaled_ref, active_ref, d_hid_ref, theirs_ref,
@@ -247,7 +261,7 @@
     width, channels = near_ref.shape[0] - 80, near_ref.shape[1]
     take_strips(core_ref[0], odd_ref[0], (s0, s1, s2, s3), strips_ref)
     halo = dot(strips_ref[...], near_ref[0:width]).astype(BF16)
-    ring_ref[...] = dot(place_ref[...], halo)
+    ring_ref[...] = dot(place_ref[:, : 4 * STRIP], halo)
     field_ref[...] = own_ref[...]
     for at, x, y in ring():
         skip, count = (0, 8) if x in OUTER else (0, HALO) if y == 0 else (HALO, HALO)
@@ -372,7 +386,7 @@
             for g in range(0, SIDE, 8):
                 own_ref[pl.ds(i * SIDE + g, 8), lanes] = part(i + HALO, g + HALO, cb)
     take_strips(core_ref[0], odd_ref[0], (s0, s1, s2, s3), strips_ref)
-    d_halo = dot(place_ref[...], ring_ref[...].astype(BF16), TN).astype(BF16)
+    d_halo = dot(place_ref[:, : 4 * STRIP], ring_ref[...].astype(BF16), TN).astype(BF16)
     d_own = (own_ref[...] + cot_ref[...].astype(F32)).astype(BF16)
     grad_embed = dot(grid_ref[...], d_own, TN) + dot(strips_ref[...], d_halo, TN)
 
@@ -425,7 +439,7 @@
     def add(d, sums):
         return [s + in_ref[d, t].astype(F32) for t, s in enumerate(sums)]
 
-    sums = lax.fori_loop(0, parts, add, [jnp.zeros(in_ref.shape[2:], F32)] * tiles)
+    sums = lax.fori_loop(0, parts, add, [jnp.zeros(in_ref.shape[2:], F32)] * tiles, unroll=4)
     sums = [s.astype(BF16) for s in sums]
 
     def spread(d, carry):
@@ -433,7 +447,7 @@
             out_ref[d, t] = sums[t]
         return carry
 
-    lax.fori_loop(0, parts, spread, 0)
+    lax.fori_loop(0, parts, spread, 0, unroll=4)
 
 
 def assemble_half(core, in_ref, one_far, two_far, one_ref, two_ref, sem):
@@ -517,9 +531,7 @@
     return by_row, by_col
 
 
-def arriving_strips(spin):
-    x = jnp.asarray([x for _, x, _ in ring() for _ in range(8)], jnp.int32)
-    y = jnp.asarray([y + k for _, _, y in ring() for k in range(8)], jnp.int32)
+def arriving_strips(spin, x, y):
     row, col = turned(spin, x, y, FULL - 1)
     end = SIDE + HALO
     in_row, in_col = (row >= HALO) & (row < end), (col >= HALO) & (col < end)
@@ -529,11 +541,7 @@
         jnp.where((col < HALO) & in_row, 2 * STRIP + col * SIDE + row - HALO,
         jnp.where((col >= end) & in_row, 3 * STRIP + (col - end) * SIDE + row - HALO, -1))),
     )
-    strip = jnp.where(y < FULL, strip, -1)
-    k = jnp.arange(4 * STRIP, dtype=jnp.int32)
-    place = (strip[:, None] == k[None]).astype(BF16)
-
-    return place
+    return jnp.where(y < FULL, strip, -1)
 
 
 def exchange(far, one, two, by):
@@ -558,7 +566,6 @@
     hidden = w_one.shape[1]
     slots = interp.shape[2]
     core, odd = lax.axis_index("core").reshape(1), (lax.axis_index("face") % 2).reshape(1)
-    place = arriving_strips(tile_spin[0, 0])
     (leaving,) = call(
         route_kernel,
         [((tiles * 8, LANE), BF16)],
@@ -568,7 +575,7 @@
     arrived = lax.all_to_all(leaving.reshape(tiles, 8, LANE), ALL, 0, 0, tiled=True)
     stacked = ((CELLS, tiles * slots), BF16)
     near = ((width + 80, channels), BF16)
-    picks = ((4 * STRIP, CELLS), BF16)
+    picks, places = ((4 * STRIP, CELLS), BF16), ((RING, CELLS), BF16)
     shelved, d_active = call(
         prepare_kernel,
         [((SHELF, channels), BF16), ((SHELF // 8, hidden), F32)],
@@ -576,7 +583,7 @@
             (interp.shape[1:], BF16),
             (w_embed.shape, BF16),
             (dw_kernel.shape, BF16),
-            ((1, channels), F32),
+            ((channels // LANE, LANE), BF16),
             (w_two.shape, BF16),
             (cotangent.shape, BF16),
             ((CELLS, hidden), F32),
@@ -584,15 +591,16 @@
             picks,
             ((80, channels), F32),
             near,
+            places,
         ],
-        60.5, tile_spin.reshape(1), interp[0], w_embed, dw_kernel, norm_gain.astype(F32)[None], w_two, cotangent,
-        far=(1, 2, 3, 4, 5, 6), far_outs=(0, 1), copies=9 + hidden // (2 * STEP),
-    )
-    gridded, embedded, nearby, *strips = call(
+        60.5, tile_spin.reshape(1), interp[0], w_embed, dw_kernel, norm_gain.reshape(-1, LANE), w_two, cotangent,
+        far=(1, 2, 3, 4, 5, 6), far_outs=(0, 1), copies=10 + hidden // (2 * STEP),
+    )
+    gridded, embedded, nearby, place, *strips = call(
         embed_kernel,
-        [((CELLS, width), BF16), ((CELLS, channels), BF16), near] + [((STRIP, width), BF16)] * 4,
+        [((CELLS, width), BF16), ((CELLS, channels), BF16), near, places] + [((STRIP, width), BF16)] * 4,
         [((tiles * 8, LANE), F32), ((tiles * slots, width), BF16), stacked, picks, ((4 * STRIP, width), BF16)],
-        16, core, odd, arrived.reshape(tiles * 8, LANE), shelved, far=(3,), copies=3,
+        16, core, odd, arrived.reshape(tiles * 8, LANE), shelved, far=(3,), copies=4,
     )
     strips = exchange(*strips)
     cells2 = ((ROWS2 * PITCH * 8, LANE), F32)

time: 130 us -> 130 us (level)
  waiting for transfers between devices: 6.61 us -> 9.27 us
  other arithmetic: 1.4 us -> 0 us
    ppermute x4, waiting for transfers between devices: 0.14 us -> 1.51 us  [between(): return lax.ppermute(value, axes, pairs + [(j, i) for i, j in pairs])]
  transfers between devices with their start and end apart: 8 -> 8, of which waited for: 4 -> 4; matrix products, arithmetic and copies ran while one was open for 1% -> 0% of each run, Pallas kernels for 12% -> 12%
where the time goes in v7:
time: 130 us; the launch traced here: 129 us
  blocking collectives  73.2 us (56%)
  Pallas kernels  24.6 us (19%)
  starting transfers between devices  20.7 us (16%)
  waiting for transfers between devices  9.27 us (7%)
  between operations  1.57 us (1%)
    all_to_all x1, blocking collectives, on_device(): paired = lax.all_to_all(paired, CHIPS, 0, 0, tiled=True)  37 us
    all_to_all x1, blocking collectives, on_device(): here = lax.all_to_all(summed, CHIPS, 0, 0, tiled=True)  36.2 us
    pallas_call x11, Pallas kernels, call(): pl.pallas_call(kernel, out_shape=[jax.ShapeDtypeStruct(s, d) for s, d in...  24.6 us
    all_to_all x1, starting transfers between devices, on_device(): lax.all_to_all(leaving.reshape(tiles, 8, LANE), ALL, 0, 0, tiled=True)  11.5 us
    all_to_all x1, waiting for transfers between devices, on_device(): lax.all_to_all(leaving.reshape(tiles, 8, LANE), ALL, 0, 0, tiled=True)  6.26 us
    ppermute x3, starting transfers between devices, swap(): return lax.ppermute(value, 'core', [(0, 1), (1, 0)])  5.54 us
    ppermute x4, starting transfers between devices, between(): return lax.ppermute(value, axes, pairs + [(j, i) for i, j in pairs])  3.66 us
  transfers between devices with their start and end apart: 8, of which 4 were waited for; matrix products, arithmetic and copies ran while one was open for 0% of the time, Pallas kernels for 12%

profile of v7, /device:TPU:1, one launch (start us, length us, event | category | flops | bytes accessed | tf_op | source)
XLA Modules:
  0.0 129.4 jit_solution(14827372212210825697)
XLA Ops:
  0.6 1.9 %shard_map.145 = bf16[1024,128]{1,0:T(8,128)(2,1)} custom-call(s32[1]{0:T(128)} %bitcast.core_ref, s32[1]{0:T(128)} %bitcast.1.odd_ref, s32[1,256]{1,0:T(1,128)} %bitcast.13, bf16[256,256]{1,0:T(8,128)(2,1)} %obs_far.1), custom_call_target="tpu_custom_call" | custom-call | tf_op jit(solution)/shard_map/pallas_call | solution.py:39
  2.6 11.5 %all-to-all-start = ((bf16[128,8,128]{2,1,0:T(8,128)(2,1)}), bf16[128,8,128]{2,1,0:T(8,128)(2,1)S(1)}, u32[]{:S(2)}, u32[]{:S(2)}) async-start(bf16[128,8,128]{2,1,0:T(8,128)(2,1)} %bitcast.11), calls=%async_computation | async-start | bytes 524288 | tf_op jit(solution)/shard_map/all_to_all | solution.py:575
  14.7 3.8 %shard_map.146 = (bf16[65536,512]{1,0:T(8,128)(2,1)}, f32[8192,2048]{1,0:T(8,128)}) custom-call(s32[1]{0:T(128)} %bitcast.9.spin_ref, bf16[128,4,256]{2,1,0:T(4,128)(2,1)} %bitcast.12, bf16[256,512]{1,0:T(8,128)(2,1)} %w_embed_far.1, bf16[49,512]{1,0:T(8,128)(2,1)} %dw_far.1, bf16[4,128]{1,0:T(4,128)(2,1)} %bitcast.14, bf16[2048,512]{1,0:T(8,128)(2,1)} %w_two_ref.1, ...), custom_call_target="tpu_custom_call" | custom-call | tf_op jit(solution)/shard_map/pallas_call | solution.py:39
  18.6 6.3 %all-to-all-done = bf16[128,8,128]{2,1,0:T(8,128)(2,1)S(1)} async-done(((bf16[128,8,128]{2,1,0:T(8,128)(2,1)}), bf16[128,8,128]{2,1,0:T(8,128)(2,1)S(1)}, u32[]{:S(2)}, u32[]{:S(2)}) %all-to-all-start) | async-done | bytes 262176 | tf_op jit(solution)/shard_map/all_to_all | solution.py:575
  24.9 1.8 %shard_map.147 = (bf16[256,256]{1,0:T(8,128)(2,1)S(1)}, bf16[256,512]{1,0:T(8,128)(2,1)S(1)}, bf16[336,512]{1,0:T(8,128)(2,1)S(1)}, bf16[400,256]{1,0:T(8,128)(2...) custom-call(s32[1]{0:T(128)} %bitcast.core_ref, ...), custom_call_target="tpu_custom_call" | custom-call | tf_op jit(solution)/shard_map/pallas_call | solution.py:39
  26.6 1.7 %collective-permute-start = (bf16[48,256]{1,0:T(8,128)(2,1)S(1)}, bf16[48,256]{1,0:T(8,128)(2,1)S(1)}, u32[]{:S(2)}, u32[]{:S(2)}) collective-permute-start(bf16[48,256]{1,0:T(8,128)(2,1)S(1)} %get-tuple-element.39), channel_id=1, source_target_pairs={{1,2},{3,4},{5,6},{7,8},{9,10},{11,12},{13,14},{15,0},{2,1},{4,3},... | collective-permute-start | bytes 73736 | tf_op jit(solution)/shard_map/ppermute | solution.py:551
  28.3 0.3 collective-permute-start.1
  28.6 0.8 collective-permute-start.2
  29.5 0.8 collective-permute-start.3
  30.3 1.7 %shard_map.148 = (f32[2688,128]{1,0:T(8,128)S(1)}, f32[1024,128]{1,0:T(8,128)S(1)}, f32[392,128]{1,0:T(8,128)S(1)}, f32[256,2048]{1,0:T(8,128)S(1)}) custom-call(bf16[256,512]{1,0:T(8,128)(2,1)S(1)} %get-tuple-element.45.emb_ref, bf16[336,512]{1,0:T(8,128)(2,1)S(1)} %get-tuple-element.44.near_ref, f32[8192,2048]{1,0:T(8,128)} %get-tuple-element.46.d_act_far), custom_call_target="tpu_custom_call" | custom-call | tf_op jit(solution)/shard_map/pallas_call | solution.py:39
  32.1 1.5 %collective-permute-done.2.s2 = bf16[48,256]{1,0:T(8,128)(2,1)S(1)} collective-permute-done((bf16[48,256]{1,0:T(8,128)(2,1)S(1)}, bf16[48,256]{1,0:T(8,128)(2,1)S(1)}, u32[]{:S(2)}, u32[]{:S(2)}) %collective-permute-start.2) | collective-permute-done | bytes 24608 | tf_op jit(solution)/shard_map/ppermute | solution.py:551
  33.6 2.8 %shard_map.149 = (f32[2688,128]{1,0:T(8,128)S(1)}, f32[256,512]{1,0:T(8,128)S(1)}, f32[256,128]{1,0:T(8,128)S(1)}, bf16[256,512]{1,0:T(8,128)(2,1)S(1)}, bf16[25...) custom-call(s32[1]{0:T(128)} %bitcast.core_ref, s32[1]{0:T(128)} %bitcast.1.odd_ref, ...), custom_call_target="tpu_custom_call" | custom-call | tf_op jit(solution)/shard_map/pallas_call | solution.py:39
  36.4 2.6 %collective-permute-start.5 = (bf16[256,3072]{1,0:T(8,128)(2,1)S(1)}, bf16[256,3072]{1,0:T(8,128)(2,1)S(1)}, u32[]{:S(2)}, u32[]{:S(2)}) collective-permute-start(bf16[256,3072]{1,0:T(8,128)(2,1)S(1)} %get-tuple-element.59), channel_id=1, source_target_pairs={{0,1},{1,0},{2,3},{3,2},{4,5},{5,4},{6,7},{7,6},{8,9},{9,8},{10,11... | collective-permute-start | bytes 4718600 | tf_op jit(solution)/shard_map/ppermute | solution.py:558
  39.0 5.3 %shard_map.150 = (f32[64,16,128]{2,1,0:T(8,128)S(1)}, bf16[64,16,128]{2,1,0:T(8,128)(2,1)S(1)}) custom-call(s32[1]{0:T(128)} %bitcast.core_ref, s32[1]{0:T(128)} %bitcast.1.odd_ref, bf16[256,256]{1,0:T(8,128)(2,1)S(1)} %get-tuple-element.38.grid_ref, bf16[48,256]{1,0:T(8,128)(2,1)S(1)} %collective-permute-done.s0, ...), custom_call_target="tpu_custom_call" | custom-call | tf_op jit(solution)/shard_map/pallas_call | solution.py:39
  44.3 0.1 collective-permute-start.4
  44.4 1.3 %shard_map.151.paired_far = bf16[64,9,16,128]{3,2,1,0:T(8,128)(2,1)S(1)} custom-call(s32[1]{0:T(128)} %bitcast.core_ref, bf16[256,512]{1,0:T(8,128)(2,1)S(1)} %get-tuple-element.57.scaled_ref, bf16[256,2048]{1,0:T(8,128)(2,1)S(1)} %get-tuple-element.58.active_ref, bf16[256,2048]{1,0:T(8,128)(2,1)S(1)} %get-tuple-element.54.d_hid_ref, ...), custom_call_target="tpu_custom_call" | custom-call | tf_op jit(solution)/shard_map/pallas_call | solution.py:39
  45.7 0.2 collective-permute-done.4.small_ref
  46.0 37.0 %all_to_all.15.in_ref = bf16[64,9,16,128]{3,2,1,0:T(8,128)(2,1)S(1)} all-to-all(bf16[64,9,16,128]{3,2,1,0:T(8,128)(2,1)S(1)} %shard_map.152), channel_id=1, replica_groups=mesh['face'=8,'col'=8,'core'=2] {'face','col'}, dimensions={0} | all-to-all | bytes 4718592 | tf_op jit(solution)/shard_map/all_to_all | solution.py:648
  83.0 0.6 shard_map.153
  83.6 36.2 %all_to_all.16.in_ref.mine_ref = bf16[64,9,16,128]{3,2,1,0:T(8,128)(2,1)S(1)} all-to-all(bf16[64,9,16,128]{3,2,1,0:T(8,128)(2,1)S(1)} %shard_map.153), channel_id=1, replica_groups=mesh['face'=8,'col'=8,'core'=2] {'face','col'}, dimensions={0} | all-to-all | bytes 4718592 | tf_op jit(solution)/shard_map/all_to_all | solution.py:650
  119.8 2.9 %collective-permute-start.6 = (bf16[64,9,16,128]{3,2,1,0:T(8,128)(2,1)S(1)}, bf16[64,9,16,128]{3,2,1,0:T(8,128)(2,1)S(1)}, u32[]{:S(2)}, u32[]{:S(2)}) collective-permute-start(bf16[64,9,16,128]{3,2,1,0:T(8,128)(2,1)S(1)} %all_to_all.16.in_ref.mine_ref), channel_id=1, source_target_pairs={{0,1},{1,0},{2,3},{3,2},{4,5},{5,4},{6,7},{7,6},{8,9},{9,8},{10,11... | collective-permute-start | bytes 7077896 | tf_op jit(solution)/shard_map/ppermute | solution.py:558
  122.7 2.8 %shard_map.154 = (f32[512,2048]{1,0:T(8,128)}, f32[2048,512]{1,0:T(8,128)}, bf16[256,512]{1,0:T(8,128)(2,1)}) custom-call(s32[1]{0:T(128)} %bitcast.core_ref, bf16[64,9,16,128]{3,2,1,0:T(8,128)(2,1)S(1)} %all_to_all.16.in_ref.mine_ref, bf16[256,512]{1,0:T(8,128)(2,1)S(1)} %get-tuple-element.45.emb_ref, bf16[256,2048]{1,0:T(8,128)(2,1)S(1)} %get-tuple-element.58.active_ref, ...), custom_call_target="tpu_custom_call" | custom-call | tf_op jit(solution)/shard_map/pallas_call | solution.py:39
  125.5 1.3 %collective-permute-done.6.in_ref = bf16[64,9,16,128]{3,2,1,0:T(8,128)(2,1)S(1)} collective-permute-done((bf16[64,9,16,128]{3,2,1,0:T(8,128)(2,1)S(1)}, bf16[64,9,16,128]{3,2,1,0:T(8,128)(2,1)S(1)}, u32[]{:S(2)}, u32[]{:S(2)}) %collective-permute-start.6) | collective-permute-done | bytes 2359328 | tf_op jit(solution)/shard_map/ppermute | solution.py:558
  126.8 2.4 %shard_map.155 = (f32[512,2048]{1,0:T(8,128)}, f32[2048,512]{1,0:T(8,128)}, f32[256,512]{1,0:T(8,128)}, f32[49,512]{1,0:T(8,128)}, f32[1,512]{1,0:T(1,128)}) custom-call(s32[1]{0:T(128)} %bitcast.core_ref, bf16[64,9,16,128]{3,2,1,0:T(8,128)(2,1)S(1)} %collective-permute-done.6.in_ref, ...), custom_call_target="tpu_custom_call", output_to_operand_aliasing={{0}: (3, {}), {1}: (4, {})} | custom-call | tf_op jit(solution)/shard_map/pallas_call | solution.py:39
  (11 shorter events, 0.1 us)
Async XLA Ops:
  2.6 22.3 %all-to-all-start = ((bf16[128,8,128]{2,1,0:T(8,128)(2,1)}), bf16[128,8,128]{2,1,0:T(8,128)(2,1)S(1)}, u32[]{:S(2)}, u32[]{:S(2)}) async-start(bf16[128,8,128]{2,1,0:T(8,128)(2,1)} %bitcast.11), calls=%async_computation | async-start | bytes 524288 | tf_op jit(solution)/shard_map/all_to_all | solution.py:575
  26.6 5.4 %collective-permute-start = (bf16[48,256]{1,0:T(8,128)(2,1)S(1)}, bf16[48,256]{1,0:T(8,128)(2,1)S(1)}, u32[]{:S(2)}, u32[]{:S(2)}) collective-permute-start(bf16[48,256]{1,0:T(8,128)(2,1)S(1)} %get-tuple-element.39), channel_id=1, source_target_pairs={{1,2},{3,4},{5,6},{7,8},{9,10},{11,12},{13,14},{15,0},{2,1},{4,3},... | collective-permute-start | bytes 73736 | tf_op jit(solution)/shard_map/ppermute | solution.py:551
  28.3 3.8 %collective-permute-start.1 = (bf16[48,256]{1,0:T(8,128)(2,1)S(1)}, bf16[48,256]{1,0:T(8,128)(2,1)S(1)}, u32[]{:S(2)}, u32[]{:S(2)}) collective-permute-start(bf16[48,256]{1,0:T(8,128)(2,1)S(1)} %get-tuple-element.40), channel_id=1, source_target_pairs={{0,16},{32,48},{64,80},{96,112},{16,0},{48,32},{80,64},{112,96},{1... | collective-permute-start | bytes 73736 | tf_op jit(solution)/shard_map/ppermute | solution.py:551
  28.6 4.9 %collective-permute-start.2 = (bf16[48,256]{1,0:T(8,128)(2,1)S(1)}, bf16[48,256]{1,0:T(8,128)(2,1)S(1)}, u32[]{:S(2)}, u32[]{:S(2)}) collective-permute-start(bf16[48,256]{1,0:T(8,128)(2,1)S(1)} %get-tuple-element.41), channel_id=1, source_target_pairs={{16,32},{48,64},{80,96},{112,0},{32,16},{64,48},{96,80},{0,112},{1... | collective-permute-start | bytes 73736 | tf_op jit(solution)/shard_map/ppermute | solution.py:551
  29.5 4.1 %collective-permute-start.3 = (bf16[48,256]{1,0:T(8,128)(2,1)S(1)}, bf16[48,256]{1,0:T(8,128)(2,1)S(1)}, u32[]{:S(2)}, u32[]{:S(2)}) collective-permute-start(bf16[48,256]{1,0:T(8,128)(2,1)S(1)} %get-tuple-element.42), channel_id=1, source_target_pairs={{0,1},{2,3},{4,5},{6,7},{8,9},{10,11},{12,13},{14,15},{1,0},{3,2},... | collective-permute-start | bytes 73736 | tf_op jit(solution)/shard_map/ppermute | solution.py:551
  30.3 3.3 %copy-start.1 = (bf16[512,2048]{1,0:T(8,128)(2,1)S(1)}, bf16[512,2048]{1,0:T(8,128)(2,1)}, u32[]{:S(2)}) copy-start(bf16[512,2048]{1,0:T(8,128)(2,1)} %w_one_ref.3) | copy-start | bytes 6291460
  30.3 3.3 %copy-start.2 = (bf16[256,512]{1,0:T(8,128)(2,1)S(1)}, bf16[256,512]{1,0:T(8,128)(2,1)}, u32[]{:S(2)}) copy-start(bf16[256,512]{1,0:T(8,128)(2,1)} %cot_ref.5) | copy-start | bytes 786436
  36.4 8.0 %collective-permute-start.5 = (bf16[256,3072]{1,0:T(8,128)(2,1)S(1)}, bf16[256,3072]{1,0:T(8,128)(2,1)S(1)}, u32[]{:S(2)}, u32[]{:S(2)}) collective-permute-start(bf16[256,3072]{1,0:T(8,128)(2,1)S(1)} %get-tuple-element.59), channel_id=1, source_target_pairs={{0,1},{1,0},{2,3},{3,2},{4,5},{5,4},{6,7},{7,6},{8,9},{9,8},{10,11... | collective-permute-start | bytes 4718600 | tf_op jit(solution)/shard_map/ppermute | solution.py:558
  44.3 1.6 %collective-permute-start.4 = (bf16[64,16,128]{2,1,0:T(8,128)(2,1)S(1)}, bf16[64,16,128]{2,1,0:T(8,128)(2,1)S(1)}, u32[]{:S(2)}, u32[]{:S(2)}) collective-permute-start(bf16[64,16,128]{2,1,0:T(8,128)(2,1)S(1)} %get-tuple-element.56), channel_id=1, source_target_pairs={{0,1},{1,0},{2,3},{3,2},{4,5},{5,4},{6,7},{7,6},{8,9},{9,8},{10,11... | collective-permute-start | bytes 786440 | tf_op jit(solution)/shard_map/ppermute | solution.py:558
  83.6 39.1 %copy-start = (bf16[2048,512]{1,0:T(8,128)(2,1)S(1)}, bf16[2048,512]{1,0:T(8,128)(2,1)}, u32[]{:S(2)}) copy-start(bf16[2048,512]{1,0:T(8,128)(2,1)} %w_two_ref.1) | copy-start | bytes 6291460
  119.8 7.0 %collective-permute-start.6 = (bf16[64,9,16,128]{3,2,1,0:T(8,128)(2,1)S(1)}, bf16[64,9,16,128]{3,2,1,0:T(8,128)(2,1)S(1)}, u32[]{:S(2)}, u32[]{:S(2)}) collective-permute-start(bf16[64,9,16,128]{3,2,1,0:T(8,128)(2,1)S(1)} %all_to_all.16.in_ref.mine_ref), channel_id=1, source_target_pairs={{0,1},{1,0},{2,3},{3,2},{4,5},{5,4},{6,7},{7,6},{8,9},{9,8},{10,11... | collective-permute-start | bytes 7077896 | tf_op jit(solution)/shard_map/ppermute | solution.py:558

commit v8 on v7

--- a/solution.py
+++ b/solution.py
@@ -121,19 +121,18 @@
 
 
 def prepare_kernel(
-    spin_ref, interp_far, w_embed_far, dw_far, gain_far, w_two_far, cot_far, shelf_far, d_act_far,
-    interp_ref, w_embed_ref, dw_ref, gain_ref, w_two_ref, cot_ref, d_act_ref, weights_ref, pick_ref, small_ref, near_ref,
-    place_ref, sem,
+    spin_ref, interp_far, w_embed_far, small_far, w_two_far, cot_far, shelf_far, d_act_far,
+    interp_ref, w_two_ref, cot_ref, d_act_ref, weights_ref, pick_ref, near_ref, place_ref, sem,
 ):
     tiles, slots = interp_ref.shape[:2]
-    width, channels = w_embed_ref.shape
+    width, channels = w_embed_far.shape
     spots = shelf(width, tiles * slots, channels)
     fetches = start(
-        sem, (interp_far, interp_ref), (cot_far, cot_ref), (w_embed_far, w_embed_ref), (dw_far, dw_ref),
-        (gain_far, gain_ref), (w_two_far, w_two_ref),
+        sem, (interp_far, interp_ref), (w_embed_far, near_ref.at[pl.ds(0, width)]),
+        (small_far, near_ref.at[pl.ds(width, 80)]), (cot_far, cot_ref), (w_two_far, w_two_ref),
     )
     put_weights, put_pick, put_near, put_place = (
-        pltpu.make_async_copy(a, shelf_far.at[spot], sem.at[6 + k])
+        pltpu.make_async_copy(a, shelf_far.at[spot], sem.at[5 + k])
         for k, (a, spot) in enumerate(zip((weights_ref, pick_ref, near_ref, place_ref), spots))
     )
     spin = spin_ref[0]
@@ -156,22 +155,17 @@
     k = lax.broadcasted_iota(jnp.int32, place_ref.shape, 1)
     place_ref[...] = jnp.where(strip == k, 1.0, 0.0).astype(BF16)
     put_place.start()
-    for fetch in fetches[1:]:
+    for fetch in fetches[1:3]:
         fetch.wait()
-    small_ref[...] = jnp.zeros_like(small_ref)
-    small_ref[0 : TAPS * TAPS] = dw_ref[...].astype(F32)
-    gain = gain_ref[...].astype(F32)
-    for c in range(channels // LANE):
-        small_ref[64:, c * LANE : (c + 1) * LANE] = jnp.broadcast_to(gain[c : c + 1], (16, LANE))
-    near_ref[0:width] = w_embed_ref[...]
-    near_ref[width:] = small_ref[...].astype(BF16)
     put_near.start()
+    for fetch in fetches[3:]:
+        fetch.wait()
     puts = []
     for k in range(0, w_two_ref.shape[0], 2 * STEP):
         some = pl.ds(k, 2 * STEP)
         d_act_ref[:, some] = dot(cot_ref[...], w_two_ref[some, :], NT)
         target = d_act_far.at[pl.ds(0, CELLS), some]
-        puts.append(pltpu.make_async_copy(d_act_ref.at[:, some], target, sem.at[10 + len(puts)]))
+        puts.append(pltpu.make_async_copy(d_act_ref.at[:, some], target, sem.at[9 + len(puts)]))
         puts[-1].start()
     for put in [put_pick, put_near, put_weights, put_place] + puts:
         put.wait()
@@ -414,15 +408,16 @@
     half, channels = active_ref.shape[1] // 2, cot_ref.shape[1]
     their_scaled = their_ref[:, 2 * half : 2 * half + channels]
     their_cot = their_ref[:, 2 * half + channels :]
+    mine = pl.ds(pl.multiple_of(core_ref[0] * half, half), half)
+    one_ref[...] = dot(scaled_ref[...], d_hid_ref[:, mine], TN) + dot(
+        their_scaled, their_ref[:, half : 2 * half], TN
+    )
     for k in range(half // STEP):
         some = pl.ds(pl.multiple_of(core_ref[0] * half + k * STEP, STEP), STEP)
         two_ref[...] = dot(active_ref[:, some], cot_ref[...], TN) + dot(
             their_ref[:, k * STEP : (k + 1) * STEP], their_cot, TN
         )
-        one_ref[...] = dot(scaled_ref[...], d_hid_ref[:, some], TN) + dot(
-            their_scaled, their_ref[:, half + k * STEP : half + (k + 1) * STEP], TN
-        )
-        for t, ref, rows, lanes in tiles_of(k, two_ref, one_ref):
+        for t, ref, rows, lanes in tiles_of(k, two_ref, one_ref.at[:, k * STEP : (k + 1) * STEP]):
             out_ref[t // 8, t % 8] = ref[rows, lanes].astype(BF16)
 
 
@@ -575,26 +570,25 @@
     arrived = lax.all_to_all(leaving.reshape(tiles, 8, LANE), ALL, 0, 0, tiled=True)
     stacked = ((CELLS, tiles * slots), BF16)
     near = ((width + 80, channels), BF16)
+    taps_gain = jnp.concatenate(
+        [dw_kernel, jnp.zeros((64 - TAPS * TAPS, channels), BF16), jnp.broadcast_to(norm_gain, (16, channels))]
+    )
     picks, places = ((4 * STRIP, CELLS), BF16), ((RING, CELLS), BF16)
     shelved, d_active = call(
         prepare_kernel,
         [((SHELF, channels), BF16), ((SHELF // 8, hidden), F32)],
         [
             (interp.shape[1:], BF16),
-            (w_embed.shape, BF16),
-            (dw_kernel.shape, BF16),
-            ((channels // LANE, LANE), BF16),
             (w_two.shape, BF16),
             (cotangent.shape, BF16),
             ((CELLS, hidden), F32),
             stacked,
             picks,
-            ((80, channels), F32),
             near,
             places,
         ],
-        60.5, tile_spin.reshape(1), interp[0], w_embed, dw_kernel, norm_gain.reshape(-1, LANE), w_two, cotangent,
-        far=(1, 2, 3, 4, 5, 6), far_outs=(0, 1), copies=10 + hidden // (2 * STEP),
+        60.5, tile_spin.reshape(1), interp[0], w_embed, taps_gain, w_two, cotangent,
+        far=(1, 2, 3, 4, 5), far_outs=(0, 1), copies=9 + hidden // (2 * STEP),
     )
     gridded, embedded, nearby, place, *strips = call(
         embed_kernel,
@@ -607,7 +601,7 @@
     kernel = ((TAPS * TAPS * 8, LANE), F32)
     blocks, cells = ((CELLS * 4, LANE), F32), ((CELLS, channels), F32)
     around = ((RING, channels), F32)
-    step_sums = [((STEP, channels), F32), ((channels, STEP), F32)]
+    step_sums = [((STEP, channels), F32), ((channels, hidden // 2), F32)]
     field, conv, taps, d_active = call(
         inner_kernel, [cells2, blocks, kernel, ((CELLS, hidden), F32)], [], 20,
         embedded, nearby, d_active, far=(2,), copies=1,

time: 130 us -> 130 us (level)
  waiting for transfers between devices: 9.27 us -> 5.64 us
  other arithmetic: 0 us -> 1.53 us
    all_to_all x1, waiting for transfers between devices: 6.26 us -> 4.1 us  [on_device(): lax.all_to_all(leaving.reshape(tiles, 8, LANE), ALL, 0, 0, tiled=True)]
    ppermute x4, starting transfers between devices: 3.66 us -> 5.76 us  [between(): return lax.ppermute(value, axes, pairs + [(j, i) for i, j in pairs])]
    concatenate x0 -> x1, other arithmetic: none -> 1.53 us  [on_device(): jnp.concatenate([dw_kernel, jnp.zeros((64 - TAPS * TAPS, channels), BF16)...]
    ppermute x4, waiting for transfers between devices: 1.51 us -> 0.01 us  [between(): return lax.ppermute(value, axes, pairs + [(j, i) for i, j in pairs])]
  transfers between devices with their start and end apart: 8 -> 8, of which waited for: 4 -> 3; matrix products, arithmetic and copies ran while one was open for 0% -> 2% of each run, Pallas kernels for 12% -> 12%
where the time goes in v8:
time: 130 us; the launch traced here: 129 us
  blocking collectives  72.9 us (56%)
  Pallas kernels  24.4 us (19%)
  starting transfers between devices  21.8 us (17%)
  waiting for transfers between devices  5.64 us (4%)
  between operations  1.6 us (1%)
  other arithmetic  1.53 us (1%)
    all_to_all x1, blocking collectives, on_device(): paired = lax.all_to_all(paired, CHIPS, 0, 0, tiled=True)  36.7 us
    all_to_all x1, blocking collectives, on_device(): here = lax.all_to_all(summed, CHIPS, 0, 0, tiled=True)  36.2 us
    pallas_call x11, Pallas kernels, call(): pl.pallas_call(kernel, out_shape=[jax.ShapeDtypeStruct(s, d) for s, d in...  24.4 us
    all_to_all x1, starting transfers between devices, on_device(): lax.all_to_all(leaving.reshape(tiles, 8, LANE), ALL, 0, 0, tiled=True)  11.5 us
    ppermute x4, starting transfers between devices, between(): return lax.ppermute(value, axes, pairs + [(j, i) for i, j in pairs])  5.76 us
    ppermute x3, starting transfers between devices, swap(): return lax.ppermute(value, 'core', [(0, 1), (1, 0)])  4.58 us
    all_to_all x1, waiting for transfers between devices, on_device(): lax.all_to_all(leaving.reshape(tiles, 8, LANE), ALL, 0, 0, tiled=True)  4.1 us
  transfers between devices with their start and end apart: 8, of which 3 were waited for; matrix products, arithmetic and copies ran while one was open for 2% of the time, Pallas kernels for 12%

profile of v8, /device:TPU:1, one launch (start us, length us, event | category | flops | bytes accessed | tf_op | source)
XLA Modules:
  0.0 129.1 jit_solution(10236739447027684823)
XLA Ops:
  0.6 1.9 %shard_map.145 = bf16[1024,128]{1,0:T(8,128)(2,1)} custom-call(s32[1]{0:T(128)} %bitcast.core_ref, s32[1]{0:T(128)} %bitcast.1.odd_ref, s32[1,256]{1,0:T(1,128)} %bitcast.12, bf16[256,256]{1,0:T(8,128)(2,1)} %obs_far.1), custom_call_target="tpu_custom_call" | custom-call | tf_op jit(solution)/shard_map/pallas_call | solution.py:39
  2.6 11.5 %all-to-all-start = ((bf16[128,8,128]{2,1,0:T(8,128)(2,1)}), bf16[128,8,128]{2,1,0:T(8,128)(2,1)S(1)}, u32[]{:S(2)}, u32[]{:S(2)}) async-start(bf16[128,8,128]{2,1,0:T(8,128)(2,1)} %bitcast.10), calls=%async_computation | async-start | bytes 524288 | tf_op jit(solution)/shard_map/all_to_all | solution.py:570
  14.8 0.7 broadcast_in_dim.7
  15.5 1.5 %pad_maximum_fusion.small_far = bf16[80,512]{1,0:T(8,128)(2,1)} fusion(bf16[16,512]{1,0:T(8,128)(2,1)S(1)} %broadcast_in_dim.7, bf16[49,512]{1,0:T(8,128)(2,1)} %param.15, bf16[80]{0:T(256)(128)(2,1)S(1)} %pad.1.clone), kind=kLoop, calls=%fused_computation | loop fusion | flops 245760 | bytes 148640 | tf_op jit(solution)/shard_map/concatenate | solution.py:573
  17.1 3.7 %shard_map.146 = (bf16[65536,512]{1,0:T(8,128)(2,1)}, f32[8192,2048]{1,0:T(8,128)}) custom-call(s32[1]{0:T(128)} %bitcast.8.spin_ref, bf16[128,4,256]{2,1,0:T(4,128)(2,1)} %bitcast.11, bf16[256,512]{1,0:T(8,128)(2,1)} %w_embed_far.1, bf16[80,512]{1,0:T(8,128)(2,1)} %pad_maximum_fusion.small_far, bf16[2048,512]{1,0:T(8,128)(2,1)} %w_two_ref.1, ...), custom_call_target="tpu_custom_call" | custom-call | tf_op jit(solution)/shard_map/pallas_call | solution.py:39
  20.8 4.1 %all-to-all-done = bf16[128,8,128]{2,1,0:T(8,128)(2,1)S(1)} async-done(((bf16[128,8,128]{2,1,0:T(8,128)(2,1)}), bf16[128,8,128]{2,1,0:T(8,128)(2,1)S(1)}, u32[]{:S(2)}, u32[]{:S(2)}) %all-to-all-start) | async-done | bytes 262176 | tf_op jit(solution)/shard_map/all_to_all | solution.py:570
  24.9 1.8 %shard_map.147 = (bf16[256,256]{1,0:T(8,128)(2,1)S(1)}, bf16[256,512]{1,0:T(8,128)(2,1)S(1)}, bf16[336,512]{1,0:T(8,128)(2,1)S(1)}, bf16[400,256]{1,0:T(8,128)(2...) custom-call(s32[1]{0:T(128)} %bitcast.core_ref, ...), custom_call_target="tpu_custom_call" | custom-call | tf_op jit(solution)/shard_map/pallas_call | solution.py:39
  26.6 1.7 %collective-permute-start = (bf16[48,256]{1,0:T(8,128)(2,1)S(1)}, bf16[48,256]{1,0:T(8,128)(2,1)S(1)}, u32[]{:S(2)}, u32[]{:S(2)}) collective-permute-start(bf16[48,256]{1,0:T(8,128)(2,1)S(1)} %get-tuple-element.39), channel_id=1, source_target_pairs={{1,2},{3,4},{5,6},{7,8},{9,10},{11,12},{13,14},{15,0},{2,1},{4,3},... | collective-permute-start | bytes 73736 | tf_op jit(solution)/shard_map/ppermute | solution.py:546
  28.3 0.3 collective-permute-start.1
  28.6 0.9 collective-permute-start.2
  29.5 2.9 %collective-permute-start.3 = (bf16[48,256]{1,0:T(8,128)(2,1)S(1)}, bf16[48,256]{1,0:T(8,128)(2,1)S(1)}, u32[]{:S(2)}, u32[]{:S(2)}) collective-permute-start(bf16[48,256]{1,0:T(8,128)(2,1)S(1)} %get-tuple-element.42), channel_id=1, source_target_pairs={{0,1},{2,3},{4,5},{6,7},{8,9},{10,11},{12,13},{14,15},{1,0},{3,2},... | collective-permute-start | bytes 73736 | tf_op jit(solution)/shard_map/ppermute | solution.py:546
  32.4 1.7 %shard_map.148 = (f32[2688,128]{1,0:T(8,128)S(1)}, f32[1024,128]{1,0:T(8,128)S(1)}, f32[392,128]{1,0:T(8,128)S(1)}, f32[256,2048]{1,0:T(8,128)S(1)}) custom-call(bf16[256,512]{1,0:T(8,128)(2,1)S(1)} %get-tuple-element.45.emb_ref, bf16[336,512]{1,0:T(8,128)(2,1)S(1)} %get-tuple-element.44.near_ref, f32[8192,2048]{1,0:T(8,128)} %get-tuple-element.46.d_act_far), custom_call_target="tpu_custom_call" | custom-call | tf_op jit(solution)/shard_map/pallas_call | solution.py:39
  34.2 0.4 copy-done.1
  34.6 2.8 %shard_map.149 = (f32[2688,128]{1,0:T(8,128)S(1)}, f32[256,512]{1,0:T(8,128)S(1)}, f32[256,128]{1,0:T(8,128)S(1)}, bf16[256,512]{1,0:T(8,128)(2,1)S(1)}, bf16[25...) custom-call(s32[1]{0:T(128)} %bitcast.core_ref, s32[1]{0:T(128)} %bitcast.1.odd_ref, ...), custom_call_target="tpu_custom_call" | custom-call | tf_op jit(solution)/shard_map/pallas_call | solution.py:39
  37.4 1.6 %collective-permute-start.5 = (bf16[256,3072]{1,0:T(8,128)(2,1)S(1)}, bf16[256,3072]{1,0:T(8,128)(2,1)S(1)}, u32[]{:S(2)}, u32[]{:S(2)}) collective-permute-start(bf16[256,3072]{1,0:T(8,128)(2,1)S(1)} %get-tuple-element.59), channel_id=1, source_target_pairs={{0,1},{1,0},{2,3},{3,2},{4,5},{5,4},{6,7},{7,6},{8,9},{9,8},{10,11... | collective-permute-start | bytes 4718600 | tf_op jit(solution)/shard_map/ppermute | solution.py:553
  39.0 5.3 %shard_map.150 = (f32[64,16,128]{2,1,0:T(8,128)S(1)}, bf16[64,16,128]{2,1,0:T(8,128)(2,1)S(1)}) custom-call(s32[1]{0:T(128)} %bitcast.core_ref, s32[1]{0:T(128)} %bitcast.1.odd_ref, bf16[256,256]{1,0:T(8,128)(2,1)S(1)} %get-tuple-element.38.grid_ref, bf16[48,256]{1,0:T(8,128)(2,1)S(1)} %collective-permute-done.s0, ...), custom_call_target="tpu_custom_call" | custom-call | tf_op jit(solution)/shard_map/pallas_call | solution.py:39
  44.4 1.3 %shard_map.151.paired_far = bf16[64,9,16,128]{3,2,1,0:T(8,128)(2,1)S(1)} custom-call(s32[1]{0:T(128)} %bitcast.core_ref, bf16[256,512]{1,0:T(8,128)(2,1)S(1)} %get-tuple-element.57.scaled_ref, bf16[256,2048]{1,0:T(8,128)(2,1)S(1)} %get-tuple-element.58.active_ref, bf16[256,2048]{1,0:T(8,128)(2,1)S(1)} %get-tuple-element.54.d_hid_ref, ...), custom_call_target="tpu_custom_call" | custom-call | tf_op jit(solution)/shard_map/pallas_call | solution.py:39
  46.0 36.7 %all_to_all.15.in_ref = bf16[64,9,16,128]{3,2,1,0:T(8,128)(2,1)S(1)} all-to-all(bf16[64,9,16,128]{3,2,1,0:T(8,128)(2,1)S(1)} %shard_map.152), channel_id=1, replica_groups=mesh['face'=8,'col'=8,'core'=2] {'face','col'}, dimensions={0} | all-to-all | bytes 4718592 | tf_op jit(solution)/shard_map/all_to_all | solution.py:642
  82.7 0.6 shard_map.153
  83.3 36.2 %all_to_all.16.in_ref.mine_ref = bf16[64,9,16,128]{3,2,1,0:T(8,128)(2,1)S(1)} all-to-all(bf16[64,9,16,128]{3,2,1,0:T(8,128)(2,1)S(1)} %shard_map.153), channel_id=1, replica_groups=mesh['face'=8,'col'=8,'core'=2] {'face','col'}, dimensions={0} | all-to-all | bytes 4718592 | tf_op jit(solution)/shard_map/all_to_all | solution.py:644
  119.5 2.9 %collective-permute-start.6 = (bf16[64,9,16,128]{3,2,1,0:T(8,128)(2,1)S(1)}, bf16[64,9,16,128]{3,2,1,0:T(8,128)(2,1)S(1)}, u32[]{:S(2)}, u32[]{:S(2)}) collective-permute-start(bf16[64,9,16,128]{3,2,1,0:T(8,128)(2,1)S(1)} %all_to_all.16.in_ref.mine_ref), channel_id=1, source_target_pairs={{0,1},{1,0},{2,3},{3,2},{4,5},{5,4},{6,7},{7,6},{8,9},{9,8},{10,11... | collective-permute-start | bytes 7077896 | tf_op jit(solution)/shard_map/ppermute | solution.py:553
  122.5 2.8 %shard_map.154 = (f32[512,2048]{1,0:T(8,128)}, f32[2048,512]{1,0:T(8,128)}, bf16[256,512]{1,0:T(8,128)(2,1)}) custom-call(s32[1]{0:T(128)} %bitcast.core_ref, bf16[64,9,16,128]{3,2,1,0:T(8,128)(2,1)S(1)} %all_to_all.16.in_ref.mine_ref, bf16[256,512]{1,0:T(8,128)(2,1)S(1)} %get-tuple-element.45.emb_ref, bf16[256,2048]{1,0:T(8,128)(2,1)S(1)} %get-tuple-element.58.active_ref, ...), custom_call_target="tpu_custom_call" | custom-call | tf_op jit(solution)/shard_map/pallas_call | solution.py:39
  125.3 1.3 %collective-permute-done.6.in_ref = bf16[64,9,16,128]{3,2,1,0:T(8,128)(2,1)S(1)} collective-permute-done((bf16[64,9,16,128]{3,2,1,0:T(8,128)(2,1)S(1)}, bf16[64,9,16,128]{3,2,1,0:T(8,128)(2,1)S(1)}, u32[]{:S(2)}, u32[]{:S(2)}) %collective-permute-start.6) | collective-permute-done | bytes 2359328 | tf_op jit(solution)/shard_map/ppermute | solution.py:553
  126.6 2.4 %shard_map.155 = (f32[512,2048]{1,0:T(8,128)}, f32[2048,512]{1,0:T(8,128)}, f32[256,512]{1,0:T(8,128)}, f32[49,512]{1,0:T(8,128)}, f32[1,512]{1,0:T(1,128)}) custom-call(s32[1]{0:T(128)} %bitcast.core_ref, bf16[64,9,16,128]{3,2,1,0:T(8,128)(2,1)S(1)} %collective-permute-done.6.in_ref, ...), custom_call_target="tpu_custom_call", output_to_operand_aliasing={{0}: (3, {}), {1}: (4, {})} | custom-call | tf_op jit(solution)/shard_map/pallas_call | solution.py:39
  (15 shorter events, 0.5 us)
Async XLA Ops:
  2.6 22.3 %all-to-all-start = ((bf16[128,8,128]{2,1,0:T(8,128)(2,1)}), bf16[128,8,128]{2,1,0:T(8,128)(2,1)S(1)}, u32[]{:S(2)}, u32[]{:S(2)}) async-start(bf16[128,8,128]{2,1,0:T(8,128)(2,1)} %bitcast.10), calls=%async_computation | async-start | bytes 524288 | tf_op jit(solution)/shard_map/all_to_all | solution.py:570
  26.6 7.5 %collective-permute-start = (bf16[48,256]{1,0:T(8,128)(2,1)S(1)}, bf16[48,256]{1,0:T(8,128)(2,1)S(1)}, u32[]{:S(2)}, u32[]{:S(2)}) collective-permute-start(bf16[48,256]{1,0:T(8,128)(2,1)S(1)} %get-tuple-element.39), channel_id=1, source_target_pairs={{1,2},{3,4},{5,6},{7,8},{9,10},{11,12},{13,14},{15,0},{2,1},{4,3},... | collective-permute-start | bytes 73736 | tf_op jit(solution)/shard_map/ppermute | solution.py:546
  28.3 5.9 %collective-permute-start.1 = (bf16[48,256]{1,0:T(8,128)(2,1)S(1)}, bf16[48,256]{1,0:T(8,128)(2,1)S(1)}, u32[]{:S(2)}, u32[]{:S(2)}) collective-permute-start(bf16[48,256]{1,0:T(8,128)(2,1)S(1)} %get-tuple-element.40), channel_id=1, source_target_pairs={{0,16},{32,48},{64,80},{96,112},{16,0},{48,32},{80,64},{112,96},{1... | collective-permute-start | bytes 73736 | tf_op jit(solution)/shard_map/ppermute | solution.py:546
  28.6 5.5 %collective-permute-start.2 = (bf16[48,256]{1,0:T(8,128)(2,1)S(1)}, bf16[48,256]{1,0:T(8,128)(2,1)S(1)}, u32[]{:S(2)}, u32[]{:S(2)}) collective-permute-start(bf16[48,256]{1,0:T(8,128)(2,1)S(1)} %get-tuple-element.41), channel_id=1, source_target_pairs={{16,32},{48,64},{80,96},{112,0},{32,16},{64,48},{96,80},{0,112},{1... | collective-permute-start | bytes 73736 | tf_op jit(solution)/shard_map/ppermute | solution.py:546
  29.5 4.7 %collective-permute-start.3 = (bf16[48,256]{1,0:T(8,128)(2,1)S(1)}, bf16[48,256]{1,0:T(8,128)(2,1)S(1)}, u32[]{:S(2)}, u32[]{:S(2)}) collective-permute-start(bf16[48,256]{1,0:T(8,128)(2,1)S(1)} %get-tuple-element.42), channel_id=1, source_target_pairs={{0,1},{2,3},{4,5},{6,7},{8,9},{10,11},{12,13},{14,15},{1,0},{3,2},... | collective-permute-start | bytes 73736 | tf_op jit(solution)/shard_map/ppermute | solution.py:546
  32.4 2.2 %copy-start.1 = (bf16[512,2048]{1,0:T(8,128)(2,1)S(1)}, bf16[512,2048]{1,0:T(8,128)(2,1)}, u32[]{:S(2)}) copy-start(bf16[512,2048]{1,0:T(8,128)(2,1)} %w_one_ref.3) | copy-start | bytes 6291460
  32.4 2.2 %copy-start.2 = (bf16[256,512]{1,0:T(8,128)(2,1)S(1)}, bf16[256,512]{1,0:T(8,128)(2,1)}, u32[]{:S(2)}) copy-start(bf16[256,512]{1,0:T(8,128)(2,1)} %cot_ref.5) | copy-start | bytes 786436
  37.4 7.0 %collective-permute-start.5 = (bf16[256,3072]{1,0:T(8,128)(2,1)S(1)}, bf16[256,3072]{1,0:T(8,128)(2,1)S(1)}, u32[]{:S(2)}, u32[]{:S(2)}) collective-permute-start(bf16[256,3072]{1,0:T(8,128)(2,1)S(1)} %get-tuple-element.59), channel_id=1, source_target_pairs={{0,1},{1,0},{2,3},{3,2},{4,5},{5,4},{6,7},{7,6},{8,9},{9,8},{10,11... | collective-permute-start | bytes 4718600 | tf_op jit(solution)/shard_map/ppermute | solution.py:553
  44.3 1.6 %collective-permute-start.4 = (bf16[64,16,128]{2,1,0:T(8,128)(2,1)S(1)}, bf16[64,16,128]{2,1,0:T(8,128)(2,1)S(1)}, u32[]{:S(2)}, u32[]{:S(2)}) collective-permute-start(bf16[64,16,128]{2,1,0:T(8,128)(2,1)S(1)} %get-tuple-element.56), channel_id=1, source_target_pairs={{0,1},{1,0},{2,3},{3,2},{4,5},{5,4},{6,7},{7,6},{8,9},{9,8},{10,11... | collective-permute-start | bytes 786440 | tf_op jit(solution)/shard_map/ppermute | solution.py:553
  83.3 39.1 %copy-start = (bf16[2048,512]{1,0:T(8,128)(2,1)S(1)}, bf16[2048,512]{1,0:T(8,128)(2,1)}, u32[]{:S(2)}) copy-start(bf16[2048,512]{1,0:T(8,128)(2,1)} %w_two_ref.1) | copy-start | bytes 6291460
  119.5 7.1 %collective-permute-start.6 = (bf16[64,9,16,128]{3,2,1,0:T(8,128)(2,1)S(1)}, bf16[64,9,16,128]{3,2,1,0:T(8,128)(2,1)S(1)}, u32[]{:S(2)}, u32[]{:S(2)}) collective-permute-start(bf16[64,9,16,128]{3,2,1,0:T(8,128)(2,1)S(1)} %all_to_all.16.in_ref.mine_ref), channel_id=1, source_target_pairs={{0,1},{1,0},{2,3},{3,2},{4,5},{5,4},{6,7},{7,6},{8,9},{9,8},{10,11... | collective-permute-start | bytes 7077896 | tf_op jit(solution)/shard_map/ppermute | solution.py:553

commit v9 on v8

--- a/solution.py
+++ b/solution.py
@@ -172,7 +172,7 @@
 
 
 def embed_kernel(
-    core_ref, odd_ref, got_ref, shelf_far, grid_ref, emb_ref, near_ref, place_ref, far_ref, one_ref, two_ref, by_ref,
+    core_ref, odd_ref, got_ref, shelf_far, grid_ref, near_ref, place_ref, far_ref, one_ref, two_ref, by_ref,
     wide_ref, rows_ref, weights_ref, pick_ref, strips_ref, sem,
 ):
     width, channels = near_ref.shape[0] - 80, near_ref.shape[1]
@@ -190,15 +190,16 @@
                 rows_ref[pl.ds(k * tiles + g, 16), pl.ds(half * LANE, LANE)] = jnp.concatenate(
                     two, axis=0
                 ).astype(BF16)
-    for fetch in fetches:
-        fetch.wait()
+    fetches[0].wait()
     gridded = dot(weights_ref[...], rows_ref[...]).astype(BF16)
     grid_ref[...] = gridded
+    fetches[1].wait()
     strips_ref[...] = dot(pick_ref[...], gridded).astype(BF16)
     core, odd = core_ref[0], odd_ref[0]
     for ref, k in ((far_ref, 3 - core), (one_ref, odd), (two_ref, 1 - odd), (by_ref, 2 + core)):
         ref[...] = strips_ref[strip_at(k), :]
-    emb_ref[...] = dot(gridded, near_ref[0:width]).astype(BF16)
+    for fetch in fetches[2:]:
+        fetch.wait()
 
 
 def tiles_of(part, two, one):
@@ -211,10 +212,11 @@
 
 
 def inner_kernel(
-    emb_ref, near_ref, d_act_far, field_ref, conv_ref, kern_ref, d_act_ref, sem
+    grid_ref, near_ref, d_act_far, emb_ref, field_ref, conv_ref, kern_ref, d_act_ref, sem
 ):
     width = near_ref.shape[0] - 80
     (fetch,) = start(sem, (d_act_far.at[pl.ds(0, CELLS), :], d_act_ref))
+    emb_ref[...] = dot(grid_ref[...], near_ref[0:width]).astype(BF16)
     taps = near_ref[width : width + 64].astype(F32)
     last = TAPS * TAPS - 1
     for h in range(2):
@@ -590,9 +592,9 @@
         60.5, tile_spin.reshape(1), interp[0], w_embed, taps_gain, w_two, cotangent,
         far=(1, 2, 3, 4, 5), far_outs=(0, 1), copies=9 + hidden // (2 * STEP),
     )
-    gridded, embedded, nearby, place, *strips = call(
+    gridded, nearby, place, *strips = call(
         embed_kernel,
-        [((CELLS, width), BF16), ((CELLS, channels), BF16), near, places] + [((STRIP, width), BF16)] * 4,
+        [((CELLS, width), BF16), near, places] + [((STRIP, width), BF16)] * 4,
         [((tiles * 8, LANE), F32), ((tiles * slots, width), BF16), stacked, picks, ((4 * STRIP, width), BF16)],
         16, core, odd, arrived.reshape(tiles * 8, LANE), shelved, far=(3,), copies=4,
     )
@@ -602,9 +604,9 @@
     blocks, cells = ((CELLS * 4, LANE), F32), ((CELLS, channels), F32)
     around = ((RING, channels), F32)
     step_sums = [((STEP, channels), F32), ((channels, hidden // 2), F32)]
-    field, conv, taps, d_active = call(
-        inner_kernel, [cells2, blocks, kernel, ((CELLS, hidden), F32)], [], 20,
-        embedded, nearby, d_active, far=(2,), copies=1,
+    embedded, field, conv, taps, d_active = call(
+        inner_kernel, [((CELLS, channels), BF16), cells2, blocks, kernel, ((CELLS, hidden), F32)], [], 20,
+        gridded, nearby, d_active, far=(2,), copies=1,
     )
     field, normal, inverse, scaled, active, d_hidden, theirs = call(
         forward_kernel,

time: 130 us -> 129 us (level)
  no operation moved by 1% of the time
where the time goes in v9:
time: 129 us
  blocking collectives  72.9 us (57%)
  Pallas kernels  24.1 us (19%)
  starting transfers between devices  21.8 us (17%)
  waiting for transfers between devices  5.64 us (4%)
  between operations  1.6 us (1%)
  other arithmetic  1.53 us (1%)
    all_to_all x1, blocking collectives, on_device(): paired = lax.all_to_all(paired, CHIPS, 0, 0, tiled=True)  36.7 us
    all_to_all x1, blocking collectives, on_device(): here = lax.all_to_all(summed, CHIPS, 0, 0, tiled=True)  36.2 us
    pallas_call x11, Pallas kernels, call(): pl.pallas_call(kernel, out_shape=[jax.ShapeDtypeStruct(s, d) for s, d in...  24.1 us
    all_to_all x1, starting transfers between devices, on_device(): lax.all_to_all(leaving.reshape(tiles, 8, LANE), ALL, 0, 0, tiled=True)  11.5 us
    ppermute x4, starting transfers between devices, between(): return lax.ppermute(value, axes, pairs + [(j, i) for i, j in pairs])  5.76 us
    ppermute x3, starting transfers between devices, swap(): return lax.ppermute(value, 'core', [(0, 1), (1, 0)])  4.58 us
    all_to_all x1, waiting for transfers between devices, on_device(): lax.all_to_all(leaving.reshape(tiles, 8, LANE), ALL, 0, 0, tiled=True)  4.1 us
  transfers between devices with their start and end apart: 8, of which 3 were waited for; matrix products, arithmetic and copies ran while one was open for 2% of the time, Pallas kernels for 12%

profile of v9, /device:TPU:1, one launch (start us, length us, event | category | flops | bytes accessed | tf_op | source)
XLA Modules:
  0.0 128.8 jit_solution(10642334141797803583)
XLA Ops:
  0.6 1.9 %shard_map.145 = bf16[1024,128]{1,0:T(8,128)(2,1)} custom-call(s32[1]{0:T(128)} %bitcast.core_ref, s32[1]{0:T(128)} %bitcast.1.odd_ref, s32[1,256]{1,0:T(1,128)} %bitcast.12, bf16[256,256]{1,0:T(8,128)(2,1)} %obs_far.1), custom_call_target="tpu_custom_call" | custom-call | tf_op jit(solution)/shard_map/pallas_call | solution.py:39
  2.6 11.5 %all-to-all-start = ((bf16[128,8,128]{2,1,0:T(8,128)(2,1)}), bf16[128,8,128]{2,1,0:T(8,128)(2,1)S(1)}, u32[]{:S(2)}, u32[]{:S(2)}) async-start(bf16[128,8,128]{2,1,0:T(8,128)(2,1)} %bitcast.10), calls=%async_computation | async-start | bytes 524288 | tf_op jit(solution)/shard_map/all_to_all | solution.py:572
  14.8 0.7 broadcast_in_dim.7
  15.5 1.5 %pad_maximum_fusion.small_far = bf16[80,512]{1,0:T(8,128)(2,1)} fusion(bf16[16,512]{1,0:T(8,128)(2,1)S(1)} %broadcast_in_dim.7, bf16[49,512]{1,0:T(8,128)(2,1)} %param.15, bf16[80]{0:T(256)(128)(2,1)S(1)} %pad.1.clone), kind=kLoop, calls=%fused_computation | loop fusion | flops 245760 | bytes 148640 | tf_op jit(solution)/shard_map/concatenate | solution.py:575
  17.1 3.7 %shard_map.146 = (bf16[65536,512]{1,0:T(8,128)(2,1)}, f32[8192,2048]{1,0:T(8,128)}) custom-call(s32[1]{0:T(128)} %bitcast.8.spin_ref, bf16[128,4,256]{2,1,0:T(4,128)(2,1)} %bitcast.11, bf16[256,512]{1,0:T(8,128)(2,1)} %w_embed_far.1, bf16[80,512]{1,0:T(8,128)(2,1)} %pad_maximum_fusion.small_far, bf16[2048,512]{1,0:T(8,128)(2,1)} %w_two_ref.1, ...), custom_call_target="tpu_custom_call" | custom-call | tf_op jit(solution)/shard_map/pallas_call | solution.py:39
  20.8 4.1 %all-to-all-done = bf16[128,8,128]{2,1,0:T(8,128)(2,1)S(1)} async-done(((bf16[128,8,128]{2,1,0:T(8,128)(2,1)}), bf16[128,8,128]{2,1,0:T(8,128)(2,1)S(1)}, u32[]{:S(2)}, u32[]{:S(2)}) %all-to-all-start) | async-done | bytes 262176 | tf_op jit(solution)/shard_map/all_to_all | solution.py:572
  24.9 1.4 %shard_map.147 = (bf16[256,256]{1,0:T(8,128)(2,1)S(1)}, bf16[336,512]{1,0:T(8,128)(2,1)S(1)}, bf16[400,256]{1,0:T(8,128)(2,1)S(1)}, bf16[48,256]{1,0:T(8,128)(2,...) custom-call(s32[1]{0:T(128)} %bitcast.core_ref, s32[1]{0:T(128)} %bitcast.1.odd_ref, ...), custom_call_target="tpu_custom_call" | custom-call | tf_op jit(solution)/shard_map/pallas_call | solution.py:39
  26.3 1.7 %collective-permute-start = (bf16[48,256]{1,0:T(8,128)(2,1)S(1)}, bf16[48,256]{1,0:T(8,128)(2,1)S(1)}, u32[]{:S(2)}, u32[]{:S(2)}) collective-permute-start(bf16[48,256]{1,0:T(8,128)(2,1)S(1)} %get-tuple-element.39), channel_id=1, source_target_pairs={{1,2},{3,4},{5,6},{7,8},{9,10},{11,12},{13,14},{15,0},{2,1},{4,3},... | collective-permute-start | bytes 73736 | tf_op jit(solution)/shard_map/ppermute | solution.py:548
  28.0 0.3 collective-permute-start.1
  28.3 0.9 collective-permute-start.2
  29.2 2.9 %collective-permute-start.3 = (bf16[48,256]{1,0:T(8,128)(2,1)S(1)}, bf16[48,256]{1,0:T(8,128)(2,1)S(1)}, u32[]{:S(2)}, u32[]{:S(2)}) collective-permute-start(bf16[48,256]{1,0:T(8,128)(2,1)S(1)} %get-tuple-element.42), channel_id=1, source_target_pairs={{0,1},{2,3},{4,5},{6,7},{8,9},{10,11},{12,13},{14,15},{1,0},{3,2},... | collective-permute-start | bytes 73736 | tf_op jit(solution)/shard_map/ppermute | solution.py:548
  32.1 1.8 %shard_map.148 = (bf16[256,512]{1,0:T(8,128)(2,1)S(1)}, f32[2688,128]{1,0:T(8,128)S(1)}, f32[1024,128]{1,0:T(8,128)S(1)}, f32[392,128]{1,0:T(8,128)S(1)}, f32[256,2048]{1,0:T(8,128)S(1)}) custom-call(bf16[256,256]{1,0:T(8,128)(2,1)S(1)} %get-tuple-element.38.grid_ref, bf16[336,512]{1,0:T(8,128)(2,1)S(1)} %get-tuple-element.44.near_ref, ...), custom_call_target="tpu_custom_call" | custom-call | tf_op jit(solution)/shard_map/pallas_call | solution.py:39
  33.9 0.4 copy-done.1
  34.3 2.8 %shard_map.149 = (f32[2688,128]{1,0:T(8,128)S(1)}, f32[256,512]{1,0:T(8,128)S(1)}, f32[256,128]{1,0:T(8,128)S(1)}, bf16[256,512]{1,0:T(8,128)(2,1)S(1)}, bf16[25...) custom-call(s32[1]{0:T(128)} %bitcast.core_ref, s32[1]{0:T(128)} %bitcast.1.odd_ref, ...), custom_call_target="tpu_custom_call" | custom-call | tf_op jit(solution)/shard_map/pallas_call | solution.py:39
  37.1 1.6 %collective-permute-start.5 = (bf16[256,3072]{1,0:T(8,128)(2,1)S(1)}, bf16[256,3072]{1,0:T(8,128)(2,1)S(1)}, u32[]{:S(2)}, u32[]{:S(2)}) collective-permute-start(bf16[256,3072]{1,0:T(8,128)(2,1)S(1)} %get-tuple-element.58), channel_id=1, source_target_pairs={{0,1},{1,0},{2,3},{3,2},{4,5},{5,4},{6,7},{7,6},{8,9},{9,8},{10,11... | collective-permute-start | bytes 4718600 | tf_op jit(solution)/shard_map/ppermute | solution.py:555
  38.7 5.3 %shard_map.150 = (f32[64,16,128]{2,1,0:T(8,128)S(1)}, bf16[64,16,128]{2,1,0:T(8,128)(2,1)S(1)}) custom-call(s32[1]{0:T(128)} %bitcast.core_ref, s32[1]{0:T(128)} %bitcast.1.odd_ref, bf16[256,256]{1,0:T(8,128)(2,1)S(1)} %get-tuple-element.38.grid_ref, bf16[48,256]{1,0:T(8,128)(2,1)S(1)} %collective-permute-done.s0, ...), custom_call_target="tpu_custom_call" | custom-call | tf_op jit(solution)/shard_map/pallas_call | solution.py:39
  44.1 1.3 %shard_map.151.paired_far = bf16[64,9,16,128]{3,2,1,0:T(8,128)(2,1)S(1)} custom-call(s32[1]{0:T(128)} %bitcast.core_ref, bf16[256,512]{1,0:T(8,128)(2,1)S(1)} %get-tuple-element.56.scaled_ref, bf16[256,2048]{1,0:T(8,128)(2,1)S(1)} %get-tuple-element.57.active_ref, bf16[256,2048]{1,0:T(8,128)(2,1)S(1)} %get-tuple-element.53.d_hid_ref, ...), custom_call_target="tpu_custom_call" | custom-call | tf_op jit(solution)/shard_map/pallas_call | solution.py:39
  45.7 36.7 %all_to_all.15.in_ref = bf16[64,9,16,128]{3,2,1,0:T(8,128)(2,1)S(1)} all-to-all(bf16[64,9,16,128]{3,2,1,0:T(8,128)(2,1)S(1)} %shard_map.152), channel_id=1, replica_groups=mesh['face'=8,'col'=8,'core'=2] {'face','col'}, dimensions={0} | all-to-all | bytes 4718592 | tf_op jit(solution)/shard_map/all_to_all | solution.py:644
  82.4 0.6 shard_map.153
  83.0 36.2 %all_to_all.16.in_ref.mine_ref = bf16[64,9,16,128]{3,2,1,0:T(8,128)(2,1)S(1)} all-to-all(bf16[64,9,16,128]{3,2,1,0:T(8,128)(2,1)S(1)} %shard_map.153), channel_id=1, replica_groups=mesh['face'=8,'col'=8,'core'=2] {'face','col'}, dimensions={0} | all-to-all | bytes 4718592 | tf_op jit(solution)/shard_map/all_to_all | solution.py:646
  119.2 2.9 %collective-permute-start.6 = (bf16[64,9,16,128]{3,2,1,0:T(8,128)(2,1)S(1)}, bf16[64,9,16,128]{3,2,1,0:T(8,128)(2,1)S(1)}, u32[]{:S(2)}, u32[]{:S(2)}) collective-permute-start(bf16[64,9,16,128]{3,2,1,0:T(8,128)(2,1)S(1)} %all_to_all.16.in_ref.mine_ref), channel_id=1, source_target_pairs={{0,1},{1,0},{2,3},{3,2},{4,5},{5,4},{6,7},{7,6},{8,9},{9,8},{10,11... | collective-permute-start | bytes 7077896 | tf_op jit(solution)/shard_map/ppermute | solution.py:555
  122.2 2.8 %shard_map.154 = (f32[512,2048]{1,0:T(8,128)}, f32[2048,512]{1,0:T(8,128)}, bf16[256,512]{1,0:T(8,128)(2,1)}) custom-call(s32[1]{0:T(128)} %bitcast.core_ref, bf16[64,9,16,128]{3,2,1,0:T(8,128)(2,1)S(1)} %all_to_all.16.in_ref.mine_ref, bf16[256,512]{1,0:T(8,128)(2,1)S(1)} %get-tuple-element.59.emb_ref, bf16[256,2048]{1,0:T(8,128)(2,1)S(1)} %get-tuple-element.57.active_ref, ...), custom_call_target="tpu_custom_call" | custom-call | tf_op jit(solution)/shard_map/pallas_call | solution.py:39
  125.0 1.3 %collective-permute-done.6.in_ref = bf16[64,9,16,128]{3,2,1,0:T(8,128)(2,1)S(1)} collective-permute-done((bf16[64,9,16,128]{3,2,1,0:T(8,128)(2,1)S(1)}, bf16[64,9,16,128]{3,2,1,0:T(8,128)(2,1)S(1)}, u32[]{:S(2)}, u32[]{:S(2)}) %collective-permute-start.6) | collective-permute-done | bytes 2359328 | tf_op jit(solution)/shard_map/ppermute | solution.py:555
  126.3 2.4 %shard_map.155 = (f32[512,2048]{1,0:T(8,128)}, f32[2048,512]{1,0:T(8,128)}, f32[256,512]{1,0:T(8,128)}, f32[49,512]{1,0:T(8,128)}, f32[1,512]{1,0:T(1,128)}) custom-call(s32[1]{0:T(128)} %bitcast.core_ref, bf16[64,9,16,128]{3,2,1,0:T(8,128)(2,1)S(1)} %collective-permute-done.6.in_ref, ...), custom_call_target="tpu_custom_call", output_to_operand_aliasing={{0}: (3, {}), {1}: (4, {})} | custom-call | tf_op jit(solution)/shard_map/pallas_call | solution.py:39
  (15 shorter events, 0.5 us)
Async XLA Ops:
  2.6 22.3 %all-to-all-start = ((bf16[128,8,128]{2,1,0:T(8,128)(2,1)}), bf16[128,8,128]{2,1,0:T(8,128)(2,1)S(1)}, u32[]{:S(2)}, u32[]{:S(2)}) async-start(bf16[128,8,128]{2,1,0:T(8,128)(2,1)} %bitcast.10), calls=%async_computation | async-start | bytes 524288 | tf_op jit(solution)/shard_map/all_to_all | solution.py:572
  26.3 7.5 %collective-permute-start = (bf16[48,256]{1,0:T(8,128)(2,1)S(1)}, bf16[48,256]{1,0:T(8,128)(2,1)S(1)}, u32[]{:S(2)}, u32[]{:S(2)}) collective-permute-start(bf16[48,256]{1,0:T(8,128)(2,1)S(1)} %get-tuple-element.39), channel_id=1, source_target_pairs={{1,2},{3,4},{5,6},{7,8},{9,10},{11,12},{13,14},{15,0},{2,1},{4,3},... | collective-permute-start | bytes 73736 | tf_op jit(solution)/shard_map/ppermute | solution.py:548
  28.0 5.9 %collective-permute-start.1 = (bf16[48,256]{1,0:T(8,128)(2,1)S(1)}, bf16[48,256]{1,0:T(8,128)(2,1)S(1)}, u32[]{:S(2)}, u32[]{:S(2)}) collective-permute-start(bf16[48,256]{1,0:T(8,128)(2,1)S(1)} %get-tuple-element.40), channel_id=1, source_target_pairs={{0,16},{32,48},{64,80},{96,112},{16,0},{48,32},{80,64},{112,96},{1... | collective-permute-start | bytes 73736 | tf_op jit(solution)/shard_map/ppermute | solution.py:548
  28.3 5.6 %collective-permute-start.2 = (bf16[48,256]{1,0:T(8,128)(2,1)S(1)}, bf16[48,256]{1,0:T(8,128)(2,1)S(1)}, u32[]{:S(2)}, u32[]{:S(2)}) collective-permute-start(bf16[48,256]{1,0:T(8,128)(2,1)S(1)} %get-tuple-element.41), channel_id=1, source_target_pairs={{16,32},{48,64},{80,96},{112,0},{32,16},{64,48},{96,80},{0,112},{1... | collective-permute-start | bytes 73736 | tf_op jit(solution)/shard_map/ppermute | solution.py:548
  29.2 4.7 %collective-permute-start.3 = (bf16[48,256]{1,0:T(8,128)(2,1)S(1)}, bf16[48,256]{1,0:T(8,128)(2,1)S(1)}, u32[]{:S(2)}, u32[]{:S(2)}) collective-permute-start(bf16[48,256]{1,0:T(8,128)(2,1)S(1)} %get-tuple-element.42), channel_id=1, source_target_pairs={{0,1},{2,3},{4,5},{6,7},{8,9},{10,11},{12,13},{14,15},{1,0},{3,2},... | collective-permute-start | bytes 73736 | tf_op jit(solution)/shard_map/ppermute | solution.py:548
  32.1 2.2 %copy-start.1 = (bf16[512,2048]{1,0:T(8,128)(2,1)S(1)}, bf16[512,2048]{1,0:T(8,128)(2,1)}, u32[]{:S(2)}) copy-start(bf16[512,2048]{1,0:T(8,128)(2,1)} %w_one_ref.3) | copy-start | bytes 6291460
  32.1 2.2 %copy-start.2 = (bf16[256,512]{1,0:T(8,128)(2,1)S(1)}, bf16[256,512]{1,0:T(8,128)(2,1)}, u32[]{:S(2)}) copy-start(bf16[256,512]{1,0:T(8,128)(2,1)} %cot_ref.5) | copy-start | bytes 786436
  37.1 7.0 %collective-permute-start.5 = (bf16[256,3072]{1,0:T(8,128)(2,1)S(1)}, bf16[256,3072]{1,0:T(8,128)(2,1)S(1)}, u32[]{:S(2)}, u32[]{:S(2)}) collective-permute-start(bf16[256,3072]{1,0:T(8,128)(2,1)S(1)} %get-tuple-element.58), channel_id=1, source_target_pairs={{0,1},{1,0},{2,3},{3,2},{4,5},{5,4},{6,7},{7,6},{8,9},{9,8},{10,11... | collective-permute-start | bytes 4718600 | tf_op jit(solution)/shard_map/ppermute | solution.py:555
  44.0 1.6 %collective-permute-start.4 = (bf16[64,16,128]{2,1,0:T(8,128)(2,1)S(1)}, bf16[64,16,128]{2,1,0:T(8,128)(2,1)S(1)}, u32[]{:S(2)}, u32[]{:S(2)}) collective-permute-start(bf16[64,16,128]{2,1,0:T(8,128)(2,1)S(1)} %get-tuple-element.55), channel_id=1, source_target_pairs={{0,1},{1,0},{2,3},{3,2},{4,5},{5,4},{6,7},{7,6},{8,9},{9,8},{10,11... | collective-permute-start | bytes 786440 | tf_op jit(solution)/shard_map/ppermute | solution.py:555
  83.0 39.1 %copy-start = (bf16[2048,512]{1,0:T(8,128)(2,1)S(1)}, bf16[2048,512]{1,0:T(8,128)(2,1)}, u32[]{:S(2)}) copy-start(bf16[2048,512]{1,0:T(8,128)(2,1)} %w_two_ref.1) | copy-start | bytes 6291460
  119.2 7.1 %collective-permute-start.6 = (bf16[64,9,16,128]{3,2,1,0:T(8,128)(2,1)S(1)}, bf16[64,9,16,128]{3,2,1,0:T(8,128)(2,1)S(1)}, u32[]{:S(2)}, u32[]{:S(2)}) collective-permute-start(bf16[64,9,16,128]{3,2,1,0:T(8,128)(2,1)S(1)} %all_to_all.16.in_ref.mine_ref), channel_id=1, source_target_pairs={{0,1},{1,0},{2,3},{3,2},{4,5},{5,4},{6,7},{7,6},{8,9},{9,8},{10,11... | collective-permute-start | bytes 7077896 | tf_op jit(solution)/shard_map/ppermute | solution.py:555

commit v10 on v9

--- a/solution.py
+++ b/solution.py
@@ -76,9 +76,11 @@
 
 def route_kernel(core_ref, odd_ref, row_far, obs_far, out_ref, row_ref, obs_ref, sem):
     fetch_row, fetch_obs = start(sem, (row_far, row_ref), (obs_far, obs_ref))
+    count, lines = row_ref.shape[1], out_ref.shape[0]
+    line = lax.broadcasted_iota(jnp.int32, (lines, count), 0)
+    line = line - (line & 4)
     fetch_row.wait()
     row = row_ref[...]
-    count = row.shape[1]
     across = jnp.broadcast_to(row, (count, count)).astype(F32)
     earlier = lax.broadcasted_iota(jnp.int32, (count, count), 0) < lax.broadcasted_iota(
         jnp.int32, (count, count), 1
@@ -86,9 +88,7 @@
     same = jnp.where((across.T == across) & earlier, 1.0, 0.0)
     rank = jnp.sum(same, axis=0, keepdims=True).astype(jnp.int32)
     place = row * 8 + rank
-    lines = out_ref.shape[0]
-    line = lax.broadcasted_iota(jnp.int32, (lines, count), 0)
-    chosen = jnp.where((line - (line & 4)) == place, 1.0, 0.0).astype(BF16)
+    chosen = jnp.where(line == place, 1.0, 0.0).astype(BF16)
     fetch_obs.wait()
     moved = dot(chosen, obs_ref[...])
     first = (lax.broadcasted_iota(jnp.int32, (lines, LANE), 0) & 4) == 0
@@ -258,7 +258,9 @@
     take_strips(core_ref[0], odd_ref[0], (s0, s1, s2, s3), strips_ref)
     halo = dot(strips_ref[...], near_ref[0:width]).astype(BF16)
     ring_ref[...] = dot(place_ref[:, : 4 * STRIP], halo)
-    field_ref[...] = own_ref[...]
+    for x in range(ROWS2):
+        own = pl.ds((x * PITCH + HALO) * 8, SIDE * 8)
+        field_ref[own, :] = own_ref[own, :]
     for at, x, y in ring():
         skip, count = (0, 8) if x in OUTER else (0, HALO) if y == 0 else (HALO, HALO)
         for cb in range(4):
@@ -436,7 +438,7 @@
     def add(d, sums):
         return [s + in_ref[d, t].astype(F32) for t, s in enumerate(sums)]
 
-    sums = lax.fori_loop(0, parts, add, [jnp.zeros(in_ref.shape[2:], F32)] * tiles, unroll=4)
+    sums = lax.fori_loop(0, parts, add, [jnp.zeros(in_ref.shape[2:], F32)] * tiles, unroll=8)
     sums = [s.astype(BF16) for s in sums]
 
     def spread(d, carry):
@@ -444,7 +446,7 @@
             out_ref[d, t] = sums[t]
         return carry
 
-    lax.fori_loop(0, parts, spread, 0, unroll=4)
+    lax.fori_loop(0, parts, spread, 0, unroll=8)
 
 
 def assemble_half(core, in_ref, one_far, two_far, one_ref, two_ref, sem):

time: 129 us -> 129 us (level)
  no operation moved by 1% of the time
where the time goes in v10:
time: 129 us
  blocking collectives  72.9 us (57%)
  Pallas kernels  24 us (19%)
  starting transfers between devices  21.8 us (17%)
  waiting for transfers between devices  5.64 us (4%)
  between operations  1.6 us (1%)
  other arithmetic  1.53 us (1%)
    all_to_all x1, blocking collectives, on_device(): paired = lax.all_to_all(paired, CHIPS, 0, 0, tiled=True)  36.7 us
    all_to_all x1, blocking collectives, on_device(): here = lax.all_to_all(summed, CHIPS, 0, 0, tiled=True)  36.2 us
    pallas_call x11, Pallas kernels, call(): pl.pallas_call(kernel, out_shape=[jax.ShapeDtypeStruct(s, d) for s, d in...  24 us
    all_to_all x1, starting transfers between devices, on_device(): lax.all_to_all(leaving.reshape(tiles, 8, LANE), ALL, 0, 0, tiled=True)  11.5 us
    ppermute x4, starting transfers between devices, between(): return lax.ppermute(value, axes, pairs + [(j, i) for i, j in pairs])  5.76 us
    ppermute x3, starting transfers between devices, swap(): return lax.ppermute(value, 'core', [(0, 1), (1, 0)])  4.58 us
    all_to_all x1, waiting for transfers between devices, on_device(): lax.all_to_all(leaving.reshape(tiles, 8, LANE), ALL, 0, 0, tiled=True)  4.1 us
  transfers between devices with their start and end apart: 8, of which 3 were waited for; matrix products, arithmetic and copies ran while one was open for 2% of the time, Pallas kernels for 12%

profile of v10, /device:TPU:1, one launch (start us, length us, event | category | flops | bytes accessed | tf_op | source)
XLA Modules:
  0.0 128.8 jit_solution(9323423286991242540)
XLA Ops:
  0.6 1.9 %shard_map.145 = bf16[1024,128]{1,0:T(8,128)(2,1)} custom-call(s32[1]{0:T(128)} %bitcast.core_ref, s32[1]{0:T(128)} %bitcast.1.odd_ref, s32[1,256]{1,0:T(1,128)} %bitcast.12, bf16[256,256]{1,0:T(8,128)(2,1)} %obs_far.1), custom_call_target="tpu_custom_call" | custom-call | tf_op jit(solution)/shard_map/pallas_call | solution.py:39
  2.6 11.5 %all-to-all-start = ((bf16[128,8,128]{2,1,0:T(8,128)(2,1)}), bf16[128,8,128]{2,1,0:T(8,128)(2,1)S(1)}, u32[]{:S(2)}, u32[]{:S(2)}) async-start(bf16[128,8,128]{2,1,0:T(8,128)(2,1)} %bitcast.10), calls=%async_computation | async-start | bytes 524288 | tf_op jit(solution)/shard_map/all_to_all | solution.py:574
  14.8 0.7 broadcast_in_dim.7
  15.5 1.5 %pad_maximum_fusion.small_far = bf16[80,512]{1,0:T(8,128)(2,1)} fusion(bf16[16,512]{1,0:T(8,128)(2,1)S(1)} %broadcast_in_dim.7, bf16[49,512]{1,0:T(8,128)(2,1)} %param.15, bf16[80]{0:T(256)(128)(2,1)S(1)} %pad.1.clone), kind=kLoop, calls=%fused_computation | loop fusion | flops 245760 | bytes 148640 | tf_op jit(solution)/shard_map/concatenate | solution.py:577
  17.1 3.7 %shard_map.146 = (bf16[65536,512]{1,0:T(8,128)(2,1)}, f32[8192,2048]{1,0:T(8,128)}) custom-call(s32[1]{0:T(128)} %bitcast.8.spin_ref, bf16[128,4,256]{2,1,0:T(4,128)(2,1)} %bitcast.11, bf16[256,512]{1,0:T(8,128)(2,1)} %w_embed_far.1, bf16[80,512]{1,0:T(8,128)(2,1)} %pad_maximum_fusion.small_far, bf16[2048,512]{1,0:T(8,128)(2,1)} %w_two_ref.1, ...), custom_call_target="tpu_custom_call" | custom-call | tf_op jit(solution)/shard_map/pallas_call | solution.py:39
  20.8 4.1 %all-to-all-done = bf16[128,8,128]{2,1,0:T(8,128)(2,1)S(1)} async-done(((bf16[128,8,128]{2,1,0:T(8,128)(2,1)}), bf16[128,8,128]{2,1,0:T(8,128)(2,1)S(1)}, u32[]{:S(2)}, u32[]{:S(2)}) %all-to-all-start) | async-done | bytes 262176 | tf_op jit(solution)/shard_map/all_to_all | solution.py:574
  24.9 1.4 %shard_map.147 = (bf16[256,256]{1,0:T(8,128)(2,1)S(1)}, bf16[336,512]{1,0:T(8,128)(2,1)S(1)}, bf16[400,256]{1,0:T(8,128)(2,1)S(1)}, bf16[48,256]{1,0:T(8,128)(2,...) custom-call(s32[1]{0:T(128)} %bitcast.core_ref, s32[1]{0:T(128)} %bitcast.1.odd_ref, ...), custom_call_target="tpu_custom_call" | custom-call | tf_op jit(solution)/shard_map/pallas_call | solution.py:39
  26.3 1.7 %collective-permute-start = (bf16[48,256]{1,0:T(8,128)(2,1)S(1)}, bf16[48,256]{1,0:T(8,128)(2,1)S(1)}, u32[]{:S(2)}, u32[]{:S(2)}) collective-permute-start(bf16[48,256]{1,0:T(8,128)(2,1)S(1)} %get-tuple-element.39), channel_id=1, source_target_pairs={{1,2},{3,4},{5,6},{7,8},{9,10},{11,12},{13,14},{15,0},{2,1},{4,3},... | collective-permute-start | bytes 73736 | tf_op jit(solution)/shard_map/ppermute | solution.py:550
  28.0 0.3 collective-permute-start.1
  28.3 0.9 collective-permute-start.2
  29.2 2.9 %collective-permute-start.3 = (bf16[48,256]{1,0:T(8,128)(2,1)S(1)}, bf16[48,256]{1,0:T(8,128)(2,1)S(1)}, u32[]{:S(2)}, u32[]{:S(2)}) collective-permute-start(bf16[48,256]{1,0:T(8,128)(2,1)S(1)} %get-tuple-element.42), channel_id=1, source_target_pairs={{0,1},{2,3},{4,5},{6,7},{8,9},{10,11},{12,13},{14,15},{1,0},{3,2},... | collective-permute-start | bytes 73736 | tf_op jit(solution)/shard_map/ppermute | solution.py:550
  32.1 1.8 %shard_map.148 = (bf16[256,512]{1,0:T(8,128)(2,1)S(1)}, f32[2688,128]{1,0:T(8,128)S(1)}, f32[1024,128]{1,0:T(8,128)S(1)}, f32[392,128]{1,0:T(8,128)S(1)}, f32[256,2048]{1,0:T(8,128)S(1)}) custom-call(bf16[256,256]{1,0:T(8,128)(2,1)S(1)} %get-tuple-element.38.grid_ref, bf16[336,512]{1,0:T(8,128)(2,1)S(1)} %get-tuple-element.44.near_ref, ...), custom_call_target="tpu_custom_call" | custom-call | tf_op jit(solution)/shard_map/pallas_call | solution.py:39
  33.9 0.4 copy-done.1
  34.3 2.8 %shard_map.149 = (f32[2688,128]{1,0:T(8,128)S(1)}, f32[256,512]{1,0:T(8,128)S(1)}, f32[256,128]{1,0:T(8,128)S(1)}, bf16[256,512]{1,0:T(8,128)(2,1)S(1)}, bf16[25...) custom-call(s32[1]{0:T(128)} %bitcast.core_ref, s32[1]{0:T(128)} %bitcast.1.odd_ref, ...), custom_call_target="tpu_custom_call" | custom-call | tf_op jit(solution)/shard_map/pallas_call | solution.py:39
  37.1 1.6 %collective-permute-start.5 = (bf16[256,3072]{1,0:T(8,128)(2,1)S(1)}, bf16[256,3072]{1,0:T(8,128)(2,1)S(1)}, u32[]{:S(2)}, u32[]{:S(2)}) collective-permute-start(bf16[256,3072]{1,0:T(8,128)(2,1)S(1)} %get-tuple-element.58), channel_id=1, source_target_pairs={{0,1},{1,0},{2,3},{3,2},{4,5},{5,4},{6,7},{7,6},{8,9},{9,8},{10,11... | collective-permute-start | bytes 4718600 | tf_op jit(solution)/shard_map/ppermute | solution.py:557
  38.7 5.3 %shard_map.150 = (f32[64,16,128]{2,1,0:T(8,128)S(1)}, bf16[64,16,128]{2,1,0:T(8,128)(2,1)S(1)}) custom-call(s32[1]{0:T(128)} %bitcast.core_ref, s32[1]{0:T(128)} %bitcast.1.odd_ref, bf16[256,256]{1,0:T(8,128)(2,1)S(1)} %get-tuple-element.38.grid_ref, bf16[48,256]{1,0:T(8,128)(2,1)S(1)} %collective-permute-done.s0, ...), custom_call_target="tpu_custom_call" | custom-call | tf_op jit(solution)/shard_map/pallas_call | solution.py:39
  44.1 1.3 %shard_map.151.paired_far = bf16[64,9,16,128]{3,2,1,0:T(8,128)(2,1)S(1)} custom-call(s32[1]{0:T(128)} %bitcast.core_ref, bf16[256,512]{1,0:T(8,128)(2,1)S(1)} %get-tuple-element.56.scaled_ref, bf16[256,2048]{1,0:T(8,128)(2,1)S(1)} %get-tuple-element.57.active_ref, bf16[256,2048]{1,0:T(8,128)(2,1)S(1)} %get-tuple-element.53.d_hid_ref, ...), custom_call_target="tpu_custom_call" | custom-call | tf_op jit(solution)/shard_map/pallas_call | solution.py:39
  45.7 36.7 %all_to_all.15.in_ref = bf16[64,9,16,128]{3,2,1,0:T(8,128)(2,1)S(1)} all-to-all(bf16[64,9,16,128]{3,2,1,0:T(8,128)(2,1)S(1)} %shard_map.152), channel_id=1, replica_groups=mesh['face'=8,'col'=8,'core'=2] {'face','col'}, dimensions={0} | all-to-all | bytes 4718592 | tf_op jit(solution)/shard_map/all_to_all | solution.py:646
  82.4 0.5 shard_map.153
  83.0 36.2 %all_to_all.16.in_ref.mine_ref = bf16[64,9,16,128]{3,2,1,0:T(8,128)(2,1)S(1)} all-to-all(bf16[64,9,16,128]{3,2,1,0:T(8,128)(2,1)S(1)} %shard_map.153), channel_id=1, replica_groups=mesh['face'=8,'col'=8,'core'=2] {'face','col'}, dimensions={0} | all-to-all | bytes 4718592 | tf_op jit(solution)/shard_map/all_to_all | solution.py:648
  119.1 2.9 %collective-permute-start.6 = (bf16[64,9,16,128]{3,2,1,0:T(8,128)(2,1)S(1)}, bf16[64,9,16,128]{3,2,1,0:T(8,128)(2,1)S(1)}, u32[]{:S(2)}, u32[]{:S(2)}) collective-permute-start(bf16[64,9,16,128]{3,2,1,0:T(8,128)(2,1)S(1)} %all_to_all.16.in_ref.mine_ref), channel_id=1, source_target_pairs={{0,1},{1,0},{2,3},{3,2},{4,5},{5,4},{6,7},{7,6},{8,9},{9,8},{10,11... | collective-permute-start | bytes 7077896 | tf_op jit(solution)/shard_map/ppermute | solution.py:557
  122.1 2.8 %shard_map.154 = (f32[512,2048]{1,0:T(8,128)}, f32[2048,512]{1,0:T(8,128)}, bf16[256,512]{1,0:T(8,128)(2,1)}) custom-call(s32[1]{0:T(128)} %bitcast.core_ref, bf16[64,9,16,128]{3,2,1,0:T(8,128)(2,1)S(1)} %all_to_all.16.in_ref.mine_ref, bf16[256,512]{1,0:T(8,128)(2,1)S(1)} %get-tuple-element.59.emb_ref, bf16[256,2048]{1,0:T(8,128)(2,1)S(1)} %get-tuple-element.57.active_ref, ...), custom_call_target="tpu_custom_call" | custom-call | tf_op jit(solution)/shard_map/pallas_call | solution.py:39
  124.9 1.3 %collective-permute-done.6.in_ref = bf16[64,9,16,128]{3,2,1,0:T(8,128)(2,1)S(1)} collective-permute-done((bf16[64,9,16,128]{3,2,1,0:T(8,128)(2,1)S(1)}, bf16[64,9,16,128]{3,2,1,0:T(8,128)(2,1)S(1)}, u32[]{:S(2)}, u32[]{:S(2)}) %collective-permute-start.6) | collective-permute-done | bytes 2359328 | tf_op jit(solution)/shard_map/ppermute | solution.py:557
  126.2 2.4 %shard_map.155 = (f32[512,2048]{1,0:T(8,128)}, f32[2048,512]{1,0:T(8,128)}, f32[256,512]{1,0:T(8,128)}, f32[49,512]{1,0:T(8,128)}, f32[1,512]{1,0:T(1,128)}) custom-call(s32[1]{0:T(128)} %bitcast.core_ref, bf16[64,9,16,128]{3,2,1,0:T(8,128)(2,1)S(1)} %collective-permute-done.6.in_ref, ...), custom_call_target="tpu_custom_call", output_to_operand_aliasing={{0}: (3, {}), {1}: (4, {})} | custom-call | tf_op jit(solution)/shard_map/pallas_call | solution.py:39
  (15 shorter events, 0.5 us)
Async XLA Ops:
  2.6 22.3 %all-to-all-start = ((bf16[128,8,128]{2,1,0:T(8,128)(2,1)}), bf16[128,8,128]{2,1,0:T(8,128)(2,1)S(1)}, u32[]{:S(2)}, u32[]{:S(2)}) async-start(bf16[128,8,128]{2,1,0:T(8,128)(2,1)} %bitcast.10), calls=%async_computation | async-start | bytes 524288 | tf_op jit(solution)/shard_map/all_to_all | solution.py:574
  26.3 7.5 %collective-permute-start = (bf16[48,256]{1,0:T(8,128)(2,1)S(1)}, bf16[48,256]{1,0:T(8,128)(2,1)S(1)}, u32[]{:S(2)}, u32[]{:S(2)}) collective-permute-start(bf16[48,256]{1,0:T(8,128)(2,1)S(1)} %get-tuple-element.39), channel_id=1, source_target_pairs={{1,2},{3,4},{5,6},{7,8},{9,10},{11,12},{13,14},{15,0},{2,1},{4,3},... | collective-permute-start | bytes 73736 | tf_op jit(solution)/shard_map/ppermute | solution.py:550
  28.0 5.9 %collective-permute-start.1 = (bf16[48,256]{1,0:T(8,128)(2,1)S(1)}, bf16[48,256]{1,0:T(8,128)(2,1)S(1)}, u32[]{:S(2)}, u32[]{:S(2)}) collective-permute-start(bf16[48,256]{1,0:T(8,128)(2,1)S(1)} %get-tuple-element.40), channel_id=1, source_target_pairs={{0,16},{32,48},{64,80},{96,112},{16,0},{48,32},{80,64},{112,96},{1... | collective-permute-start | bytes 73736 | tf_op jit(solution)/shard_map/ppermute | solution.py:550
  28.3 5.6 %collective-permute-start.2 = (bf16[48,256]{1,0:T(8,128)(2,1)S(1)}, bf16[48,256]{1,0:T(8,128)(2,1)S(1)}, u32[]{:S(2)}, u32[]{:S(2)}) collective-permute-start(bf16[48,256]{1,0:T(8,128)(2,1)S(1)} %get-tuple-element.41), channel_id=1, source_target_pairs={{16,32},{48,64},{80,96},{112,0},{32,16},{64,48},{96,80},{0,112},{1... | collective-permute-start | bytes 73736 | tf_op jit(solution)/shard_map/ppermute | solution.py:550
  29.2 4.7 %collective-permute-start.3 = (bf16[48,256]{1,0:T(8,128)(2,1)S(1)}, bf16[48,256]{1,0:T(8,128)(2,1)S(1)}, u32[]{:S(2)}, u32[]{:S(2)}) collective-permute-start(bf16[48,256]{1,0:T(8,128)(2,1)S(1)} %get-tuple-element.42), channel_id=1, source_target_pairs={{0,1},{2,3},{4,5},{6,7},{8,9},{10,11},{12,13},{14,15},{1,0},{3,2},... | collective-permute-start | bytes 73736 | tf_op jit(solution)/shard_map/ppermute | solution.py:550
  32.1 2.2 %copy-start.1 = (bf16[512,2048]{1,0:T(8,128)(2,1)S(1)}, bf16[512,2048]{1,0:T(8,128)(2,1)}, u32[]{:S(2)}) copy-start(bf16[512,2048]{1,0:T(8,128)(2,1)} %w_one_ref.3) | copy-start | bytes 6291460
  32.1 2.2 %copy-start.2 = (bf16[256,512]{1,0:T(8,128)(2,1)S(1)}, bf16[256,512]{1,0:T(8,128)(2,1)}, u32[]{:S(2)}) copy-start(bf16[256,512]{1,0:T(8,128)(2,1)} %cot_ref.5) | copy-start | bytes 786436
  37.1 7.0 %collective-permute-start.5 = (bf16[256,3072]{1,0:T(8,128)(2,1)S(1)}, bf16[256,3072]{1,0:T(8,128)(2,1)S(1)}, u32[]{:S(2)}, u32[]{:S(2)}) collective-permute-start(bf16[256,3072]{1,0:T(8,128)(2,1)S(1)} %get-tuple-element.58), channel_id=1, source_target_pairs={{0,1},{1,0},{2,3},{3,2},{4,5},{5,4},{6,7},{7,6},{8,9},{9,8},{10,11... | collective-permute-start | bytes 4718600 | tf_op jit(solution)/shard_map/ppermute | solution.py:557
  44.0 1.6 %collective-permute-start.4 = (bf16[64,16,128]{2,1,0:T(8,128)(2,1)S(1)}, bf16[64,16,128]{2,1,0:T(8,128)(2,1)S(1)}, u32[]{:S(2)}, u32[]{:S(2)}) collective-permute-start(bf16[64,16,128]{2,1,0:T(8,128)(2,1)S(1)} %get-tuple-element.55), channel_id=1, source_target_pairs={{0,1},{1,0},{2,3},{3,2},{4,5},{5,4},{6,7},{7,6},{8,9},{9,8},{10,11... | collective-permute-start | bytes 786440 | tf_op jit(solution)/shard_map/ppermute | solution.py:557
  82.9 39.1 %copy-start = (bf16[2048,512]{1,0:T(8,128)(2,1)S(1)}, bf16[2048,512]{1,0:T(8,128)(2,1)}, u32[]{:S(2)}) copy-start(bf16[2048,512]{1,0:T(8,128)(2,1)} %w_two_ref.1) | copy-start | bytes 6291460
  119.1 7.1 %collective-permute-start.6 = (bf16[64,9,16,128]{3,2,1,0:T(8,128)(2,1)S(1)}, bf16[64,9,16,128]{3,2,1,0:T(8,128)(2,1)S(1)}, u32[]{:S(2)}, u32[]{:S(2)}) collective-permute-start(bf16[64,9,16,128]{3,2,1,0:T(8,128)(2,1)S(1)} %all_to_all.16.in_ref.mine_ref), channel_id=1, source_target_pairs={{0,1},{1,0},{2,3},{3,2},{4,5},{5,4},{6,7},{7,6},{8,9},{9,8},{10,11... | collective-permute-start | bytes 7077896 | tf_op jit(solution)/shard_map/ppermute | solution.py:557
